TPU v7x, 128 devices: a whole 4x4x4 slice. The times are simulated.
128 devices in a mesh: dp: 8 (over z, y_lo), tensor: 16 (over y_hi, x, core).
Axes of the slice: x: 4, y: 4 (y_hi: 2, y_lo: 2; y = y_hi * 2 + y_lo), z: 4, core: 2. Of those that a mesh axis runs over, the one named last changes fastest.
Arguments:
- gate_input: bfloat16 [2048, 26624], P('dp', 'tensor'), parts along dimension 0, may hold values from -6 to 6
- up_input: bfloat16 [2048, 26624], P('dp', 'tensor'), parts along dimension 0, may hold values from -6 to 6
- down_low: int32 [3328, 8192], P('tensor'), may hold values from -34952 to 30583
- down_high: int32 [3328, 8192], P('tensor'), may hold values from -34952 to 30583
- down_scales: bfloat16 [208, 8192], P('tensor'), may hold values from 0.00024414062 to 0.002746582
Outputs:
- mixed: bfloat16 [2048, 8192], P('dp'), parts along dimension 0
There are 8 independent parts, one for each index of `dp`. A program takes and returns all parts, laid end to end along the dimension named above; an argument that names none is the same for every part. Nothing has to cross between parts.
All inputs are finite; a program needn't handle non-finite values.
Results may differ from a plain program's by a relative error of at most 0.0065.
Values may be sent and summed in bfloat16 or wider, within the bound.
No kernel may reach another device: no remote copies, remote signals or barrier semaphores. Data moves between devices by JAX's collectives and lax.ppermute only.
A program may use at most 192 MiB of HBM per device.

v0:
```python
import math

import jax
import jax.numpy as jnp
import numpy as np
from jax import lax
from jax.sharding import PartitionSpec as P

FF = 26624
GROUP = 128


code_offset = 34952


def swapped(x, axis, distance):
    return lax.ppermute(x, axis, [(i, i ^ 1 << distance) for i in range(lax.axis_size(axis))])


def paley_table():
    elements = [(u, v) for v in range(5) for u in range(5)]
    squares = set()
    for u, v in elements:
        if u != 0 or v != 0:
            squares.add(((u * u + 2 * v * v) % 5, 2 * u * v % 5))
    quad = np.zeros((25, 25))
    for i, first in enumerate(elements):
        for j, second in enumerate(elements):
            diff = ((first[0] - second[0]) % 5, (first[1] - second[1]) % 5)
            if diff != (0, 0):
                quad[i, j] = 1.0 if diff in squares else -1.0
    core = np.zeros((26, 26))
    core[0, 1:] = 1.0
    core[1:, 0] = 1.0
    core[1:, 1:] = quad
    return np.kron(core, np.array([[1.0, 1.0], [1.0, -1.0]])) + np.kron(
        np.eye(26), np.array([[1.0, -1.0], [-1.0, -1.0]])
    )


def sylvester(order):
    table = np.ones((1, 1))
    while table.shape[0] < order:
        table = np.kron(np.array([[1.0, 1.0], [1.0, -1.0]]), table)
    return table


def dequant(low_words, high_words, scales):
    shifts = 4 * jnp.arange(4, dtype=jnp.int32)
    low = (low_words + code_offset)[:, None, :] >> shifts[None, :, None] & 15
    high = (high_words + code_offset)[:, None, :] >> shifts[None, :, None] & 15
    nibbles = jnp.concatenate([low, high], axis=1)
    count = low_words.shape[0] * 8
    width = low_words.shape[1]
    codes = nibbles.reshape(count, width).astype(jnp.float32) - 8.0
    groups = scales.shape[0]
    scaled = codes.reshape(groups, count // groups, width) * scales.astype(jnp.float32)[:, None, :]
    return scaled.reshape(count, width).astype(jnp.bfloat16)


def dequant_all(down_low, down_high, down_scales):
    local_ff = down_low.shape[0] * 8
    width = down_low.shape[1]
    blocks = local_ff // GROUP
    low_words = down_low.reshape(blocks, GROUP // 8, width)
    high_words = down_high.reshape(blocks, GROUP // 8, width)
    parts = down_scales.reshape(blocks, 1, width)

    def one_block(item):
        return dequant(item[0], item[1], item[2])

    weights = lax.map(one_block, (low_words, high_words, parts))
    return weights.reshape(local_ff, width)


def local(gate_input, up_input, down_low, down_high, down_scales):
    local_ff = gate_input.shape[1]
    hidden = (jax.nn.silu(gate_input.astype(jnp.float32)) * up_input.astype(jnp.float32)).astype(
        jnp.bfloat16
    )
    table = jnp.asarray(np.kron(sylvester(local_ff // 52), paley_table()), jnp.bfloat16)
    partial_rot = jnp.dot(hidden, table, preferred_element_type=jnp.float32)
    shards = lax.axis_size("tensor")
    position = lax.axis_index("tensor")
    turned = partial_rot
    for bit in range(shards.bit_length() - 1):
        partner = swapped(turned, "tensor", bit)
        upper = position >> bit & 1 == 1
        turned = jnp.where(upper, partner - turned, turned + partner)
    rotated = (turned * (1.0 / math.sqrt(FF))).astype(jnp.bfloat16)
    down_weight = dequant_all(down_low, down_high, down_scales)
    term = jnp.dot(rotated, down_weight, preferred_element_type=jnp.float32)
    total = lax.psum(term, "tensor")
    return total.astype(jnp.bfloat16)


def solution(mesh):
    placed = (
        P("dp", "tensor"),
        P("dp", "tensor"),
        P("tensor", None),
        P("tensor", None),
        P("tensor", None),
    )
    return jax.shard_map(
        local, mesh=mesh, in_specs=placed, out_specs=P("dp", None), check_vma=False
    )
```

profile of v0, /device:TPU:1, one launch (start us, length us, event | category | flops | bytes accessed | tf_op | source)
XLA Modules:
  0.0 290.3 jit_solution(9136870397023269002)
XLA Ops:
  0.0 5.0 %fusion.13 = f32[256,1664]{1,0:T(8,128)S(1)} fusion(bf16[1664,1664]{1,0:T(8,128)(2,1)} %constant.62.clone, bf16[256,1664]{1,0:T(8,128)(2,1)} %param.9, bf16[256,1664]{1,0:T(8,128)(2,1)} %param.8), kind=kOutput, calls=%fused_computation.26 | convolution fusion | flops 1421082624 | bytes 8945664 | tf_op jit(solution)/shard_map/dot_general | solution.py:82
  6.5 3.4 %collective-permute-done = f32[256,1664]{1,0:T(8,128)} collective-permute-done((f32[256,1664]{1,0:T(8,128)S(1)}, f32[256,1664]{1,0:T(8,128)}, u32[]{:S(2)}, u32[]{:S(2)}) %collective-permute-start) | collective-permute-done | bytes 1703968 | tf_op jit(solution)/shard_map/ppermute | solution.py:17
  12.8 37.2 %collective-permute-done.1 = f32[256,1664]{1,0:T(8,128)} collective-permute-done((f32[256,1664]{1,0:T(8,128)S(1)}, f32[256,1664]{1,0:T(8,128)}, u32[]{:S(2)}, u32[]{:S(2)}) %collective-permute-start.1) | collective-permute-done | bytes 1703968 | tf_op jit(solution)/shard_map/ppermute | solution.py:17
  50.1 1.6 add_select_fusion.1
  51.7 2.9 %collective-permute-start.2 = (f32[256,1664]{1,0:T(8,128)S(1)}, f32[256,1664]{1,0:T(8,128)}, u32[]{:S(2)}, u32[]{:S(2)}) collective-permute-start(f32[256,1664]{1,0:T(8,128)S(1)} %add_select_fusion.1), channel_id=1, source_target_pairs={{0,4},{1,5},{2,6},{3,7},{4,0},{5,1},{6,2},{7,3},{8,12},{9,13},{10,... | collective-permute-start | bytes 5111816 | tf_op jit(solution)/shard_map/ppermute | solution.py:17
  54.6 36.3 %collective-permute-done.2 = f32[256,1664]{1,0:T(8,128)} collective-permute-done((f32[256,1664]{1,0:T(8,128)S(1)}, f32[256,1664]{1,0:T(8,128)}, u32[]{:S(2)}, u32[]{:S(2)}) %collective-permute-start.2) | collective-permute-done | bytes 1703968 | tf_op jit(solution)/shard_map/ppermute | solution.py:17
  90.9 1.6 add_select_fusion
  92.5 3.1 %collective-permute-start.3 = (f32[256,1664]{1,0:T(8,128)S(1)}, f32[256,1664]{1,0:T(8,128)S(1)}, u32[]{:S(2)}, u32[]{:S(2)}) collective-permute-start(f32[256,1664]{1,0:T(8,128)S(1)} %add_select_fusion), channel_id=1, source_target_pairs={{0,8},{1,9},{2,10},{3,11},{4,12},{5,13},{6,14},{7,15},{8,0},{9,1},... | collective-permute-start | bytes 5111816 | tf_op jit(solution)/shard_map/ppermute | solution.py:17
  95.6 76.5 %while.12 = (s32[]{:T(128)}, bf16[13,128,8192]{2,1,0:T(8,128)(2,1)}, s32[13,16,8192]{2,1,0:T(8,128)}, s32[13,16,8192]{2,1,0:T(8,128)}, bf16[13,1,8192]{2,0,1:T(8,128)(2,1)}, /*index=5*/s32[]{:T(128)}) while((s32[]{:T(128)}, bf16[13,128,8192]{2,1,0:T(8,128)(2,1)}, s32[13,16,8192]{2,1,0:T(8,128)}, s32[13,16,8192]{2,1,0:T(8,128)}, ...), condition=%wide.region_1.2_spmd, body=%wide.region_0.1_spmd.sunk | while | flops 7610374 | bytes 13713529 | solution.py:72
  99.1 2.4 fusion.20
  105.0 2.4 fusion.20
  110.9 2.4 fusion.20
  116.8 2.4 fusion.20
  122.6 2.4 fusion.20
  128.6 2.4 fusion.20
  134.4 2.4 fusion.20
  140.3 2.4 fusion.20
  146.2 2.4 fusion.20
  152.1 2.4 fusion.20
  157.9 2.4 fusion.20
  163.8 2.4 fusion.20
  169.7 2.4 fusion.20
  172.1 14.8 %fusion.10 = f32[256,8192]{1,0:T(8,128)} fusion(bf16[1664,8192]{1,0:T(8,128)(2,1)} %bitcast.33, f32[256,1664]{1,0:T(8,128)S(1)} %add_select_fusion, f32[256,1664]{1,0:T(8,128)S(1)} %collective-permute-done.3, pred[]{:T(512)S(6)} %eq.12), kind=kOutput, calls=%fused_computation.23 | convolution fusion | flops 6981451776 | bytes 39059456 | tf_op jit(solution)/shard_map/dot_general | solution.py:92
  187.0 103.3 %all-reduce.1 = bf16[256,8192]{1,0:T(8,128)(2,1)} all-reduce(f32[256,8192]{1,0:T(8,128)} %fusion.10), channel_id=1, replica_groups=mesh['dp'=8,'tensor'=16] {'tensor'}, use_global_device_ids=true, to_apply=%region_2.3 | all-reduce | flops 2097152 | bytes 12582912 | tf_op jit(solution)/shard_map/psum | solution.py:93
  (57 shorter events, 49.8 us)
Async XLA Ops:
  5.0 4.9 %collective-permute-start = (f32[256,1664]{1,0:T(8,128)S(1)}, f32[256,1664]{1,0:T(8,128)}, u32[]{:S(2)}, u32[]{:S(2)}) collective-permute-start(f32[256,1664]{1,0:T(8,128)S(1)} %fusion.13), channel_id=1, source_target_pairs={{0,1},{1,0},{2,3},{3,2},{4,5},{5,4},{6,7},{7,6},{8,9},{9,8},{10,11... | collective-permute-start | bytes 5111816 | tf_op jit(solution)/shard_map/ppermute | solution.py:17
  11.5 38.6 %collective-permute-start.1 = (f32[256,1664]{1,0:T(8,128)S(1)}, f32[256,1664]{1,0:T(8,128)}, u32[]{:S(2)}, u32[]{:S(2)}) collective-permute-start(f32[256,1664]{1,0:T(8,128)S(1)} %add_select_fusion.2), channel_id=1, source_target_pairs={{0,2},{1,3},{2,0},{3,1},{4,6},{5,7},{6,4},{7,5},{8,10},{9,11},{10,... | collective-permute-start | bytes 5111816 | tf_op jit(solution)/shard_map/ppermute | solution.py:17
  51.7 39.2 %collective-permute-start.2 = (f32[256,1664]{1,0:T(8,128)S(1)}, f32[256,1664]{1,0:T(8,128)}, u32[]{:S(2)}, u32[]{:S(2)}) collective-permute-start(f32[256,1664]{1,0:T(8,128)S(1)} %add_select_fusion.1), channel_id=1, source_target_pairs={{0,4},{1,5},{2,6},{3,7},{4,0},{5,1},{6,2},{7,3},{8,12},{9,13},{10,... | collective-permute-start | bytes 5111816 | tf_op jit(solution)/shard_map/ppermute | solution.py:17
  92.5 79.6 %collective-permute-start.3 = (f32[256,1664]{1,0:T(8,128)S(1)}, f32[256,1664]{1,0:T(8,128)S(1)}, u32[]{:S(2)}, u32[]{:S(2)}) collective-permute-start(f32[256,1664]{1,0:T(8,128)S(1)} %add_select_fusion), channel_id=1, source_target_pairs={{0,8},{1,9},{2,10},{3,11},{4,12},{5,13},{6,14},{7,15},{8,0},{9,1},... | collective-permute-start | bytes 5111816 | tf_op jit(solution)/shard_map/ppermute | solution.py:17
where the time goes:
time: 294 us; the launch traced here: 290 us
  blocking collectives  103 us (35%)
  other arithmetic  81.2 us (28%)
  waiting for transfers between devices  76.9 us (26%)
  matrix products  19.8 us (7%)
  starting transfers between devices  8.86 us (3%)
    psum x1, blocking collectives, local(): total = lax.psum(term, 'tensor')  103 us
    ppermute x4, waiting for transfers between devices, swapped(): lax.ppermute(x, axis, [(i, i ^ 1 << distance) for i in range(lax.axis_siz...  76.9 us
    dynamic_update_slice x13, other arithmetic, dequant_all(): weights = lax.map(one_block, (low_words, high_words, parts))  31 us
    and x13, other arithmetic, dequant(): low = (low_words + code_offset)[:, None, :] >> shifts[None, :, None] & 15  16.6 us
    add x13, other arithmetic, dequant(): high = (high_words + code_offset)[:, None, :] >> shifts[None, :, None] & 15  16.5 us
    dot_general x1, matrix products, local(): term = jnp.dot(rotated, down_weight, preferred_element_type=jnp.float32)  14.8 us
    mul x13, other arithmetic, dequant(): codes.reshape(groups, count // groups, width)  12.2 us
    ppermute x4, starting transfers between devices, swapped(): lax.ppermute(x, axis, [(i, i ^ 1 << distance) for i in range(lax.axis_siz...  8.86 us
  transfers between devices with their start and end apart: 4, of which 3 were waited for; matrix products, arithmetic and copies ran while one was open for 26% of the time, Pallas kernels for 0%

commit v1 on v0

v1 whole, which is shorter than its diff:
```python
import functools
import math

import jax
import jax.numpy as jnp
import numpy as np
from jax import lax
from jax.experimental import pallas as pl
from jax.experimental.pallas import tpu as pltpu
from jax.sharding import PartitionSpec as P

FF = 26624
GROUP = 128
CODE_FLIP = 0x8888
VMEM_LIMIT = 48 * 1024 * 1024


def paley_table():
    elements = [(u, v) for v in range(5) for u in range(5)]
    squares = set()
    for u, v in elements:
        if u != 0 or v != 0:
            squares.add(((u * u + 2 * v * v) % 5, 2 * u * v % 5))
    quad = np.zeros((25, 25))
    for i, first in enumerate(elements):
        for j, second in enumerate(elements):
            diff = ((first[0] - second[0]) % 5, (first[1] - second[1]) % 5)
            if diff != (0, 0):
                quad[i, j] = 1.0 if diff in squares else -1.0
    core = np.zeros((26, 26))
    core[0, 1:] = 1.0
    core[1:, 0] = 1.0
    core[1:, 1:] = quad
    return np.kron(core, np.array([[1.0, 1.0], [1.0, -1.0]])) + np.kron(
        np.eye(26), np.array([[1.0, -1.0], [-1.0, -1.0]])
    )


def sylvester(order):
    table = np.ones((1, 1))
    while table.shape[0] < order:
        table = np.kron(np.array([[1.0, 1.0], [1.0, -1.0]]), table)
    return table


def local_table(local_ff):
    table = np.kron(sylvester(local_ff // 52), paley_table())
    order = np.arange(local_ff).reshape(-1, GROUP // 8, 8).transpose(0, 2, 1).reshape(-1)
    return jnp.asarray(table[:, order], jnp.bfloat16)


def rotate_body(hidden_ref, table_ref, out_ref):
    shards, rows, depth = hidden_ref.shape
    flat = hidden_ref[...].reshape(shards * rows, depth)
    turned = jnp.dot(flat, table_ref[...], preferred_element_type=jnp.float32)
    parts = [turned[rows * s : rows * (s + 1)] for s in range(shards)]
    step = 1
    while step < shards:
        parts = [
            parts[s] + parts[s + step] if s & step == 0 else parts[s - step] - parts[s]
            for s in range(shards)
        ]
        step *= 2
    for s in range(shards):
        out_ref[s] = (parts[s] * (1.0 / math.sqrt(FF))).astype(jnp.bfloat16)


def rotate(hidden, table):
    shards, rows, depth = hidden.shape
    tile = GROUP
    return pl.pallas_call(
        rotate_body,
        grid=(depth // tile,),
        in_specs=[
            pl.BlockSpec((shards, rows, depth), lambda j: (0, 0, 0)),
            pl.BlockSpec((depth, tile), lambda j: (0, j)),
        ],
        out_specs=pl.BlockSpec((shards, rows, tile), lambda j: (0, 0, j)),
        out_shape=jax.ShapeDtypeStruct(hidden.shape, jnp.bfloat16),
        compiler_params=pltpu.CompilerParams(vmem_limit_bytes=VMEM_LIMIT),
        cost_estimate=pl.CostEstimate(
            flops=2 * shards * rows * depth * depth,
            bytes_accessed=2 * depth * depth + 4 * shards * rows * depth,
            transcendentals=0,
        ),
        name="rotate",
    )(hidden, table)


def dequant_body(low_ref, high_ref, scale_ref, out_ref):
    groups, words, width = low_ref.shape
    for g in range(groups):
        scale = jnp.broadcast_to(scale_ref[g], (words, width))
        for half, ref in enumerate((low_ref, high_ref)):
            nibbles = (ref[g] + 34952) ^ CODE_FLIP
            for k in range(4):
                code = (nibbles << (28 - 4 * k)) >> 28
                out_ref[g, 4 * half + k] = code.astype(jnp.bfloat16) * scale


def dequant(low, high, scales):
    groups, words, width = low.shape
    tile = 512
    return pl.pallas_call(
        dequant_body,
        grid=(width // tile,),
        in_specs=[
            pl.BlockSpec((groups, words, tile), lambda j: (0, 0, j)),
            pl.BlockSpec((groups, words, tile), lambda j: (0, 0, j)),
            pl.BlockSpec((groups, 1, tile), lambda j: (0, 0, j)),
        ],
        out_specs=pl.BlockSpec((groups, 8, words, tile), lambda j: (0, 0, 0, j)),
        out_shape=jax.ShapeDtypeStruct((groups, 8, words, width), jnp.bfloat16),
        compiler_params=pltpu.CompilerParams(vmem_limit_bytes=VMEM_LIMIT),
        cost_estimate=pl.CostEstimate(
            flops=groups * words * 8 * width * 8,
            bytes_accessed=groups * words * width * 24,
            transcendentals=0,
        ),
        name="dequant",
    )(low, high, scales)


def project_body(core_ref, rot_ref, weight_ref, keep_ref, send_ref):
    core = core_ref[0]
    groups, planes, words, tile = weight_ref.shape
    pairs, _, rows, depth = rot_ref.shape
    weight = weight_ref[...].reshape(depth, tile)
    for out_ref, which in ((send_ref, 1 - core), (keep_ref, core)):
        lhs = rot_ref[:, pl.ds(which, 1)].reshape(pairs * rows, depth)
        term = jnp.dot(lhs, weight, preferred_element_type=jnp.float32)
        out_ref[...] = term.astype(jnp.bfloat16).reshape(pairs, rows, tile)


def project(core, rot, weight, first, width):
    pairs, two, rows, depth = rot.shape
    groups, planes, words, _ = weight.shape
    tile = 512
    start = first // tile
    shape = jax.ShapeDtypeStruct((pairs, rows, width), jnp.bfloat16)
    return pl.pallas_call(
        project_body,
        grid_spec=pltpu.PrefetchScalarGridSpec(
            num_scalar_prefetch=1,
            grid=(width // tile,),
            in_specs=[
                pl.BlockSpec((pairs, two, rows, depth), lambda j, c: (0, 0, 0, 0)),
                pl.BlockSpec((groups, planes, words, tile), lambda j, c: (0, 0, 0, j + start)),
            ],
            out_specs=[
                pl.BlockSpec((pairs, rows, tile), lambda j, c: (0, 0, j)),
                pl.BlockSpec((pairs, rows, tile), lambda j, c: (0, 0, j)),
            ],
        ),
        out_shape=[shape, shape],
        compiler_params=pltpu.CompilerParams(vmem_limit_bytes=VMEM_LIMIT),
        cost_estimate=pl.CostEstimate(
            flops=4 * pairs * rows * depth * width,
            bytes_accessed=2 * depth * width + 8 * pairs * rows * width,
            transcendentals=0,
        ),
        name="project",
    )(core, rot, weight)


def local(gate_input, up_input, down_low, down_high, down_scales):
    shards = lax.axis_size("tensor")
    position = lax.axis_index("tensor")
    core = position % 2
    total_rows, local_ff = gate_input.shape
    rows = total_rows // shards
    pairs = shards // 2
    groups = local_ff // GROUP
    width = down_low.shape[1]
    same_core = [[2 * i + c for i in range(pairs)] for c in range(2)]
    other_core = [(i, i ^ 1) for i in range(shards)]

    hidden = (jax.nn.silu(gate_input.astype(jnp.float32)) * up_input.astype(jnp.float32)).astype(jnp.bfloat16)
    mine = lax.all_to_all(hidden.reshape(shards, rows, local_ff), "tensor", 0, 0)
    turned = rotate(mine, local_table(local_ff))
    rot = lax.all_to_all(turned, "tensor", 0, 0).reshape(pairs, 2, rows, local_ff)

    weight = dequant(
        down_low.reshape(groups, GROUP // 8, width),
        down_high.reshape(groups, GROUP // 8, width),
        down_scales.reshape(groups, 1, width),
    )

    core_arg = core.astype(jnp.int32).reshape(1)
    chunks = 2
    part = width // chunks
    sums = []
    for j in range(chunks):
        keep, send = project(core_arg, rot, weight, j * part, part)
        got = lax.ppermute(send, "tensor", other_core)
        chip = (keep.astype(jnp.float32) + got.astype(jnp.float32)).astype(jnp.bfloat16)
        pieces = lax.all_to_all(chip, "tensor", 0, 0, axis_index_groups=same_core)
        sums.append(jnp.sum(pieces.astype(jnp.float32), axis=0).astype(jnp.bfloat16))
    outs = []
    for j in range(chunks):
        spread = jnp.broadcast_to(sums[j][None], (pairs, rows, part))
        own = lax.all_to_all(spread, "tensor", 0, 0, axis_index_groups=same_core)
        theirs = lax.ppermute(own, "tensor", other_core)
        first = jnp.where(core == 0, own, theirs)
        second = jnp.where(core == 0, theirs, own)
        outs.append(jnp.stack([first, second], axis=1).reshape(total_rows, part))
    return jnp.concatenate(outs, axis=1)


def solution(mesh):
    placed = (
        P("dp", "tensor"),
        P("dp", "tensor"),
        P("tensor", None),
        P("tensor", None),
        P("tensor", None),
    )
    return jax.shard_map(local, mesh=mesh, in_specs=placed, out_specs=P("dp", None), check_vma=False)
```

time: 294 us -> 179 us (0.61)
  other arithmetic: 81.2 us -> 10.5 us
  blocking collectives: 103 us -> 46.5 us
  Pallas kernels: 0 us -> 50.9 us
  waiting for transfers between devices: 76.9 us -> 49.1 us
  matrix products: 19.8 us -> 0 us
  starting transfers between devices: 8.86 us -> 18.2 us
    psum x1 -> x0, blocking collectives: 103 us -> none  [local(): total = lax.psum(term, 'tensor')]
    ppermute x4, waiting for transfers between devices: 76.9 us -> 0.58 us  [the longest x2 0.57 us: local(): theirs = lax.ppermute(own, 'tensor', other_core)]
    pallas_call x0 -> x4, Pallas kernels: none -> 50.9 us  [the longest x1 20.7 us: dequant(): pl.pallas_call(dequant_body, grid=(width // tile,), in_specs=[pl.BlockSpe...]
    all_to_all x0 -> x4, waiting for transfers between devices: none -> 48.5 us  [the longest x2 32.1 us: local(): own = lax.all_to_all(spread, 'tensor', 0, 0, axis_index_groups=same_core)]
    all_to_all x0 -> x2, blocking collectives: none -> 46.5 us  [the longest x1 23.5 us: local(): pieces = lax.all_to_all(chip, 'tensor', 0, 0, axis_index_groups=same_core)]
    dynamic_update_slice x13 -> x0, other arithmetic: 31 us -> none  [dequant_all(): weights = lax.map(one_block, (low_words, high_words, parts))]
    dot_general x2 -> x0, matrix products: 19.8 us -> none  [the longest x1 14.8 us: local(): term = jnp.dot(rotated, down_weight, preferred_element_type=jnp.float32)]
    and x13 -> x0, other arithmetic: 16.6 us -> none  [dequant(): low = (low_words + code_offset)[:, None, :] >> shifts[None, :, None] & 15]
  transfers between devices with their start and end apart: 4 -> 8, of which waited for: 3 -> 4; matrix products, arithmetic and copies ran while one was open for 26% -> 5% of each run, Pallas kernels for 0% -> 17%
where the time goes in v1:
time: 179 us; the launch traced here: 178 us
  Pallas kernels  50.9 us (28%)
  waiting for transfers between devices  49.1 us (27%)
  blocking collectives  46.5 us (26%)
  starting transfers between devices  18.2 us (10%)
  other arithmetic  10.5 us (6%)
  local copies, waits for them, and re-layouts  2.68 us (1%)
    all_to_all x2, waiting for transfers between devices, local(): own = lax.all_to_all(spread, 'tensor', 0, 0, axis_index_groups=same_core)  32.1 us
    all_to_all x1, blocking collectives, local(): pieces = lax.all_to_all(chip, 'tensor', 0, 0, axis_index_groups=same_core)  23.5 us
    all_to_all x1, blocking collectives, local(): lax.all_to_all(hidden.reshape(shards, rows, local_ff), 'tensor', 0, 0)  23 us
    pallas_call x1, Pallas kernels, dequant(): pl.pallas_call(dequant_body, grid=(width // tile,), in_specs=[pl.BlockSpe...  20.7 us
    pallas_call x2, Pallas kernels, project(): pl.pallas_call(project_body, grid_spec=pltpu.PrefetchScalarGridSpec(num_s...  19.4 us
    all_to_all x1, waiting for transfers between devices, local(): pieces = lax.all_to_all(chip, 'tensor', 0, 0, axis_index_groups=same_core)  16.3 us
    pallas_call x1, Pallas kernels, rotate(): pl.pallas_call(rotate_body, grid=(depth // tile,), in_specs=[pl.BlockSpec...  10.9 us
    all_to_all x2, starting transfers between devices, local(): own = lax.all_to_all(spread, 'tensor', 0, 0, axis_index_groups=same_core)  7.79 us
  transfers between devices with their start and end apart: 8, of which 4 were waited for; matrix products, arithmetic and copies ran while one was open for 5% of the time, Pallas kernels for 17%

profile of v1, /device:TPU:1, one launch (start us, length us, event | category | flops | bytes accessed | tf_op | source)
XLA Modules:
  0.0 177.9 jit_solution(15596185623661565178)
XLA Ops:
  0.0 1.9 %fusion.4 = bf16[256,1664]{1,0:T(8,128)(2,1)S(1)} fusion(bf16[256,1664]{1,0:T(8,128)(2,1)} %param.7, bf16[256,1664]{1,0:T(8,128)(2,1)} %param.6), kind=kLoop, calls=%fused_computation.11 | loop fusion | flops 3407872 | bytes 2555904 | tf_op jit(solution)/shard_map/convert_element_type | solution.py:178
  1.9 23.0 %all_to_all.30.hidden_ref = bf16[16,16,1664]{2,1,0:T(8,128)(2,1)S(1)} all-to-all(bf16[16,16,1664]{2,1,0:T(8,128)(2,1)S(1)} %bitcast.24), channel_id=1, replica_groups=mesh['dp'=8,'tensor'=16] {'tensor'}, dimensions={0} | all-to-all | bytes 1703936 | tf_op jit(solution)/shard_map/all_to_all | solution.py:179
  24.9 10.9 %rotate.1 = bf16[16,16,1664]{2,1,0:T(8,128)(2,1)} custom-call(bf16[16,16,1664]{2,1,0:T(8,128)(2,1)S(1)} %all_to_all.30.hidden_ref, bf16[1664,1664]{1,0:T(8,128)(2,1)} %constant.27.clone.table_ref), custom_call_target="tpu_custom_call" | custom-call | flops 1417674752 | bytes 7241728 | tf_op jit(solution)/shard_map/rotate/pallas_call | solution.py:71
  35.8 4.4 %all-to-all-start.1 = ((bf16[16,16,1664]{2,1,0:T(8,128)(2,1)}), bf16[16,16,1664]{2,1,0:T(8,128)(2,1)S(1)}, u32[]{:S(2)}, u32[]{:S(2)}) async-start(bf16[16,16,1664]{2,1,0:T(8,128)(2,1)} %rotate.1), calls=%async_computation.1 | async-start | bytes 1703936 | tf_op jit(solution)/shard_map/all_to_all | solution.py:181
  40.2 0.4 copy.9.scale_ref
  40.6 20.7 %dequant.1.weight_ref = bf16[13,8,16,8192]{3,2,1,0:T(8,128)(2,1)} custom-call(s32[13,16,8192]{2,1,0:T(8,128)} %bitcast.22, s32[13,16,8192]{2,1,0:T(8,128)} %bitcast.23, bf16[13,1,8192]{2,1,0:T(2,128)(2,1)S(1)} %copy.9.scale_ref), custom_call_target="tpu_custom_call" | custom-call | flops 109051904 | bytes 40894464 | tf_op jit(solution)/shard_map/dequant/pallas_call | solution.py:104
  61.3 9.7 %project.2 = (bf16[8,16,4096]{2,1,0:T(8,128)(2,1)S(1)}, bf16[8,16,4096]{2,1,0:T(8,128)(2,1)S(1)}) custom-call(s32[1]{0:T(128)} %bitcast.core_ref, bf16[8,2,16,1664]{3,2,1,0:T(8,128)(2,1)S(1)} %bitcast.18, bf16[13,8,16,8192]{3,2,1,0:T(8,128)(2,1)} %dequant.1.weight_ref), custom_call_target="tpu_custom_call" | custom-call | flops 3489660928 | bytes 17825792 | tf_op jit(solution)/shard_map/project/pallas_call | solution.py:141
  71.2 9.7 %project.3 = (bf16[8,16,4096]{2,1,0:T(8,128)(2,1)S(1)}, bf16[8,16,4096]{2,1,0:T(8,128)(2,1)S(1)}) custom-call(s32[1]{0:T(128)} %bitcast.core_ref, bf16[8,2,16,1664]{3,2,1,0:T(8,128)(2,1)S(1)} %bitcast.19, bf16[13,8,16,8192]{3,2,1,0:T(8,128)(2,1)} %dequant.1.weight_ref), custom_call_target="tpu_custom_call" | custom-call | flops 3489660928 | bytes 17825792 | tf_op jit(solution)/shard_map/project/pallas_call | solution.py:141
  81.5 23.5 %all_to_all.31 = bf16[8,16,4096]{2,1,0:T(8,128)(2,1)} all-to-all(bf16[8,16,4096]{2,1,0:T(8,128)(2,1)S(1)} %add_convert_fusion.1), channel_id=1, replica_groups={{0,2,4,6,8,10,12,14},{1,3,5,7,9,11,13,15},{16,18,20,22,24,26,28,30},{17..., dimensions={0} | all-to-all | bytes 2097152 | tf_op jit(solution)/shard_map/all_to_all | solution.py:197
  105.1 1.4 reduce_sum.24
  106.4 1.1 broadcast_in_dim.4
  107.5 4.2 %all-to-all-start.3 = ((bf16[8,16,4096]{2,1,0:T(8,128)(2,1)}), bf16[8,16,4096]{2,1,0:T(8,128)(2,1)}, u32[]{:S(2)}, u32[]{:S(2)}) async-start(bf16[8,16,4096]{2,1,0:T(8,128)(2,1)} %broadcast_in_dim.4), calls=%async_computation.3 | async-start | bytes 2097152 | tf_op jit(solution)/shard_map/all_to_all | solution.py:202
  111.8 2.4 %add_convert_fusion = bf16[8,16,4096]{2,1,0:T(8,128)(2,1)} fusion(bf16[8,16,4096]{2,1,0:T(8,128)(2,1)} %collective-permute-done.2, bf16[8,16,4096]{2,1,0:T(8,128)(2,1)S(1)} %get-tuple-element.11), kind=kLoop, calls=%fused_computation.5 | loop fusion | flops 2097152 | bytes 3145728 | tf_op jit(solution)/shard_map/convert_element_type | solution.py:196
  114.2 14.9 %all-to-all-done.3 = bf16[8,16,4096]{2,1,0:T(8,128)(2,1)} async-done(((bf16[8,16,4096]{2,1,0:T(8,128)(2,1)}), bf16[8,16,4096]{2,1,0:T(8,128)(2,1)}, u32[]{:S(2)}, u32[]{:S(2)}) %all-to-all-start.3) | async-done | bytes 1048608 | tf_op jit(solution)/shard_map/all_to_all | solution.py:202
  129.1 3.6 %all-to-all-start.4 = ((bf16[8,16,4096]{2,1,0:T(8,128)(2,1)}), bf16[8,16,4096]{2,1,0:T(8,128)(2,1)S(1)}, u32[]{:S(2)}, u32[]{:S(2)}) async-start(bf16[8,16,4096]{2,1,0:T(8,128)(2,1)} %add_convert_fusion), calls=%async_computation.4 | async-start | bytes 2097152 | tf_op jit(solution)/shard_map/all_to_all | solution.py:197
  132.6 0.9 collective-permute-start.1
  133.6 16.3 %all-to-all-done.4 = bf16[8,16,4096]{2,1,0:T(8,128)(2,1)S(1)} async-done(((bf16[8,16,4096]{2,1,0:T(8,128)(2,1)}), bf16[8,16,4096]{2,1,0:T(8,128)(2,1)S(1)}, u32[]{:S(2)}, u32[]{:S(2)}) %all-to-all-start.4) | async-done | bytes 1048608 | tf_op jit(solution)/shard_map/all_to_all | solution.py:197
  150.1 1.1 broadcast_in_dim.5
  151.1 3.6 %all-to-all-start.5 = ((bf16[8,16,4096]{2,1,0:T(8,128)(2,1)}), bf16[8,16,4096]{2,1,0:T(8,128)(2,1)S(1)}, u32[]{:S(2)}, u32[]{:S(2)}) async-start(bf16[8,16,4096]{2,1,0:T(8,128)(2,1)} %broadcast_in_dim.5), calls=%async_computation.5 | async-start | bytes 2097152 | tf_op jit(solution)/shard_map/all_to_all | solution.py:202
  154.7 17.3 %all-to-all-done.5 = bf16[8,16,4096]{2,1,0:T(8,128)(2,1)S(1)} async-done(((bf16[8,16,4096]{2,1,0:T(8,128)(2,1)}), bf16[8,16,4096]{2,1,0:T(8,128)(2,1)S(1)}, u32[]{:S(2)}, u32[]{:S(2)}) %all-to-all-start.5) | async-done | bytes 1048608 | tf_op jit(solution)/shard_map/all_to_all | solution.py:202
  172.0 0.8 collective-permute-start.3
  172.8 1.4 select_bitcast_fusion.3
  174.5 0.6 collective-permute-done.3
  175.4 2.5 %pad_maximum_fusion = bf16[256,8192]{1,0:T(8,128)(2,1)} fusion(bf16[256,4096]{1,0:T(8,128)(2,1)S(1)} %bitcast.21, bf16[256,4096]{1,0:T(8,128)(2,1)S(1)} %bitcast.20), kind=kLoop, calls=%fused_computation | loop fusion | flops 8388608 | bytes 8388608 | tf_op jit(solution)/shard_map/concatenate | solution.py:207
  (14 shorter events, 1.7 us)
Async XLA Ops:
  24.9 15.3 %copy-start = (bf16[13,8192]{1,0:T(8,128)(2,1)S(1)}, bf16[13,8192]{1,0:T(8,128)(2,1)}, u32[]{:S(2)}) copy-start(bf16[13,8192]{1,0:T(8,128)(2,1)} %param.10) | copy-start | bytes 638980
  35.8 25.5 %all-to-all-start.1 = ((bf16[16,16,1664]{2,1,0:T(8,128)(2,1)}), bf16[16,16,1664]{2,1,0:T(8,128)(2,1)S(1)}, u32[]{:S(2)}, u32[]{:S(2)}) async-start(bf16[16,16,1664]{2,1,0:T(8,128)(2,1)} %rotate.1), calls=%async_computation.1 | async-start | bytes 1703936 | tf_op jit(solution)/shard_map/all_to_all | solution.py:181
  71.0 10.3 %collective-permute-start = (bf16[8,16,4096]{2,1,0:T(8,128)(2,1)S(1)}, bf16[8,16,4096]{2,1,0:T(8,128)(2,1)S(1)}, u32[]{:S(2)}, u32[]{:S(2)}) collective-permute-start(bf16[8,16,4096]{2,1,0:T(8,128)(2,1)S(1)} %get-tuple-element.10), channel_id=1, source_target_pairs={{0,1},{1,0},{2,3},{3,2},{4,5},{5,4},{6,7},{7,6},{8,9},{9,8},{10,11... | collective-permute-start | bytes 3145736 | tf_op jit(solution)/shard_map/ppermute | solution.py:195
  80.9 30.8 %collective-permute-start.2 = (bf16[8,16,4096]{2,1,0:T(8,128)(2,1)S(1)}, bf16[8,16,4096]{2,1,0:T(8,128)(2,1)}, u32[]{:S(2)}, u32[]{:S(2)}) collective-permute-start(bf16[8,16,4096]{2,1,0:T(8,128)(2,1)S(1)} %get-tuple-element.12), channel_id=1, source_target_pairs={{0,1},{1,0},{2,3},{3,2},{4,5},{5,4},{6,7},{7,6},{8,9},{9,8},{10,11... | collective-permute-start | bytes 3145736 | tf_op jit(solution)/shard_map/ppermute | solution.py:195
  107.5 21.6 %all-to-all-start.3 = ((bf16[8,16,4096]{2,1,0:T(8,128)(2,1)}), bf16[8,16,4096]{2,1,0:T(8,128)(2,1)}, u32[]{:S(2)}, u32[]{:S(2)}) async-start(bf16[8,16,4096]{2,1,0:T(8,128)(2,1)} %broadcast_in_dim.4), calls=%async_computation.3 | async-start | bytes 2097152 | tf_op jit(solution)/shard_map/all_to_all | solution.py:202
  129.1 20.8 %all-to-all-start.4 = ((bf16[8,16,4096]{2,1,0:T(8,128)(2,1)}), bf16[8,16,4096]{2,1,0:T(8,128)(2,1)S(1)}, u32[]{:S(2)}, u32[]{:S(2)}) async-start(bf16[8,16,4096]{2,1,0:T(8,128)(2,1)} %add_convert_fusion), calls=%async_computation.4 | async-start | bytes 2097152 | tf_op jit(solution)/shard_map/all_to_all | solution.py:197
  132.6 40.2 %collective-permute-start.1 = (bf16[8,16,4096]{2,1,0:T(8,128)(2,1)}, bf16[8,16,4096]{2,1,0:T(8,128)(2,1)S(1)}, u32[]{:S(2)}, u32[]{:S(2)}) collective-permute-start(bf16[8,16,4096]{2,1,0:T(8,128)(2,1)} %all-to-all-done.3), channel_id=1, source_target_pairs={{0,1},{1,0},{2,3},{3,2},{4,5},{5,4},{6,7},{7,6},{8,9},{9,8},{10,11... | collective-permute-start | bytes 3145736 | tf_op jit(solution)/shard_map/ppermute | solution.py:203
  151.1 20.8 %all-to-all-start.5 = ((bf16[8,16,4096]{2,1,0:T(8,128)(2,1)}), bf16[8,16,4096]{2,1,0:T(8,128)(2,1)S(1)}, u32[]{:S(2)}, u32[]{:S(2)}) async-start(bf16[8,16,4096]{2,1,0:T(8,128)(2,1)} %broadcast_in_dim.5), calls=%async_computation.5 | async-start | bytes 2097152 | tf_op jit(solution)/shard_map/all_to_all | solution.py:202
  172.0 3.1 %collective-permute-start.3 = (bf16[8,16,4096]{2,1,0:T(8,128)(2,1)S(1)}, bf16[8,16,4096]{2,1,0:T(8,128)(2,1)S(1)}, u32[]{:S(2)}, u32[]{:S(2)}) collective-permute-start(bf16[8,16,4096]{2,1,0:T(8,128)(2,1)S(1)} %all-to-all-done.5), channel_id=1, source_target_pairs={{0,1},{1,0},{2,3},{3,2},{4,5},{5,4},{6,7},{7,6},{8,9},{9,8},{10,11... | collective-permute-start | bytes 3145736 | tf_op jit(solution)/shard_map/ppermute | solution.py:203

commit v2 on v1

v2 whole, which is shorter than its diff:
```python
import functools
import math

import jax
import jax.numpy as jnp
import numpy as np
from jax import lax
from jax.experimental import pallas as pl
from jax.experimental.pallas import tpu as pltpu
from jax.sharding import PartitionSpec as P

FF = 26624
GROUP = 128
CODE_FLIP = 0x8888
VMEM_LIMIT = 48 * 1024 * 1024


def paley_table():
    elements = [(u, v) for v in range(5) for u in range(5)]
    squares = set()
    for u, v in elements:
        if u != 0 or v != 0:
            squares.add(((u * u + 2 * v * v) % 5, 2 * u * v % 5))
    quad = np.zeros((25, 25))
    for i, first in enumerate(elements):
        for j, second in enumerate(elements):
            diff = ((first[0] - second[0]) % 5, (first[1] - second[1]) % 5)
            if diff != (0, 0):
                quad[i, j] = 1.0 if diff in squares else -1.0
    core = np.zeros((26, 26))
    core[0, 1:] = 1.0
    core[1:, 0] = 1.0
    core[1:, 1:] = quad
    return np.kron(core, np.array([[1.0, 1.0], [1.0, -1.0]])) + np.kron(
        np.eye(26), np.array([[1.0, -1.0], [-1.0, -1.0]])
    )


def sylvester(order):
    table = np.ones((1, 1))
    while table.shape[0] < order:
        table = np.kron(np.array([[1.0, 1.0], [1.0, -1.0]]), table)
    return table


def local_table(local_ff):
    table = np.kron(sylvester(local_ff // 52), paley_table())
    order = np.arange(local_ff).reshape(-1, GROUP // 8, 8).transpose(0, 2, 1).reshape(-1)
    return jnp.asarray(table[:, order], jnp.bfloat16)


def rotate_body(hidden_ref, table_ref, out_ref, turned_ref):
    shards, rows, depth = hidden_ref.shape
    flat = hidden_ref[...].reshape(shards * rows, depth)
    turned_ref[...] = jnp.dot(flat, table_ref[...], preferred_element_type=jnp.float32)
    width = table_ref.shape[1]
    for first in range(0, width, GROUP):
        cols = slice(first, first + GROUP)
        parts = [turned_ref[rows * s : rows * (s + 1), cols] for s in range(shards)]
        step = 1
        while step < shards:
            parts = [
                parts[s] + parts[s + step] if s & step == 0 else parts[s - step] - parts[s]
                for s in range(shards)
            ]
            step *= 2
        for s in range(shards):
            out_ref[s, :, cols] = (parts[s] * (1.0 / math.sqrt(FF))).astype(jnp.bfloat16)


def rotate(hidden, table):
    shards, rows, depth = hidden.shape
    tile = 896
    return pl.pallas_call(
        rotate_body,
        grid=(pl.cdiv(depth, tile),),
        in_specs=[
            pl.BlockSpec((shards, rows, depth), lambda j: (0, 0, 0)),
            pl.BlockSpec((depth, tile), lambda j: (0, j)),
        ],
        out_specs=pl.BlockSpec((shards, rows, tile), lambda j: (0, 0, j)),
        out_shape=jax.ShapeDtypeStruct(hidden.shape, jnp.bfloat16),
        scratch_shapes=[pltpu.VMEM((shards * rows, tile), jnp.float32)],
        compiler_params=pltpu.CompilerParams(vmem_limit_bytes=VMEM_LIMIT),
        cost_estimate=pl.CostEstimate(
            flops=2 * shards * rows * depth * depth,
            bytes_accessed=2 * depth * depth + 4 * shards * rows * depth,
            transcendentals=0,
        ),
        name="rotate",
    )(hidden, table)


def dequant_body(low_ref, high_ref, scale_ref, out_ref):
    groups, words, width = low_ref.shape
    for g in range(groups):
        scale = jnp.broadcast_to(scale_ref[g], (words, width))
        for half, ref in enumerate((low_ref, high_ref)):
            nibbles = (ref[g] + 34952) ^ CODE_FLIP
            for k in range(4):
                code = (nibbles << (28 - 4 * k)) >> 28
                out_ref[g, 4 * half + k] = code.astype(jnp.bfloat16) * scale


def dequant(low, high, scales):
    groups, words, width = low.shape
    tile = 512
    return pl.pallas_call(
        dequant_body,
        grid=(width // tile,),
        in_specs=[
            pl.BlockSpec((groups, words, tile), lambda j: (0, 0, j)),
            pl.BlockSpec((groups, words, tile), lambda j: (0, 0, j)),
            pl.BlockSpec((groups, 1, tile), lambda j: (0, 0, j)),
        ],
        out_specs=pl.BlockSpec((groups, 8, words, tile), lambda j: (0, 0, 0, j)),
        out_shape=jax.ShapeDtypeStruct((groups, 8, words, width), jnp.bfloat16),
        compiler_params=pltpu.CompilerParams(vmem_limit_bytes=VMEM_LIMIT),
        cost_estimate=pl.CostEstimate(
            flops=groups * words * 8 * width * 8,
            bytes_accessed=groups * words * width * 24,
            transcendentals=0,
        ),
        name="dequant",
    )(low, high, scales)


def project_body(order, place_ref, rot_ref, weight_ref, keep_ref, send_ref, lhs_ref):
    groups, planes, words, tile = weight_ref.shape
    shards, rows, depth = rot_ref.shape
    place = place_ref[0]

    @pl.when(pl.program_id(0) == 0)
    def _():
        for at, block in enumerate(order):
            lhs_ref[rows * at : rows * (at + 1)] = rot_ref[jnp.bitwise_xor(place, block)]

    weight = weight_ref[...].reshape(depth, tile)
    term = jnp.dot(lhs_ref[...], weight, preferred_element_type=jnp.float32)
    both = term.astype(jnp.bfloat16).reshape(2, shards // 2, rows, tile)
    send_ref[...] = both[0]
    keep_ref[...] = both[1]


def project(place, rot, weight, order, first, width):
    shards, rows, depth = rot.shape
    groups, planes, words, _ = weight.shape
    tile = 1024
    start = first // tile
    full = tuple(q ^ 1 for q in order) + tuple(order)
    shape = jax.ShapeDtypeStruct((shards // 2, rows, width), jnp.bfloat16)
    return pl.pallas_call(
        functools.partial(project_body, full),
        grid_spec=pltpu.PrefetchScalarGridSpec(
            num_scalar_prefetch=1,
            grid=(width // tile,),
            in_specs=[
                pl.BlockSpec((shards, rows, depth), lambda j, p: (0, 0, 0)),
                pl.BlockSpec((groups, planes, words, tile), lambda j, p: (0, 0, 0, j + start)),
            ],
            out_specs=[
                pl.BlockSpec((shards // 2, rows, tile), lambda j, p: (0, 0, j)),
                pl.BlockSpec((shards // 2, rows, tile), lambda j, p: (0, 0, j)),
            ],
            scratch_shapes=[pltpu.VMEM((shards * rows, depth), jnp.bfloat16)],
        ),
        out_shape=[shape, shape],
        compiler_params=pltpu.CompilerParams(vmem_limit_bytes=VMEM_LIMIT),
        cost_estimate=pl.CostEstimate(
            flops=2 * shards * rows * depth * width,
            bytes_accessed=2 * depth * width + 4 * shards * rows * width,
            transcendentals=0,
        ),
        name="project",
    )(place, rot, weight)


def place_body(names, first, width, count, place_ref, *refs):
    pieces, out_ref, sems = refs[:count], refs[-2], refs[-1]
    rows = pieces[0].shape[1]
    copies = []
    for piece, blocks in zip(pieces, names):
        for at, block in enumerate(blocks):
            start = pl.multiple_of(jnp.bitwise_xor(place_ref[0], block) * rows, rows)
            copies.append(
                pltpu.make_async_copy(
                    piece.at[at],
                    out_ref.at[pl.ds(start, rows), pl.ds(first, width)],
                    sems.at[len(copies)],
                )
            )
    for copy in copies:
        copy.start()
    for copy in copies:
        copy.wait()


def put(place, pieces, names, first, shape, into=None):
    count = len(pieces)
    width = pieces[0].shape[2]
    extra = () if into is None else (into,)
    return pl.pallas_call(
        functools.partial(place_body, names, first, width, count),
        in_specs=[pl.BlockSpec(memory_space=pltpu.SMEM)]
        + [pl.BlockSpec(memory_space=pl.ANY)] * (count + len(extra)),
        out_specs=pl.BlockSpec(memory_space=pl.ANY),
        out_shape=jax.ShapeDtypeStruct(shape, jnp.bfloat16),
        scratch_shapes=[pltpu.SemaphoreType.DMA((sum(map(len, names)),))],
        input_output_aliases={} if into is None else {1 + count: 0},
        compiler_params=pltpu.CompilerParams(vmem_limit_bytes=VMEM_LIMIT),
        cost_estimate=pl.CostEstimate(
            flops=0, bytes_accessed=4 * sum(p.size for p in pieces), transcendentals=0
        ),
        name="put",
    )(place, *pieces, *extra)


def local(gate_input, up_input, down_low, down_high, down_scales):
    shards = lax.axis_size("tensor")
    total_rows, local_ff = gate_input.shape
    rows = total_rows // shards
    groups = local_ff // GROUP
    width = down_low.shape[1]
    half = width // 2
    place = lax.axis_index("tensor").astype(jnp.int32).reshape(1)
    f32, bf16 = jnp.float32, jnp.bfloat16

    def swap(x, mask):
        return lax.ppermute(x, "tensor", [(i, i ^ mask) for i in range(shards)])

    CORE, Y = 1, 8
    X = (0, 2, 4, 6)
    by_x = tuple(x | y for x in X for y in (0, Y))
    by_y = tuple(x | y for y in (0, Y) for x in X)

    hidden = (jax.nn.silu(gate_input.astype(f32)) * up_input.astype(f32)).astype(bf16)
    mine = lax.all_to_all(hidden.reshape(shards, rows, local_ff), "tensor", 0, 0)
    turned = rotate(mine, local_table(local_ff))
    rot = lax.all_to_all(turned, "tensor", 0, 0)

    weight = dequant(
        down_low.reshape(groups, GROUP // 8, width),
        down_high.reshape(groups, GROUP // 8, width),
        down_scales.reshape(groups, 1, width),
    )

    keep_p, send_p = project(place, rot, weight, by_x, 0, half)
    got_p = swap(send_p, CORE)
    keep_q, send_q = project(place, rot, weight, by_y, half, half)
    got_q = swap(send_q, CORE)

    def chip_p(k):
        at = slice(2 * k, 2 * k + 2)
        return keep_p[at].astype(f32) + got_p[at].astype(f32)

    def chip_q(y):
        at = slice(4 * y, 4 * y + 4)
        return keep_q[at].astype(f32) + got_q[at].astype(f32)

    along_x = [swap(chip_p(k).astype(bf16), X[k]) for k in (2, 1, 3)]
    along_y = swap(chip_q(1).astype(bf16), Y)
    sum_p = chip_p(0) + sum(t.astype(f32) for t in along_x)
    sum_q = chip_q(0) + along_y.astype(f32)
    last_p = swap(sum_p[1].astype(bf16), Y)
    last_q = [swap(sum_q[k].astype(bf16), X[k]) for k in (2, 1, 3)]
    done_p = (sum_p[0] + last_p.astype(f32)).astype(bf16)
    done_q = (sum_q[0] + sum(t.astype(f32) for t in last_q)).astype(bf16)

    pair_p = jnp.stack([done_p, swap(done_p, Y)])
    row_q = jnp.stack([done_q] + [swap(done_q, X[k]) for k in (1, 2, 3)])
    all_p = [pair_p] + [swap(pair_p, X[k]) for k in (1, 2, 3)]
    all_q = [row_q, swap(row_q, Y)]
    names_p = [tuple(X[k] | y for y in (0, Y)) for k in range(4)]
    names_q = [tuple(x | y for x in X) for y in (0, Y)]
    far_p = [swap(t, CORE) for t in all_p]
    far_q = [swap(t, CORE) for t in all_q]

    def across(names):
        return [tuple(q | CORE for q in blocks) for blocks in names]

    shape = (total_rows, width)
    out = put(place, all_p + far_p, names_p + across(names_p), 0, shape)
    return put(place, all_q + far_q, names_q + across(names_q), half, shape, out)


def solution(mesh):
    placed = (
        P("dp", "tensor"),
        P("dp", "tensor"),
        P("tensor", None),
        P("tensor", None),
        P("tensor", None),
    )
    return jax.shard_map(local, mesh=mesh, in_specs=placed, out_specs=P("dp", None), check_vma=False)
```

time: 179 us -> 133 us (0.74)
  waiting for transfers between devices: 49.1 us -> 15 us
  starting transfers between devices: 18.2 us -> 47 us
  blocking collectives: 46.5 us -> 23 us
  other arithmetic: 10.5 us -> 2.79 us
  Pallas kernels: 50.9 us -> 43.8 us
  local copies, waits for them, and re-layouts: 2.68 us -> 0.42 us
    all_to_all x4 -> x1, waiting for transfers between devices: 48.5 us -> 0.01 us  [local(): rot = lax.all_to_all(turned, 'tensor', 0, 0)]
    ppermute x4 -> x24, starting transfers between devices: 2.4 us -> 42.5 us  [swap(): return lax.ppermute(x, 'tensor', [(i, i ^ mask) for i in range(shards)])]
    all_to_all x1 -> x0, blocking collectives: 23.5 us -> none  [local(): pieces = lax.all_to_all(chip, 'tensor', 0, 0, axis_index_groups=same_core)]
    ppermute x4 -> x24, waiting for transfers between devices: 0.58 us -> 15 us  [swap(): return lax.ppermute(x, 'tensor', [(i, i ^ mask) for i in range(shards)])]
    all_to_all x4 -> x1, starting transfers between devices: 15.8 us -> 4.56 us  [local(): rot = lax.all_to_all(turned, 'tensor', 0, 0)]
    pallas_call x3 -> x5, Pallas kernels: 30.2 us -> 23.1 us  [the longest x2 15.3 us: project(): pl.pallas_call(functools.partial(project_body, full), grid_spec=pltpu.Pre...]
    concatenate x1 -> x0, other arithmetic: 2.45 us -> none  [local(): return jnp.concatenate(outs, axis=1)]
    convert_element_type x3 -> x5, other arithmetic: 4.63 us -> 2.33 us  [the longest x1 1.93 us: local(): (jax.nn.silu(gate_input.astype(f32)) * up_input.astype(f32)).astype(bf16)]
  transfers between devices with their start and end apart: 8 -> 25, of which waited for: 4 -> 8; matrix products, arithmetic and copies ran while one was open for 5% -> 1% of each run, Pallas kernels for 17% -> 23%
where the time goes in v2:
time: 133 us; the launch traced here: 132 us
  starting transfers between devices  47 us (35%)
  Pallas kernels  43.8 us (33%)
  blocking collectives  23 us (17%)
  waiting for transfers between devices  15 us (11%)
  other arithmetic  2.79 us (2%)
    ppermute x24, starting transfers between devices, swap(): return lax.ppermute(x, 'tensor', [(i, i ^ mask) for i in range(shards)])  42.5 us
    all_to_all x1, blocking collectives, local(): lax.all_to_all(hidden.reshape(shards, rows, local_ff), 'tensor', 0, 0)  23 us
    pallas_call x1, Pallas kernels, dequant(): pl.pallas_call(dequant_body, grid=(width // tile,), in_specs=[pl.BlockSpe...  20.7 us
    pallas_call x2, Pallas kernels, project(): pl.pallas_call(functools.partial(project_body, full), grid_spec=pltpu.Pre...  15.3 us
    ppermute x24, waiting for transfers between devices, swap(): return lax.ppermute(x, 'tensor', [(i, i ^ mask) for i in range(shards)])  15 us
    pallas_call x1, Pallas kernels, rotate(): pl.pallas_call(rotate_body, grid=(pl.cdiv(depth, tile),), in_specs=[pl.Bl...  4.93 us
    all_to_all x1, starting transfers between devices, local(): rot = lax.all_to_all(turned, 'tensor', 0, 0)  4.56 us
    pallas_call x2, Pallas kernels, put(): pl.pallas_call(functools.partial(place_body, names, first, width, count),...  2.88 us
  transfers between devices with their start and end apart: 25, of which 8 were waited for; matrix products, arithmetic and copies ran while one was open for 1% of the time, Pallas kernels for 23%

profile of v2, /device:TPU:1, one launch (start us, length us, event | category | flops | bytes accessed | tf_op | source)
XLA Modules:
  0.0 132.1 jit_solution(9396248594383947812)
XLA Ops:
  0.0 1.9 %fusion.4 = bf16[256,1664]{1,0:T(8,128)(2,1)S(1)} fusion(bf16[256,1664]{1,0:T(8,128)(2,1)} %param.7, bf16[256,1664]{1,0:T(8,128)(2,1)} %param.6), kind=kLoop, calls=%fused_computation.6 | loop fusion | flops 3407872 | bytes 2555904 | tf_op jit(solution)/shard_map/convert_element_type | solution.py:236
  1.9 23.0 %all_to_all.10.hidden_ref = bf16[16,16,1664]{2,1,0:T(8,128)(2,1)S(1)} all-to-all(bf16[16,16,1664]{2,1,0:T(8,128)(2,1)S(1)} %bitcast.33), channel_id=1, replica_groups=mesh['dp'=8,'tensor'=16] {'tensor'}, dimensions={0} | all-to-all | bytes 1703936 | tf_op jit(solution)/shard_map/all_to_all | solution.py:237
  24.9 4.9 %rotate.1 = bf16[16,16,1664]{2,1,0:T(8,128)(2,1)} custom-call(bf16[16,16,1664]{2,1,0:T(8,128)(2,1)S(1)} %all_to_all.10.hidden_ref, bf16[1664,1664]{1,0:T(8,128)(2,1)} %constant.9.clone.table_ref), custom_call_target="tpu_custom_call" | custom-call | flops 1417674752 | bytes 7241728 | tf_op jit(solution)/shard_map/rotate/pallas_call | solution.py:74
  29.8 4.6 %all-to-all-start.1 = ((bf16[16,16,1664]{2,1,0:T(8,128)(2,1)}), bf16[16,16,1664]{2,1,0:T(8,128)(2,1)S(1)}, u32[]{:S(2)}, u32[]{:S(2)}) async-start(bf16[16,16,1664]{2,1,0:T(8,128)(2,1)} %rotate.1), calls=%async_computation.1 | async-start | bytes 1703936 | tf_op jit(solution)/shard_map/all_to_all | solution.py:239
  34.8 20.7 %dequant.1.weight_ref = bf16[13,8,16,8192]{3,2,1,0:T(8,128)(2,1)} custom-call(s32[13,16,8192]{2,1,0:T(8,128)} %bitcast.31, s32[13,16,8192]{2,1,0:T(8,128)} %bitcast.32, bf16[13,1,8192]{2,1,0:T(2,128)(2,1)S(1)} %copy.8.scale_ref), custom_call_target="tpu_custom_call" | custom-call | flops 109051904 | bytes 40894464 | tf_op jit(solution)/shard_map/dequant/pallas_call | solution.py:108
  55.5 7.7 %project.3 = (bf16[8,16,4096]{2,1,0:T(8,128)(2,1)S(1)}, bf16[8,16,4096]{2,1,0:T(8,128)(2,1)S(1)}) custom-call(s32[1]{0:T(128)} %bitcast.place_ref, bf16[16,16,1664]{2,1,0:T(8,128)(2,1)S(1)} %all-to-all-done.1.rot_ref, bf16[13,8,16,8192]{3,2,1,0:T(8,128)(2,1)} %dequant.1.weight_ref), custom_call_target="tpu_custom_call" | custom-call | flops 3489660928 | bytes 17825792 | tf_op jit(solution)/shard_map/project/pallas_call | solution.py:152
  63.5 7.7 %project.2 = (bf16[8,16,4096]{2,1,0:T(8,128)(2,1)S(1)}, bf16[8,16,4096]{2,1,0:T(8,128)(2,1)S(1)}) custom-call(s32[1]{0:T(128)} %bitcast.place_ref, bf16[16,16,1664]{2,1,0:T(8,128)(2,1)S(1)} %all-to-all-done.1.rot_ref, bf16[13,8,16,8192]{3,2,1,0:T(8,128)(2,1)} %dequant.1.weight_ref), custom_call_target="tpu_custom_call" | custom-call | flops 3489660928 | bytes 17825792 | tf_op jit(solution)/shard_map/project/pallas_call | solution.py:152
  71.7 2.7 %collective-permute-start.14 = (bf16[2,16,4096]{2,1,0:T(8,128)(2,1)S(1)}, bf16[2,16,4096]{2,1,0:T(8,128)(2,1)S(1)}, u32[]{:S(2)}, u32[]{:S(2)}) collective-permute-start(bf16[2,16,4096]{2,1,0:T(8,128)(2,1)S(1)} %get-tuple-element.16), channel_id=1, source_target_pairs={{0,6},{1,7},{2,4},{3,5},{4,2},{5,3},{6,0},{7,1},{8,14},{9,15},{10,... | collective-permute-start | bytes 786440 | tf_op jit(solution)/shard_map/ppermute | solution.py:229
  75.8 3.0 %collective-permute-start.1 = (bf16[4,16,4096]{2,1,0:T(8,128)(2,1)S(1)}, bf16[4,16,4096]{2,1,0:T(8,128)(2,1)S(1)}, u32[]{:S(2)}, u32[]{:S(2)}) collective-permute-start(bf16[4,16,4096]{2,1,0:T(8,128)(2,1)S(1)} %add_convert_fusion), channel_id=1, source_target_pairs={{0,8},{1,9},{2,10},{3,11},{4,12},{5,13},{6,14},{7,15},{8,0},{9,1},... | collective-permute-start | bytes 1572872 | tf_op jit(solution)/shard_map/ppermute | solution.py:229
  78.8 1.9 %collective-permute-done.14 = bf16[2,16,4096]{2,1,0:T(8,128)(2,1)S(1)} collective-permute-done((bf16[2,16,4096]{2,1,0:T(8,128)(2,1)S(1)}, bf16[2,16,4096]{2,1,0:T(8,128)(2,1)S(1)}, u32[]{:S(2)}, u32[]{:S(2)}) %collective-permute-start.14) | collective-permute-done | bytes 262176 | tf_op jit(solution)/shard_map/ppermute | solution.py:229
  81.6 5.6 %collective-permute-done.12 = bf16[2,16,4096]{2,1,0:T(8,128)(2,1)S(1)} collective-permute-done((bf16[2,16,4096]{2,1,0:T(8,128)(2,1)S(1)}, bf16[2,16,4096]{2,1,0:T(8,128)(2,1)S(1)}, u32[]{:S(2)}, u32[]{:S(2)}) %collective-permute-start.12) | collective-permute-done | bytes 262176 | tf_op jit(solution)/shard_map/ppermute | solution.py:229
  87.4 2.4 %collective-permute-done.1 = bf16[4,16,4096]{2,1,0:T(8,128)(2,1)S(1)} collective-permute-done((bf16[4,16,4096]{2,1,0:T(8,128)(2,1)S(1)}, bf16[4,16,4096]{2,1,0:T(8,128)(2,1)S(1)}, u32[]{:S(2)}, u32[]{:S(2)}) %collective-permute-start.1) | collective-permute-done | bytes 524320 | tf_op jit(solution)/shard_map/ppermute | solution.py:229
  90.0 2.5 %collective-permute-start.4 = (bf16[16,4096]{1,0:T(8,128)(2,1)S(1)}, bf16[16,4096]{1,0:T(8,128)(2,1)S(1)}, u32[]{:S(2)}, u32[]{:S(2)}) collective-permute-start(bf16[16,4096]{1,0:T(8,128)(2,1)S(1)} %get-tuple-element.19), channel_id=1, source_target_pairs={{0,6},{1,7},{2,4},{3,5},{4,2},{5,3},{6,0},{7,1},{8,14},{9,15},{10,... | collective-permute-start | bytes 393224 | tf_op jit(solution)/shard_map/ppermute | solution.py:229
  92.5 1.5 %collective-permute-start.2 = (bf16[16,4096]{1,0:T(8,128)(2,1)S(1)}, bf16[16,4096]{1,0:T(8,128)(2,1)S(1)}, u32[]{:S(2)}, u32[]{:S(2)}) collective-permute-start(bf16[16,4096]{1,0:T(8,128)(2,1)S(1)} %get-tuple-element.18), channel_id=1, source_target_pairs={{0,4},{1,5},{2,6},{3,7},{4,0},{5,1},{6,2},{7,3},{8,12},{9,13},{10,... | collective-permute-start | bytes 393224 | tf_op jit(solution)/shard_map/ppermute | solution.py:229
  94.0 2.8 %collective-permute-start.15 = (bf16[16,4096]{1,0:T(8,128)(2,1)S(1)}, bf16[16,4096]{1,0:T(8,128)(2,1)S(1)}, u32[]{:S(2)}, u32[]{:S(2)}) collective-permute-start(bf16[16,4096]{1,0:T(8,128)(2,1)S(1)} %fusion.9), channel_id=1, source_target_pairs={{0,8},{1,9},{2,10},{3,11},{4,12},{5,13},{6,14},{7,15},{8,0},{9,1},... | collective-permute-start | bytes 393224 | tf_op jit(solution)/shard_map/ppermute | solution.py:229
  98.2 2.2 %collective-permute-start.7 = (bf16[16,4096]{1,0:T(8,128)(2,1)S(1)}, bf16[16,4096]{1,0:T(8,128)(2,1)S(1)}, u32[]{:S(2)}, u32[]{:S(2)}) collective-permute-start(bf16[16,4096]{1,0:T(8,128)(2,1)S(1)} %fusion.8), channel_id=1, source_target_pairs={{0,6},{1,7},{2,4},{3,5},{4,2},{5,3},{6,0},{7,1},{8,14},{9,15},{10,... | collective-permute-start | bytes 393224 | tf_op jit(solution)/shard_map/ppermute | solution.py:229
  101.6 2.9 %collective-permute-start.16 = (bf16[16,4096]{1,0:T(8,128)(2,1)S(1)}, bf16[16,4096]{1,0:T(8,128)(2,1)S(1)}, u32[]{:S(2)}, u32[]{:S(2)}) collective-permute-start(bf16[16,4096]{1,0:T(8,128)(2,1)S(1)} %fusion.6), channel_id=1, source_target_pairs={{0,8},{1,9},{2,10},{3,11},{4,12},{5,13},{6,14},{7,15},{8,0},{9,1},... | collective-permute-start | bytes 393224 | tf_op jit(solution)/shard_map/ppermute | solution.py:229
  105.8 2.8 %collective-permute-start.8 = (bf16[4,16,4096]{2,1,0:T(8,128)(2,1)S(1)}, bf16[4,16,4096]{2,1,0:T(8,128)(2,1)S(1)}, u32[]{:S(2)}, u32[]{:S(2)}) collective-permute-start(bf16[4,16,4096]{2,1,0:T(8,128)(2,1)S(1)} %pad_maximum_fusion.refs_0_), channel_id=1, source_target_pairs={{0,8},{1,9},{2,10},{3,11},{4,12},{5,13},{6,14},{7,15},{8,0},{9,1},... | collective-permute-start | bytes 1572872 | tf_op jit(solution)/shard_map/ppermute | solution.py:229
  108.6 1.5 %collective-permute-start.17 = (bf16[2,16,4096]{2,1,0:T(8,128)(2,1)S(1)}, bf16[2,16,4096]{2,1,0:T(8,128)(2,1)S(1)}, u32[]{:S(2)}, u32[]{:S(2)}) collective-permute-start(bf16[2,16,4096]{2,1,0:T(8,128)(2,1)S(1)} %pad_maximum_fusion.1.refs_0_), channel_id=1, source_target_pairs={{0,2},{1,3},{2,0},{3,1},{4,6},{5,7},{6,4},{7,5},{8,10},{9,11},{10,... | collective-permute-start | bytes 786440 | tf_op jit(solution)/shard_map/ppermute | solution.py:229
  112.6 6.0 %collective-permute-start.20 = (bf16[2,16,4096]{2,1,0:T(8,128)(2,1)S(1)}, bf16[2,16,4096]{2,1,0:T(8,128)(2,1)S(1)}, u32[]{:S(2)}, u32[]{:S(2)}) collective-permute-start(bf16[2,16,4096]{2,1,0:T(8,128)(2,1)S(1)} %pad_maximum_fusion.1.refs_0_), channel_id=1, source_target_pairs={{0,1},{1,0},{2,3},{3,2},{4,5},{5,4},{6,7},{7,6},{8,9},{9,8},{10,11... | collective-permute-start | bytes 786440 | tf_op jit(solution)/shard_map/ppermute | solution.py:229
  118.6 1.7 %collective-permute-start.9 = (bf16[4,16,4096]{2,1,0:T(8,128)(2,1)S(1)}, bf16[4,16,4096]{2,1,0:T(8,128)(2,1)S(1)}, u32[]{:S(2)}, u32[]{:S(2)}) collective-permute-start(bf16[4,16,4096]{2,1,0:T(8,128)(2,1)S(1)} %pad_maximum_fusion.refs_0_), channel_id=1, source_target_pairs={{0,1},{1,0},{2,3},{3,2},{4,5},{5,4},{6,7},{7,6},{8,9},{9,8},{10,11... | collective-permute-start | bytes 1572872 | tf_op jit(solution)/shard_map/ppermute | solution.py:229
  120.3 2.8 %collective-permute-start.10 = (bf16[4,16,4096]{2,1,0:T(8,128)(2,1)S(1)}, bf16[4,16,4096]{2,1,0:T(8,128)(2,1)S(1)}, u32[]{:S(2)}, u32[]{:S(2)}) collective-permute-start(bf16[4,16,4096]{2,1,0:T(8,128)(2,1)S(1)} %collective-permute-done.8.refs_1_), channel_id=1, source_target_pairs={{0,1},{1,0},{2,3},{3,2},{4,5},{5,4},{6,7},{7,6},{8,9},{9,8},{10,11... | collective-permute-start | bytes 1572872 | tf_op jit(solution)/shard_map/ppermute | solution.py:229
  123.1 1.9 %collective-permute-start.21 = (bf16[2,16,4096]{2,1,0:T(8,128)(2,1)S(1)}, bf16[2,16,4096]{2,1,0:T(8,128)(2,1)S(1)}, u32[]{:S(2)}, u32[]{:S(2)}) collective-permute-start(bf16[2,16,4096]{2,1,0:T(8,128)(2,1)S(1)} %collective-permute-done.17.refs_1_), channel_id=1, source_target_pairs={{0,1},{1,0},{2,3},{3,2},{4,5},{5,4},{6,7},{7,6},{8,9},{9,8},{10,11... | collective-permute-start | bytes 786440 | tf_op jit(solution)/shard_map/ppermute | solution.py:229
  125.0 2.7 %collective-permute-start.22 = (bf16[2,16,4096]{2,1,0:T(8,128)(2,1)S(1)}, bf16[2,16,4096]{2,1,0:T(8,128)(2,1)S(1)}, u32[]{:S(2)}, u32[]{:S(2)}) collective-permute-start(bf16[2,16,4096]{2,1,0:T(8,128)(2,1)S(1)} %collective-permute-done.18.refs_2_), channel_id=1, source_target_pairs={{0,1},{1,0},{2,3},{3,2},{4,5},{5,4},{6,7},{7,6},{8,9},{9,8},{10,11... | collective-permute-start | bytes 786440 | tf_op jit(solution)/shard_map/ppermute | solution.py:229
  (47 shorter events, 14.9 us)
Async XLA Ops:
  29.8 25.6 %all-to-all-start.1 = ((bf16[16,16,1664]{2,1,0:T(8,128)(2,1)}), bf16[16,16,1664]{2,1,0:T(8,128)(2,1)S(1)}, u32[]{:S(2)}, u32[]{:S(2)}) async-start(bf16[16,16,1664]{2,1,0:T(8,128)(2,1)} %rotate.1), calls=%async_computation.1 | async-start | bytes 1703936 | tf_op jit(solution)/shard_map/all_to_all | solution.py:239
  63.1 8.3 %collective-permute-start.11 = (bf16[8,16,4096]{2,1,0:T(8,128)(2,1)S(1)}, bf16[8,16,4096]{2,1,0:T(8,128)(2,1)S(1)}, u32[]{:S(2)}, u32[]{:S(2)}) collective-permute-start(bf16[8,16,4096]{2,1,0:T(8,128)(2,1)S(1)} %get-tuple-element.12), channel_id=1, source_target_pairs={{0,1},{1,0},{2,3},{3,2},{4,5},{5,4},{6,7},{7,6},{8,9},{9,8},{10,11... | collective-permute-start | bytes 3145736 | tf_op jit(solution)/shard_map/ppermute | solution.py:229
  71.1 4.5 %collective-permute-start = (bf16[8,16,4096]{2,1,0:T(8,128)(2,1)S(1)}, bf16[8,16,4096]{2,1,0:T(8,128)(2,1)S(1)}, u32[]{:S(2)}, u32[]{:S(2)}) collective-permute-start(bf16[8,16,4096]{2,1,0:T(8,128)(2,1)S(1)} %get-tuple-element.10), channel_id=1, source_target_pairs={{0,1},{1,0},{2,3},{3,2},{4,5},{5,4},{6,7},{7,6},{8,9},{9,8},{10,11... | collective-permute-start | bytes 3145736 | tf_op jit(solution)/shard_map/ppermute | solution.py:229
  71.7 9.0 %collective-permute-start.14 = (bf16[2,16,4096]{2,1,0:T(8,128)(2,1)S(1)}, bf16[2,16,4096]{2,1,0:T(8,128)(2,1)S(1)}, u32[]{:S(2)}, u32[]{:S(2)}) collective-permute-start(bf16[2,16,4096]{2,1,0:T(8,128)(2,1)S(1)} %get-tuple-element.16), channel_id=1, source_target_pairs={{0,6},{1,7},{2,4},{3,5},{4,2},{5,3},{6,0},{7,1},{8,14},{9,15},{10,... | collective-permute-start | bytes 786440 | tf_op jit(solution)/shard_map/ppermute | solution.py:229
  74.4 7.2 %collective-permute-start.13 = (bf16[2,16,4096]{2,1,0:T(8,128)(2,1)S(1)}, bf16[2,16,4096]{2,1,0:T(8,128)(2,1)S(1)}, u32[]{:S(2)}, u32[]{:S(2)}) collective-permute-start(bf16[2,16,4096]{2,1,0:T(8,128)(2,1)S(1)} %get-tuple-element.17), channel_id=1, source_target_pairs={{0,2},{1,3},{2,0},{3,1},{4,6},{5,7},{6,4},{7,5},{8,10},{9,11},{10,... | collective-permute-start | bytes 786440 | tf_op jit(solution)/shard_map/ppermute | solution.py:229
  74.4 12.8 %collective-permute-start.12 = (bf16[2,16,4096]{2,1,0:T(8,128)(2,1)S(1)}, bf16[2,16,4096]{2,1,0:T(8,128)(2,1)S(1)}, u32[]{:S(2)}, u32[]{:S(2)}) collective-permute-start(bf16[2,16,4096]{2,1,0:T(8,128)(2,1)S(1)} %get-tuple-element.15), channel_id=1, source_target_pairs={{0,4},{1,5},{2,6},{3,7},{4,0},{5,1},{6,2},{7,3},{8,12},{9,13},{10,... | collective-permute-start | bytes 786440 | tf_op jit(solution)/shard_map/ppermute | solution.py:229
  75.8 14.0 %collective-permute-start.1 = (bf16[4,16,4096]{2,1,0:T(8,128)(2,1)S(1)}, bf16[4,16,4096]{2,1,0:T(8,128)(2,1)S(1)}, u32[]{:S(2)}, u32[]{:S(2)}) collective-permute-start(bf16[4,16,4096]{2,1,0:T(8,128)(2,1)S(1)} %add_convert_fusion), channel_id=1, source_target_pairs={{0,8},{1,9},{2,10},{3,11},{4,12},{5,13},{6,14},{7,15},{8,0},{9,1},... | collective-permute-start | bytes 1572872 | tf_op jit(solution)/shard_map/ppermute | solution.py:229
  90.0 6.8 %collective-permute-start.4 = (bf16[16,4096]{1,0:T(8,128)(2,1)S(1)}, bf16[16,4096]{1,0:T(8,128)(2,1)S(1)}, u32[]{:S(2)}, u32[]{:S(2)}) collective-permute-start(bf16[16,4096]{1,0:T(8,128)(2,1)S(1)} %get-tuple-element.19), channel_id=1, source_target_pairs={{0,6},{1,7},{2,4},{3,5},{4,2},{5,3},{6,0},{7,1},{8,14},{9,15},{10,... | collective-permute-start | bytes 393224 | tf_op jit(solution)/shard_map/ppermute | solution.py:229
  92.5 4.3 %collective-permute-start.3 = (bf16[16,4096]{1,0:T(8,128)(2,1)S(1)}, bf16[16,4096]{1,0:T(8,128)(2,1)S(1)}, u32[]{:S(2)}, u32[]{:S(2)}) collective-permute-start(bf16[16,4096]{1,0:T(8,128)(2,1)S(1)} %get-tuple-element.20), channel_id=1, source_target_pairs={{0,2},{1,3},{2,0},{3,1},{4,6},{5,7},{6,4},{7,5},{8,10},{9,11},{10,... | collective-permute-start | bytes 393224 | tf_op jit(solution)/shard_map/ppermute | solution.py:229
  92.5 5.6 %collective-permute-start.2 = (bf16[16,4096]{1,0:T(8,128)(2,1)S(1)}, bf16[16,4096]{1,0:T(8,128)(2,1)S(1)}, u32[]{:S(2)}, u32[]{:S(2)}) collective-permute-start(bf16[16,4096]{1,0:T(8,128)(2,1)S(1)} %get-tuple-element.18), channel_id=1, source_target_pairs={{0,4},{1,5},{2,6},{3,7},{4,0},{5,1},{6,2},{7,3},{8,12},{9,13},{10,... | collective-permute-start | bytes 393224 | tf_op jit(solution)/shard_map/ppermute | solution.py:229
  94.0 7.6 %collective-permute-start.15 = (bf16[16,4096]{1,0:T(8,128)(2,1)S(1)}, bf16[16,4096]{1,0:T(8,128)(2,1)S(1)}, u32[]{:S(2)}, u32[]{:S(2)}) collective-permute-start(bf16[16,4096]{1,0:T(8,128)(2,1)S(1)} %fusion.9), channel_id=1, source_target_pairs={{0,8},{1,9},{2,10},{3,11},{4,12},{5,13},{6,14},{7,15},{8,0},{9,1},... | collective-permute-start | bytes 393224 | tf_op jit(solution)/shard_map/ppermute | solution.py:229
  98.2 6.3 %collective-permute-start.7 = (bf16[16,4096]{1,0:T(8,128)(2,1)S(1)}, bf16[16,4096]{1,0:T(8,128)(2,1)S(1)}, u32[]{:S(2)}, u32[]{:S(2)}) collective-permute-start(bf16[16,4096]{1,0:T(8,128)(2,1)S(1)} %fusion.8), channel_id=1, source_target_pairs={{0,6},{1,7},{2,4},{3,5},{4,2},{5,3},{6,0},{7,1},{8,14},{9,15},{10,... | collective-permute-start | bytes 393224 | tf_op jit(solution)/shard_map/ppermute | solution.py:229
  100.4 5.3 %collective-permute-start.6 = (bf16[16,4096]{1,0:T(8,128)(2,1)S(1)}, bf16[16,4096]{1,0:T(8,128)(2,1)S(1)}, u32[]{:S(2)}, u32[]{:S(2)}) collective-permute-start(bf16[16,4096]{1,0:T(8,128)(2,1)S(1)} %fusion.8), channel_id=1, source_target_pairs={{0,4},{1,5},{2,6},{3,7},{4,0},{5,1},{6,2},{7,3},{8,12},{9,13},{10,... | collective-permute-start | bytes 393224 | tf_op jit(solution)/shard_map/ppermute | solution.py:229
  101.4 4.2 %collective-permute-start.5 = (bf16[16,4096]{1,0:T(8,128)(2,1)S(1)}, bf16[16,4096]{1,0:T(8,128)(2,1)S(1)}, u32[]{:S(2)}, u32[]{:S(2)}) collective-permute-start(bf16[16,4096]{1,0:T(8,128)(2,1)S(1)} %fusion.8), channel_id=1, source_target_pairs={{0,2},{1,3},{2,0},{3,1},{4,6},{5,7},{6,4},{7,5},{8,10},{9,11},{10,... | collective-permute-start | bytes 393224 | tf_op jit(solution)/shard_map/ppermute | solution.py:229
  101.6 7.0 %collective-permute-start.16 = (bf16[16,4096]{1,0:T(8,128)(2,1)S(1)}, bf16[16,4096]{1,0:T(8,128)(2,1)S(1)}, u32[]{:S(2)}, u32[]{:S(2)}) collective-permute-start(bf16[16,4096]{1,0:T(8,128)(2,1)S(1)} %fusion.6), channel_id=1, source_target_pairs={{0,8},{1,9},{2,10},{3,11},{4,12},{5,13},{6,14},{7,15},{8,0},{9,1},... | collective-permute-start | bytes 393224 | tf_op jit(solution)/shard_map/ppermute | solution.py:229
  105.8 14.5 %collective-permute-start.8 = (bf16[4,16,4096]{2,1,0:T(8,128)(2,1)S(1)}, bf16[4,16,4096]{2,1,0:T(8,128)(2,1)S(1)}, u32[]{:S(2)}, u32[]{:S(2)}) collective-permute-start(bf16[4,16,4096]{2,1,0:T(8,128)(2,1)S(1)} %pad_maximum_fusion.refs_0_), channel_id=1, source_target_pairs={{0,8},{1,9},{2,10},{3,11},{4,12},{5,13},{6,14},{7,15},{8,0},{9,1},... | collective-permute-start | bytes 1572872 | tf_op jit(solution)/shard_map/ppermute | solution.py:229
  108.6 10.0 %collective-permute-start.17 = (bf16[2,16,4096]{2,1,0:T(8,128)(2,1)S(1)}, bf16[2,16,4096]{2,1,0:T(8,128)(2,1)S(1)}, u32[]{:S(2)}, u32[]{:S(2)}) collective-permute-start(bf16[2,16,4096]{2,1,0:T(8,128)(2,1)S(1)} %pad_maximum_fusion.1.refs_0_), channel_id=1, source_target_pairs={{0,2},{1,3},{2,0},{3,1},{4,6},{5,7},{6,4},{7,5},{8,10},{9,11},{10,... | collective-permute-start | bytes 786440 | tf_op jit(solution)/shard_map/ppermute | solution.py:229
  110.1 13.0 %collective-permute-start.18 = (bf16[2,16,4096]{2,1,0:T(8,128)(2,1)S(1)}, bf16[2,16,4096]{2,1,0:T(8,128)(2,1)S(1)}, u32[]{:S(2)}, u32[]{:S(2)}) collective-permute-start(bf16[2,16,4096]{2,1,0:T(8,128)(2,1)S(1)} %pad_maximum_fusion.1.refs_0_), channel_id=1, source_target_pairs={{0,4},{1,5},{2,6},{3,7},{4,0},{5,1},{6,2},{7,3},{8,12},{9,13},{10,... | collective-permute-start | bytes 786440 | tf_op jit(solution)/shard_map/ppermute | solution.py:229
  111.6 13.4 %collective-permute-start.19 = (bf16[2,16,4096]{2,1,0:T(8,128)(2,1)S(1)}, bf16[2,16,4096]{2,1,0:T(8,128)(2,1)S(1)}, u32[]{:S(2)}, u32[]{:S(2)}) collective-permute-start(bf16[2,16,4096]{2,1,0:T(8,128)(2,1)S(1)} %pad_maximum_fusion.1.refs_0_), channel_id=1, source_target_pairs={{0,6},{1,7},{2,4},{3,5},{4,2},{5,3},{6,0},{7,1},{8,14},{9,15},{10,... | collective-permute-start | bytes 786440 | tf_op jit(solution)/shard_map/ppermute | solution.py:229
  112.6 15.1 %collective-permute-start.20 = (bf16[2,16,4096]{2,1,0:T(8,128)(2,1)S(1)}, bf16[2,16,4096]{2,1,0:T(8,128)(2,1)S(1)}, u32[]{:S(2)}, u32[]{:S(2)}) collective-permute-start(bf16[2,16,4096]{2,1,0:T(8,128)(2,1)S(1)} %pad_maximum_fusion.1.refs_0_), channel_id=1, source_target_pairs={{0,1},{1,0},{2,3},{3,2},{4,5},{5,4},{6,7},{7,6},{8,9},{9,8},{10,11... | collective-permute-start | bytes 786440 | tf_op jit(solution)/shard_map/ppermute | solution.py:229
  118.6 12.1 %collective-permute-start.9 = (bf16[4,16,4096]{2,1,0:T(8,128)(2,1)S(1)}, bf16[4,16,4096]{2,1,0:T(8,128)(2,1)S(1)}, u32[]{:S(2)}, u32[]{:S(2)}) collective-permute-start(bf16[4,16,4096]{2,1,0:T(8,128)(2,1)S(1)} %pad_maximum_fusion.refs_0_), channel_id=1, source_target_pairs={{0,1},{1,0},{2,3},{3,2},{4,5},{5,4},{6,7},{7,6},{8,9},{9,8},{10,11... | collective-permute-start | bytes 1572872 | tf_op jit(solution)/shard_map/ppermute | solution.py:229
  120.3 10.4 %collective-permute-start.10 = (bf16[4,16,4096]{2,1,0:T(8,128)(2,1)S(1)}, bf16[4,16,4096]{2,1,0:T(8,128)(2,1)S(1)}, u32[]{:S(2)}, u32[]{:S(2)}) collective-permute-start(bf16[4,16,4096]{2,1,0:T(8,128)(2,1)S(1)} %collective-permute-done.8.refs_1_), channel_id=1, source_target_pairs={{0,1},{1,0},{2,3},{3,2},{4,5},{5,4},{6,7},{7,6},{8,9},{9,8},{10,11... | collective-permute-start | bytes 1572872 | tf_op jit(solution)/shard_map/ppermute | solution.py:229
  123.1 4.6 %collective-permute-start.21 = (bf16[2,16,4096]{2,1,0:T(8,128)(2,1)S(1)}, bf16[2,16,4096]{2,1,0:T(8,128)(2,1)S(1)}, u32[]{:S(2)}, u32[]{:S(2)}) collective-permute-start(bf16[2,16,4096]{2,1,0:T(8,128)(2,1)S(1)} %collective-permute-done.17.refs_1_), channel_id=1, source_target_pairs={{0,1},{1,0},{2,3},{3,2},{4,5},{5,4},{6,7},{7,6},{8,9},{9,8},{10,11... | collective-permute-start | bytes 786440 | tf_op jit(solution)/shard_map/ppermute | solution.py:229
  125.0 3.9 %collective-permute-start.22 = (bf16[2,16,4096]{2,1,0:T(8,128)(2,1)S(1)}, bf16[2,16,4096]{2,1,0:T(8,128)(2,1)S(1)}, u32[]{:S(2)}, u32[]{:S(2)}) collective-permute-start(bf16[2,16,4096]{2,1,0:T(8,128)(2,1)S(1)} %collective-permute-done.18.refs_2_), channel_id=1, source_target_pairs={{0,1},{1,0},{2,3},{3,2},{4,5},{5,4},{6,7},{7,6},{8,9},{9,8},{10,11... | collective-permute-start | bytes 786440 | tf_op jit(solution)/shard_map/ppermute | solution.py:229
  (2 other events, 6.1 us)

commit v3 on v2

v3 whole, which is shorter than its diff:
```python
import functools
import math

import jax
import jax.numpy as jnp
import numpy as np
from jax import lax
from jax.experimental import pallas as pl
from jax.experimental.pallas import tpu as pltpu
from jax.sharding import PartitionSpec as P

FF = 26624
GROUP = 128
CODE_FLIP = 0x8888
VMEM_LIMIT = 32 * 1024 * 1024


def paley_table():
    elements = [(u, v) for v in range(5) for u in range(5)]
    squares = set()
    for u, v in elements:
        if u != 0 or v != 0:
            squares.add(((u * u + 2 * v * v) % 5, 2 * u * v % 5))
    quad = np.zeros((25, 25))
    for i, first in enumerate(elements):
        for j, second in enumerate(elements):
            diff = ((first[0] - second[0]) % 5, (first[1] - second[1]) % 5)
            if diff != (0, 0):
                quad[i, j] = 1.0 if diff in squares else -1.0
    core = np.zeros((26, 26))
    core[0, 1:] = 1.0
    core[1:, 0] = 1.0
    core[1:, 1:] = quad
    return np.kron(core, np.array([[1.0, 1.0], [1.0, -1.0]])) + np.kron(
        np.eye(26), np.array([[1.0, -1.0], [-1.0, -1.0]])
    )


def sylvester(order):
    table = np.ones((1, 1))
    while table.shape[0] < order:
        table = np.kron(np.array([[1.0, 1.0], [1.0, -1.0]]), table)
    return table


def local_table(local_ff):
    table = np.kron(sylvester(local_ff // 52), paley_table())
    order = np.arange(local_ff).reshape(-1, GROUP // 8, 8).transpose(0, 2, 1).reshape(-1)
    tile = 512
    table = np.pad(table[:, order], ((0, 0), (0, -local_ff % tile)))
    return jnp.asarray(table.reshape(local_ff, -1, tile).transpose(1, 0, 2), jnp.bfloat16)


def in_hbm(x):
    return pltpu.with_memory_space_constraint(x, pltpu.HBM)


def rotate_body(hidden_ref, table_ref, out_ref, table_buf, sems):
    shards, rows, depth = hidden_ref.shape
    tiles, _, tile = table_buf.shape
    copies = [pltpu.make_async_copy(table_ref.at[j], table_buf.at[j], sems.at[j]) for j in range(tiles)]
    for copy in copies:
        copy.start()
    flat = hidden_ref[...].reshape(shards * rows, depth)
    for j in range(tiles):
        copies[j].wait()
        turned = jnp.dot(flat, table_buf[j], preferred_element_type=jnp.float32)
        parts = [turned[rows * s : rows * (s + 1)] for s in range(shards)]
        step = 1
        while step < shards:
            parts = [
                parts[s] + parts[s + step] if s & step == 0 else parts[s - step] - parts[s]
                for s in range(shards)
            ]
            step *= 2
        used = min(tile, depth - tile * j)
        for s in range(shards):
            scaled = (parts[s] * (1.0 / math.sqrt(FF))).astype(jnp.bfloat16)
            out_ref[s, :, tile * j : tile * j + used] = scaled[:, :used]


def rotate(hidden, table):
    shards, rows, depth = hidden.shape
    return pl.pallas_call(
        rotate_body,
        in_specs=[pl.BlockSpec(memory_space=pltpu.VMEM), pl.BlockSpec(memory_space=pltpu.HBM)],
        out_specs=pl.BlockSpec(memory_space=pltpu.VMEM),
        out_shape=jax.ShapeDtypeStruct(hidden.shape, jnp.bfloat16),
        scratch_shapes=[
            pltpu.VMEM(table.shape, jnp.bfloat16),
            pltpu.SemaphoreType.DMA((table.shape[0],)),
        ],
        compiler_params=pltpu.CompilerParams(vmem_limit_bytes=VMEM_LIMIT),
        cost_estimate=pl.CostEstimate(
            flops=2 * shards * rows * depth * depth,
            bytes_accessed=2 * depth * depth + 4 * shards * rows * depth,
            transcendentals=0,
        ),
        name="rotate",
    )(hidden, in_hbm(table))


def unpack(low_ref, high_ref, scale_ref, first, out_ref):
    depth, tile = out_ref.shape
    words = GROUP // 8
    cols = slice(first, first + tile)
    for g in range(depth // GROUP):
        scale = jnp.broadcast_to(scale_ref[g : g + 1, cols].astype(jnp.float32), (words, tile))
        for half, ref in enumerate((low_ref, high_ref)):
            nibbles = (ref[words * g : words * (g + 1), cols] + 34952) ^ CODE_FLIP
            for k in range(4):
                code = (nibbles << (28 - 4 * k)) >> 28
                row = GROUP * g + words * (4 * half + k)
                out_ref[row : row + words] = (code.astype(jnp.float32) * scale).astype(jnp.bfloat16)


def project_body(order, place_ref, rot_ref, low_ref, high_ref, scale_ref, keep_ref, send_ref, lhs_ref, weight_ref):
    shards, rows, depth = rot_ref.shape
    tile = weight_ref.shape[1]

    @pl.when(pl.program_id(0) == 0)
    def _():
        for at, block in enumerate(order):
            lhs_ref[rows * at : rows * (at + 1)] = rot_ref[jnp.bitwise_xor(place_ref[0], block)]

    for first in range(0, keep_ref.shape[2], tile):
        unpack(low_ref, high_ref, scale_ref, first, weight_ref)
        term = jnp.dot(lhs_ref[...], weight_ref[...], preferred_element_type=jnp.float32)
        both = term.astype(jnp.bfloat16).reshape(2, shards // 2, rows, tile)
        send_ref[:, :, first : first + tile] = both[0]
        keep_ref[:, :, first : first + tile] = both[1]


def project(place, rot, low, high, scales, order, first, width):
    shards, rows, depth = rot.shape
    tile = 512
    step = 2 * tile
    start = first // step
    full = tuple(q ^ 1 for q in order) + tuple(order)
    shape = jax.ShapeDtypeStruct((shards // 2, rows, width), jnp.bfloat16)

    def columns(j, p):
        return (0, start + j)

    return pl.pallas_call(
        functools.partial(project_body, full),
        grid_spec=pltpu.PrefetchScalarGridSpec(
            num_scalar_prefetch=1,
            grid=(width // step,),
            in_specs=[
                pl.BlockSpec((shards, rows, depth), lambda j, p: (0, 0, 0)),
                pl.BlockSpec((low.shape[0], step), columns),
                pl.BlockSpec((high.shape[0], step), columns),
                pl.BlockSpec((scales.shape[0], step), columns),
            ],
            out_specs=[pl.BlockSpec((shards // 2, rows, step), lambda j, p: (0, 0, j))] * 2,
            scratch_shapes=[
                pltpu.VMEM((shards * rows, depth), jnp.bfloat16),
                pltpu.VMEM((depth, tile), jnp.bfloat16),
            ],
        ),
        out_shape=[shape, shape],
        compiler_params=pltpu.CompilerParams(vmem_limit_bytes=VMEM_LIMIT),
        cost_estimate=pl.CostEstimate(
            flops=2 * shards * rows * depth * width,
            bytes_accessed=depth * width + 4 * shards * rows * width,
            transcendentals=0,
        ),
        name="project",
    )(place, rot, in_hbm(low), in_hbm(high), in_hbm(scales))


def put_body(names, firsts, place_ref, *refs):
    pieces, out_ref, sems = refs[:-2], refs[-2], refs[-1]
    copies = []
    for piece, blocks, first in zip(pieces, names, firsts):
        _, rows, width = piece.shape
        for at, block in enumerate(blocks):
            start = pl.multiple_of(jnp.bitwise_xor(place_ref[0], block) * rows, rows)
            copies.append(
                pltpu.make_async_copy(
                    piece.at[at],
                    out_ref.at[pl.ds(start, rows), pl.ds(first, width)],
                    sems.at[len(copies)],
                )
            )
    for copy in copies:
        copy.start()
    for copy in copies:
        copy.wait()


def put(place, pieces, names, firsts, shape):
    return pl.pallas_call(
        functools.partial(put_body, names, firsts),
        in_specs=[pl.BlockSpec(memory_space=pltpu.SMEM)] + [pl.BlockSpec(memory_space=pl.ANY)] * len(pieces),
        out_specs=pl.BlockSpec(memory_space=pl.ANY),
        out_shape=jax.ShapeDtypeStruct(shape, jnp.bfloat16),
        scratch_shapes=[pltpu.SemaphoreType.DMA((sum(map(len, names)),))],
        compiler_params=pltpu.CompilerParams(vmem_limit_bytes=VMEM_LIMIT),
        cost_estimate=pl.CostEstimate(
            flops=0, bytes_accessed=4 * sum(p.size for p in pieces), transcendentals=0
        ),
        name="put",
    )(place, *pieces)


def local(gate_input, up_input, down_low, down_high, down_scales):
    shards = lax.axis_size("tensor")
    total_rows, local_ff = gate_input.shape
    rows = total_rows // shards
    width = down_low.shape[1]
    left = width // 8 * 5
    place = lax.axis_index("tensor").astype(jnp.int32).reshape(1)
    f32, bf16 = jnp.float32, jnp.bfloat16

    def swap(x, mask):
        return lax.ppermute(x, "tensor", [(i, i ^ mask) for i in range(shards)])

    CORE, Y = 1, 8
    X = (0, 2, 4, 6)
    by_x = tuple(x | y for x in X for y in (0, Y))
    by_y = tuple(x | y for y in (0, Y) for x in X)

    hidden = (jax.nn.silu(gate_input.astype(f32)) * up_input.astype(f32)).astype(bf16)
    mine = lax.all_to_all(hidden.reshape(shards, rows, local_ff), "tensor", 0, 0)
    turned = rotate(mine, local_table(local_ff))
    rot = lax.all_to_all(turned, "tensor", 0, 0)
    codes = (down_low, down_high, down_scales)

    keep_p, send_p = project(place, rot, *codes, by_x, 0, left)
    got_p = swap(send_p, CORE)
    keep_q, send_q = project(place, rot, *codes, by_y, left, width - left)
    got_q = swap(send_q, CORE)

    def chip_p(k):
        at = slice(2 * k, 2 * k + 2)
        return keep_p[at].astype(f32) + got_p[at].astype(f32)

    def chip_q(y):
        at = slice(4 * y, 4 * y + 4)
        return keep_q[at].astype(f32) + got_q[at].astype(f32)

    along_x = [swap(chip_p(k).astype(bf16), X[k]) for k in (2, 1, 3)]
    along_y = swap(chip_q(1).astype(bf16), Y)
    sum_p = chip_p(0) + sum(t.astype(f32) for t in along_x)
    sum_q = chip_q(0) + along_y.astype(f32)

    mine_p = lax.reduce_precision(sum_p, 8, 7)
    theirs_p = swap(mine_p.astype(bf16), Y)
    last_q = [swap(sum_q[k].astype(bf16), X[k]) for k in (2, 1, 3)]
    done_p = (mine_p + theirs_p[::-1].astype(f32)).astype(bf16)
    done_q = (sum_q[0] + sum(t.astype(f32) for t in last_q)).astype(bf16)

    all_p = [done_p] + [swap(done_p, X[k]) for k in (2, 1, 3)]
    row_q = jnp.stack([done_q] + [swap(done_q, X[k]) for k in (1, 2, 3)])
    all_q = [row_q, swap(row_q, Y)]
    names_p = [tuple(X[k] | y for y in (0, Y)) for k in (0, 2, 1, 3)]
    names_q = [tuple(x | y for x in X) for y in (0, Y)]
    near = all_p + all_q
    names = names_p + names_q
    far = [swap(t, CORE) for t in near]
    names += [tuple(q | CORE for q in blocks) for blocks in names]
    firsts = [0] * len(all_p) + [left] * len(all_q)
    return put(place, near + far, names, firsts * 2, (total_rows, width))


def solution(mesh):
    placed = (
        P("dp", "tensor"),
        P("dp", "tensor"),
        P("tensor", None),
        P("tensor", None),
        P("tensor", None),
    )
    return jax.shard_map(local, mesh=mesh, in_specs=placed, out_specs=P("dp", None), check_vma=False)
```

time: 133 us -> 127 us (0.955)
  waiting for transfers between devices: 15 us -> 44.6 us
  Pallas kernels: 43.8 us -> 23.9 us
  starting transfers between devices: 47 us -> 32.2 us
    pallas_call x4 -> x2, Pallas kernels: 28.5 us -> 7.61 us  [the longest x1 5.34 us: rotate(): pl.pallas_call(rotate_body, in_specs=[pl.BlockSpec(memory_space=pltpu.VME...]
    all_to_all x1, waiting for transfers between devices: 0.01 us -> 15.4 us  [local(): rot = lax.all_to_all(turned, 'tensor', 0, 0)]
    ppermute x24 -> x23, starting transfers between devices: 42.5 us -> 27.7 us  [swap(): return lax.ppermute(x, 'tensor', [(i, i ^ mask) for i in range(shards)])]
    ppermute x24 -> x23, waiting for transfers between devices: 15 us -> 29.2 us  [swap(): return lax.ppermute(x, 'tensor', [(i, i ^ mask) for i in range(shards)])]
  transfers between devices with their start and end apart: 25 -> 24, of which waited for: 8 -> 10; matrix products, arithmetic and copies ran while one was open for 1% -> 1% of each run, Pallas kernels for 23% -> 8%
where the time goes in v3:
time: 127 us
  waiting for transfers between devices  44.6 us (35%)
  starting transfers between devices  32.2 us (25%)
  Pallas kernels  23.9 us (19%)
  blocking collectives  23 us (18%)
  other arithmetic  2.99 us (2%)
    ppermute x23, waiting for transfers between devices, swap(): return lax.ppermute(x, 'tensor', [(i, i ^ mask) for i in range(shards)])  29.2 us
    ppermute x23, starting transfers between devices, swap(): return lax.ppermute(x, 'tensor', [(i, i ^ mask) for i in range(shards)])  27.7 us
    all_to_all x1, blocking collectives, local(): lax.all_to_all(hidden.reshape(shards, rows, local_ff), 'tensor', 0, 0)  23 us
    pallas_call x2, Pallas kernels, project(): pl.pallas_call(functools.partial(project_body, full), grid_spec=pltpu.Pre...  16.3 us
    all_to_all x1, waiting for transfers between devices, local(): rot = lax.all_to_all(turned, 'tensor', 0, 0)  15.4 us
    pallas_call x1, Pallas kernels, rotate(): pl.pallas_call(rotate_body, in_specs=[pl.BlockSpec(memory_space=pltpu.VME...  5.34 us
    all_to_all x1, starting transfers between devices, local(): rot = lax.all_to_all(turned, 'tensor', 0, 0)  4.44 us
  transfers between devices with their start and end apart: 24, of which 10 were waited for; matrix products, arithmetic and copies ran while one was open for 1% of the time, Pallas kernels for 8%

profile of v3, /device:TPU:1, one launch (start us, length us, event | category | flops | bytes accessed | tf_op | source)
XLA Modules:
  0.0 126.7 jit_solution(15485035356069472185)
XLA Ops:
  0.0 1.9 %fusion.4 = bf16[256,1664]{1,0:T(8,128)(2,1)S(1)} fusion(bf16[256,1664]{1,0:T(8,128)(2,1)} %param.7, bf16[256,1664]{1,0:T(8,128)(2,1)} %param.6), kind=kLoop, calls=%fused_computation.6 | loop fusion | flops 3407872 | bytes 2555904 | tf_op jit(solution)/shard_map/convert_element_type | solution.py:225
  1.9 23.0 %all_to_all.10.hidden_ref = bf16[16,16,1664]{2,1,0:T(8,128)(2,1)S(1)} all-to-all(bf16[16,16,1664]{2,1,0:T(8,128)(2,1)S(1)} %bitcast.18), channel_id=1, replica_groups=mesh['dp'=8,'tensor'=16] {'tensor'}, dimensions={0} | all-to-all | bytes 1703936 | tf_op jit(solution)/shard_map/all_to_all | solution.py:226
  24.9 5.3 %rotate.1 = bf16[16,16,1664]{2,1,0:T(8,128)(2,1)} custom-call(bf16[16,16,1664]{2,1,0:T(8,128)(2,1)S(1)} %all_to_all.10.hidden_ref, bf16[4,1664,512]{2,1,0:T(8,128)(2,1)} %constant.9.clone.table_ref), custom_call_target="tpu_custom_call" | custom-call | flops 1417674752 | bytes 7241728 | tf_op jit(solution)/shard_map/rotate/pallas_call | solution.py:84
  30.3 4.4 %all-to-all-start.1 = ((bf16[16,16,1664]{2,1,0:T(8,128)(2,1)}), bf16[16,16,1664]{2,1,0:T(8,128)(2,1)S(1)}, u32[]{:S(2)}, u32[]{:S(2)}) async-start(bf16[16,16,1664]{2,1,0:T(8,128)(2,1)} %rotate.1), calls=%async_computation.1 | async-start | bytes 1703936 | tf_op jit(solution)/shard_map/all_to_all | solution.py:228
  34.7 15.4 %all-to-all-done.1.rot_ref = bf16[16,16,1664]{2,1,0:T(8,128)(2,1)S(1)} async-done(((bf16[16,16,1664]{2,1,0:T(8,128)(2,1)}), bf16[16,16,1664]{2,1,0:T(8,128)(2,1)S(1)}, u32[]{:S(2)}, u32[]{:S(2)}) %all-to-all-start.1) | async-done | bytes 852000 | tf_op jit(solution)/shard_map/all_to_all | solution.py:228
  50.1 6.5 %project.3 = (bf16[8,16,3072]{2,1,0:T(8,128)(2,1)S(1)}, bf16[8,16,3072]{2,1,0:T(8,128)(2,1)S(1)}) custom-call(s32[1]{0:T(128)} %bitcast.place_ref, bf16[16,16,1664]{2,1,0:T(8,128)(2,1)S(1)} %all-to-all-done.1.rot_ref, s32[208,8192]{1,0:T(8,128)} %low_ref.3, s32[208,8192]{1,0:T(8,128)} %high_ref.3, bf16[13,8192]{1,0:T(8,128)(2,1)} %scale_ref.3), custom_call_target="tpu_custom_call" | custom-call | flops 2617245696 | bytes 8257536 | tf_op jit(solution)/shard_map/project/pallas_call | solution.py:145
  57.3 1.9 %collective-permute-done.8 = bf16[8,16,3072]{2,1,0:T(8,128)(2,1)S(1)} collective-permute-done((bf16[8,16,3072]{2,1,0:T(8,128)(2,1)S(1)}, bf16[8,16,3072]{2,1,0:T(8,128)(2,1)S(1)}, u32[]{:S(2)}, u32[]{:S(2)}) %collective-permute-start.8) | collective-permute-done | bytes 786464 | tf_op jit(solution)/shard_map/ppermute | solution.py:218
  59.7 9.8 %project.2 = (bf16[8,16,5120]{2,1,0:T(8,128)(2,1)S(1)}, bf16[8,16,5120]{2,1,0:T(8,128)(2,1)S(1)}) custom-call(s32[1]{0:T(128)} %bitcast.place_ref, bf16[16,16,1664]{2,1,0:T(8,128)(2,1)S(1)} %all-to-all-done.1.rot_ref, s32[208,8192]{1,0:T(8,128)} %low_ref.3, s32[208,8192]{1,0:T(8,128)} %high_ref.3, bf16[13,8192]{1,0:T(8,128)(2,1)} %scale_ref.3), custom_call_target="tpu_custom_call" | custom-call | flops 4362076160 | bytes 13762560 | tf_op jit(solution)/shard_map/project/pallas_call | solution.py:145
  72.8 1.3 %collective-permute-start.11 = (bf16[16,3072]{1,0:T(8,128)(2,1)S(1)}, bf16[16,3072]{1,0:T(8,128)(2,1)S(1)}, u32[]{:S(2)}, u32[]{:S(2)}) collective-permute-start(bf16[16,3072]{1,0:T(8,128)(2,1)S(1)} %get-tuple-element.20), channel_id=1, source_target_pairs={{0,2},{1,3},{2,0},{3,1},{4,6},{5,7},{6,4},{7,5},{8,10},{9,11},{10,... | collective-permute-start | bytes 294920 | tf_op jit(solution)/shard_map/ppermute | solution.py:218
  74.4 1.8 %collective-permute-start.1 = (bf16[2,16,5120]{2,1,0:T(8,128)(2,1)S(1)}, bf16[2,16,5120]{2,1,0:T(8,128)(2,1)S(1)}, u32[]{:S(2)}, u32[]{:S(2)}) collective-permute-start(bf16[2,16,5120]{2,1,0:T(8,128)(2,1)S(1)} %get-tuple-element.15), channel_id=1, source_target_pairs={{0,4},{1,5},{2,6},{3,7},{4,0},{5,1},{6,2},{7,3},{8,12},{9,13},{10,... | collective-permute-start | bytes 983048 | tf_op jit(solution)/shard_map/ppermute | solution.py:218
  77.2 1.7 %collective-permute-done.12 = bf16[16,3072]{1,0:T(8,128)(2,1)S(1)} collective-permute-done((bf16[16,3072]{1,0:T(8,128)(2,1)S(1)}, bf16[16,3072]{1,0:T(8,128)(2,1)S(1)}, u32[]{:S(2)}, u32[]{:S(2)}) %collective-permute-start.12) | collective-permute-done | bytes 98336 | tf_op jit(solution)/shard_map/ppermute | solution.py:218
  80.4 5.6 %collective-permute-done.1 = bf16[2,16,5120]{2,1,0:T(8,128)(2,1)S(1)} collective-permute-done((bf16[2,16,5120]{2,1,0:T(8,128)(2,1)S(1)}, bf16[2,16,5120]{2,1,0:T(8,128)(2,1)S(1)}, u32[]{:S(2)}, u32[]{:S(2)}) %collective-permute-start.1) | collective-permute-done | bytes 327712 | tf_op jit(solution)/shard_map/ppermute | solution.py:218
  86.0 8.1 %collective-permute-done.3 = bf16[2,16,5120]{2,1,0:T(8,128)(2,1)S(1)} collective-permute-done((bf16[2,16,5120]{2,1,0:T(8,128)(2,1)S(1)}, bf16[2,16,5120]{2,1,0:T(8,128)(2,1)S(1)}, u32[]{:S(2)}, u32[]{:S(2)}) %collective-permute-start.3) | collective-permute-done | bytes 327712 | tf_op jit(solution)/shard_map/ppermute | solution.py:218
  94.3 1.1 collective-permute-start.4
  95.4 2.4 %collective-permute-done.15 = bf16[16,3072]{1,0:T(8,128)(2,1)S(1)} collective-permute-done((bf16[16,3072]{1,0:T(8,128)(2,1)S(1)}, bf16[16,3072]{1,0:T(8,128)(2,1)S(1)}, u32[]{:S(2)}, u32[]{:S(2)}) %collective-permute-start.15) | collective-permute-done | bytes 98336 | tf_op jit(solution)/shard_map/ppermute | solution.py:218
  98.7 1.5 %collective-permute-start.16 = (bf16[4,16,3072]{2,1,0:T(8,128)(2,1)S(1)}, bf16[4,16,3072]{2,1,0:T(8,128)(2,1)S(1)}, u32[]{:S(2)}, u32[]{:S(2)}) collective-permute-start(bf16[4,16,3072]{2,1,0:T(8,128)(2,1)S(1)} %pad_maximum_fusion.refs_4_), channel_id=1, source_target_pairs={{0,8},{1,9},{2,10},{3,11},{4,12},{5,13},{6,14},{7,15},{8,0},{9,1},... | collective-permute-start | bytes 1179656 | tf_op jit(solution)/shard_map/ppermute | solution.py:218
  100.2 3.1 %collective-permute-done.4 = bf16[2,16,5120]{2,1,0:T(8,128)(2,1)S(1)} collective-permute-done((bf16[2,16,5120]{2,1,0:T(8,128)(2,1)S(1)}, bf16[2,16,5120]{2,1,0:T(8,128)(2,1)S(1)}, u32[]{:S(2)}, u32[]{:S(2)}) %collective-permute-start.4) | collective-permute-done | bytes 327712 | tf_op jit(solution)/shard_map/ppermute | solution.py:218
  104.0 3.4 %collective-permute-start.5 = (bf16[2,16,5120]{2,1,0:T(8,128)(2,1)S(1)}, bf16[2,16,5120]{2,1,0:T(8,128)(2,1)S(1)}, u32[]{:S(2)}, u32[]{:S(2)}) collective-permute-start(bf16[2,16,5120]{2,1,0:T(8,128)(2,1)S(1)} %add_convert_fusion.1.refs_0_), channel_id=1, source_target_pairs={{0,4},{1,5},{2,6},{3,7},{4,0},{5,1},{6,2},{7,3},{8,12},{9,13},{10,... | collective-permute-start | bytes 983048 | tf_op jit(solution)/shard_map/ppermute | solution.py:218
  107.5 4.2 %collective-permute-done.16.refs_5_ = bf16[4,16,3072]{2,1,0:T(8,128)(2,1)S(1)} collective-permute-done((bf16[4,16,3072]{2,1,0:T(8,128)(2,1)S(1)}, bf16[4,16,3072]{2,1,0:T(8,128)(2,1)S(1)}, u32[]{:S(2)}, u32[]{:S(2)}) %collective-permute-start.16) | collective-permute-done | bytes 393248 | tf_op jit(solution)/shard_map/ppermute | solution.py:218
  111.7 2.7 %collective-permute-start.22 = (bf16[4,16,3072]{2,1,0:T(8,128)(2,1)S(1)}, bf16[4,16,3072]{2,1,0:T(8,128)(2,1)S(1)}, u32[]{:S(2)}, u32[]{:S(2)}) collective-permute-start(bf16[4,16,3072]{2,1,0:T(8,128)(2,1)S(1)} %collective-permute-done.16.refs_5_), channel_id=1, source_target_pairs={{0,1},{1,0},{2,3},{3,2},{4,5},{5,4},{6,7},{7,6},{8,9},{9,8},{10,11... | collective-permute-start | bytes 1179656 | tf_op jit(solution)/shard_map/ppermute | solution.py:218
  114.4 5.2 %collective-permute-start.20 = (bf16[2,16,5120]{2,1,0:T(8,128)(2,1)S(1)}, bf16[2,16,5120]{2,1,0:T(8,128)(2,1)S(1)}, u32[]{:S(2)}, u32[]{:S(2)}) collective-permute-start(bf16[2,16,5120]{2,1,0:T(8,128)(2,1)S(1)} %collective-permute-done.7.refs_3_), channel_id=1, source_target_pairs={{0,1},{1,0},{2,3},{3,2},{4,5},{5,4},{6,7},{7,6},{8,9},{9,8},{10,11... | collective-permute-start | bytes 983048 | tf_op jit(solution)/shard_map/ppermute | solution.py:218
  119.7 3.5 %collective-permute-start.18 = (bf16[2,16,5120]{2,1,0:T(8,128)(2,1)S(1)}, bf16[2,16,5120]{2,1,0:T(8,128)(2,1)S(1)}, u32[]{:S(2)}, u32[]{:S(2)}) collective-permute-start(bf16[2,16,5120]{2,1,0:T(8,128)(2,1)S(1)} %collective-permute-done.5.refs_1_), channel_id=1, source_target_pairs={{0,1},{1,0},{2,3},{3,2},{4,5},{5,4},{6,7},{7,6},{8,9},{9,8},{10,11... | collective-permute-start | bytes 983048 | tf_op jit(solution)/shard_map/ppermute | solution.py:218
  123.2 1.2 collective-permute-done.18.refs_7_
  124.4 2.3 %put.1 = bf16[256,8192]{1,0:T(8,128)(2,1)} custom-call(s32[1]{0:T(128)} %bitcast.place_ref, bf16[2,16,5120]{2,1,0:T(8,128)(2,1)S(1)} %add_convert_fusion.1.refs_0_, bf16[2,16,5120]{2,1,0:T(8,128)(2,1)S(1)} %collective-permute-done.5.refs_1_, bf16[2,16,5120]{2,1,0:T(8,128)(2,1)S(1)} %collective-permute-done.6.refs_2_, ...), custom_call_target="tpu_custom_call" | custom-call | bytes 8388608 | tf_op jit(solution)/shard_map/put/pallas_call | solution.py:194
  (38 shorter events, 9.3 us)
Async XLA Ops:
  30.3 19.8 %all-to-all-start.1 = ((bf16[16,16,1664]{2,1,0:T(8,128)(2,1)}), bf16[16,16,1664]{2,1,0:T(8,128)(2,1)S(1)}, u32[]{:S(2)}, u32[]{:S(2)}) async-start(bf16[16,16,1664]{2,1,0:T(8,128)(2,1)} %rotate.1), calls=%async_computation.1 | async-start | bytes 1703936 | tf_op jit(solution)/shard_map/all_to_all | solution.py:228
  56.5 2.7 %collective-permute-start.8 = (bf16[8,16,3072]{2,1,0:T(8,128)(2,1)S(1)}, bf16[8,16,3072]{2,1,0:T(8,128)(2,1)S(1)}, u32[]{:S(2)}, u32[]{:S(2)}) collective-permute-start(bf16[8,16,3072]{2,1,0:T(8,128)(2,1)S(1)} %get-tuple-element.12), channel_id=1, source_target_pairs={{0,1},{1,0},{2,3},{3,2},{4,5},{5,4},{6,7},{7,6},{8,9},{9,8},{10,11... | collective-permute-start | bytes 2359304 | tf_op jit(solution)/shard_map/ppermute | solution.py:218
  59.3 11.9 %collective-permute-start.9 = (bf16[4,16,3072]{2,1,0:T(8,128)(2,1)S(1)}, bf16[4,16,3072]{2,1,0:T(8,128)(2,1)S(1)}, u32[]{:S(2)}, u32[]{:S(2)}) collective-permute-start(bf16[4,16,3072]{2,1,0:T(8,128)(2,1)S(1)} %add_convert_fusion), channel_id=1, source_target_pairs={{0,8},{1,9},{2,10},{3,11},{4,12},{5,13},{6,14},{7,15},{8,0},{9,1},... | collective-permute-start | bytes 1179656 | tf_op jit(solution)/shard_map/ppermute | solution.py:218
  69.4 4.7 %collective-permute-start = (bf16[8,16,5120]{2,1,0:T(8,128)(2,1)S(1)}, bf16[8,16,5120]{2,1,0:T(8,128)(2,1)S(1)}, u32[]{:S(2)}, u32[]{:S(2)}) collective-permute-start(bf16[8,16,5120]{2,1,0:T(8,128)(2,1)S(1)} %get-tuple-element.10), channel_id=1, source_target_pairs={{0,1},{1,0},{2,3},{3,2},{4,5},{5,4},{6,7},{7,6},{8,9},{9,8},{10,11... | collective-permute-start | bytes 3932168 | tf_op jit(solution)/shard_map/ppermute | solution.py:218
  71.4 5.6 %collective-permute-start.10 = (bf16[16,3072]{1,0:T(8,128)(2,1)S(1)}, bf16[16,3072]{1,0:T(8,128)(2,1)S(1)}, u32[]{:S(2)}, u32[]{:S(2)}) collective-permute-start(bf16[16,3072]{1,0:T(8,128)(2,1)S(1)} %get-tuple-element.18), channel_id=1, source_target_pairs={{0,4},{1,5},{2,6},{3,7},{4,0},{5,1},{6,2},{7,3},{8,12},{9,13},{10,... | collective-permute-start | bytes 294920 | tf_op jit(solution)/shard_map/ppermute | solution.py:218
  72.0 6.8 %collective-permute-start.12 = (bf16[16,3072]{1,0:T(8,128)(2,1)S(1)}, bf16[16,3072]{1,0:T(8,128)(2,1)S(1)}, u32[]{:S(2)}, u32[]{:S(2)}) collective-permute-start(bf16[16,3072]{1,0:T(8,128)(2,1)S(1)} %get-tuple-element.19), channel_id=1, source_target_pairs={{0,6},{1,7},{2,4},{3,5},{4,2},{5,3},{6,0},{7,1},{8,14},{9,15},{10,... | collective-permute-start | bytes 294920 | tf_op jit(solution)/shard_map/ppermute | solution.py:218
  72.8 6.0 %collective-permute-start.11 = (bf16[16,3072]{1,0:T(8,128)(2,1)S(1)}, bf16[16,3072]{1,0:T(8,128)(2,1)S(1)}, u32[]{:S(2)}, u32[]{:S(2)}) collective-permute-start(bf16[16,3072]{1,0:T(8,128)(2,1)S(1)} %get-tuple-element.20), channel_id=1, source_target_pairs={{0,2},{1,3},{2,0},{3,1},{4,6},{5,7},{6,4},{7,5},{8,10},{9,11},{10,... | collective-permute-start | bytes 294920 | tf_op jit(solution)/shard_map/ppermute | solution.py:218
  74.4 11.6 %collective-permute-start.1 = (bf16[2,16,5120]{2,1,0:T(8,128)(2,1)S(1)}, bf16[2,16,5120]{2,1,0:T(8,128)(2,1)S(1)}, u32[]{:S(2)}, u32[]{:S(2)}) collective-permute-start(bf16[2,16,5120]{2,1,0:T(8,128)(2,1)S(1)} %get-tuple-element.15), channel_id=1, source_target_pairs={{0,4},{1,5},{2,6},{3,7},{4,0},{5,1},{6,2},{7,3},{8,12},{9,13},{10,... | collective-permute-start | bytes 983048 | tf_op jit(solution)/shard_map/ppermute | solution.py:218
  76.2 17.9 %collective-permute-start.3 = (bf16[2,16,5120]{2,1,0:T(8,128)(2,1)S(1)}, bf16[2,16,5120]{2,1,0:T(8,128)(2,1)S(1)}, u32[]{:S(2)}, u32[]{:S(2)}) collective-permute-start(bf16[2,16,5120]{2,1,0:T(8,128)(2,1)S(1)} %get-tuple-element.16), channel_id=1, source_target_pairs={{0,6},{1,7},{2,4},{3,5},{4,2},{5,3},{6,0},{7,1},{8,14},{9,15},{10,... | collective-permute-start | bytes 983048 | tf_op jit(solution)/shard_map/ppermute | solution.py:218
  77.0 17.1 %collective-permute-start.2 = (bf16[2,16,5120]{2,1,0:T(8,128)(2,1)S(1)}, bf16[2,16,5120]{2,1,0:T(8,128)(2,1)S(1)}, u32[]{:S(2)}, u32[]{:S(2)}) collective-permute-start(bf16[2,16,5120]{2,1,0:T(8,128)(2,1)S(1)} %get-tuple-element.17), channel_id=1, source_target_pairs={{0,2},{1,3},{2,0},{3,1},{4,6},{5,7},{6,4},{7,5},{8,10},{9,11},{10,... | collective-permute-start | bytes 983048 | tf_op jit(solution)/shard_map/ppermute | solution.py:218
  78.9 18.9 %collective-permute-start.15 = (bf16[16,3072]{1,0:T(8,128)(2,1)S(1)}, bf16[16,3072]{1,0:T(8,128)(2,1)S(1)}, u32[]{:S(2)}, u32[]{:S(2)}) collective-permute-start(bf16[16,3072]{1,0:T(8,128)(2,1)S(1)} %fusion.6), channel_id=1, source_target_pairs={{0,6},{1,7},{2,4},{3,5},{4,2},{5,3},{6,0},{7,1},{8,14},{9,15},{10,... | collective-permute-start | bytes 294920 | tf_op jit(solution)/shard_map/ppermute | solution.py:218
  79.7 18.0 %collective-permute-start.14 = (bf16[16,3072]{1,0:T(8,128)(2,1)S(1)}, bf16[16,3072]{1,0:T(8,128)(2,1)S(1)}, u32[]{:S(2)}, u32[]{:S(2)}) collective-permute-start(bf16[16,3072]{1,0:T(8,128)(2,1)S(1)} %fusion.6), channel_id=1, source_target_pairs={{0,4},{1,5},{2,6},{3,7},{4,0},{5,1},{6,2},{7,3},{8,12},{9,13},{10,... | collective-permute-start | bytes 294920 | tf_op jit(solution)/shard_map/ppermute | solution.py:218
  86.0 11.8 %collective-permute-start.13 = (bf16[16,3072]{1,0:T(8,128)(2,1)S(1)}, bf16[16,3072]{1,0:T(8,128)(2,1)S(1)}, u32[]{:S(2)}, u32[]{:S(2)}) collective-permute-start(bf16[16,3072]{1,0:T(8,128)(2,1)S(1)} %fusion.6), channel_id=1, source_target_pairs={{0,2},{1,3},{2,0},{3,1},{4,6},{5,7},{6,4},{7,5},{8,10},{9,11},{10,... | collective-permute-start | bytes 294920 | tf_op jit(solution)/shard_map/ppermute | solution.py:218
  94.3 9.0 %collective-permute-start.4 = (bf16[2,16,5120]{2,1,0:T(8,128)(2,1)S(1)}, bf16[2,16,5120]{2,1,0:T(8,128)(2,1)S(1)}, u32[]{:S(2)}, u32[]{:S(2)}) collective-permute-start(bf16[2,16,5120]{2,1,0:T(8,128)(2,1)S(1)} %fusion.7), channel_id=1, source_target_pairs={{0,8},{1,9},{2,10},{3,11},{4,12},{5,13},{6,14},{7,15},{8,0},{9,1},... | collective-permute-start | bytes 983048 | tf_op jit(solution)/shard_map/ppermute | solution.py:218
  97.8 16.6 %collective-permute-start.21 = (bf16[4,16,3072]{2,1,0:T(8,128)(2,1)S(1)}, bf16[4,16,3072]{2,1,0:T(8,128)(2,1)S(1)}, u32[]{:S(2)}, u32[]{:S(2)}) collective-permute-start(bf16[4,16,3072]{2,1,0:T(8,128)(2,1)S(1)} %pad_maximum_fusion.refs_4_), channel_id=1, source_target_pairs={{0,1},{1,0},{2,3},{3,2},{4,5},{5,4},{6,7},{7,6},{8,9},{9,8},{10,11... | collective-permute-start | bytes 1179656 | tf_op jit(solution)/shard_map/ppermute | solution.py:218
  98.7 13.0 %collective-permute-start.16 = (bf16[4,16,3072]{2,1,0:T(8,128)(2,1)S(1)}, bf16[4,16,3072]{2,1,0:T(8,128)(2,1)S(1)}, u32[]{:S(2)}, u32[]{:S(2)}) collective-permute-start(bf16[4,16,3072]{2,1,0:T(8,128)(2,1)S(1)} %pad_maximum_fusion.refs_4_), channel_id=1, source_target_pairs={{0,8},{1,9},{2,10},{3,11},{4,12},{5,13},{6,14},{7,15},{8,0},{9,1},... | collective-permute-start | bytes 1179656 | tf_op jit(solution)/shard_map/ppermute | solution.py:218
  103.5 10.9 %collective-permute-start.7 = (bf16[2,16,5120]{2,1,0:T(8,128)(2,1)S(1)}, bf16[2,16,5120]{2,1,0:T(8,128)(2,1)S(1)}, u32[]{:S(2)}, u32[]{:S(2)}) collective-permute-start(bf16[2,16,5120]{2,1,0:T(8,128)(2,1)S(1)} %add_convert_fusion.1.refs_0_), channel_id=1, source_target_pairs={{0,6},{1,7},{2,4},{3,5},{4,2},{5,3},{6,0},{7,1},{8,14},{9,15},{10,... | collective-permute-start | bytes 983048 | tf_op jit(solution)/shard_map/ppermute | solution.py:218
  104.0 15.6 %collective-permute-start.6 = (bf16[2,16,5120]{2,1,0:T(8,128)(2,1)S(1)}, bf16[2,16,5120]{2,1,0:T(8,128)(2,1)S(1)}, u32[]{:S(2)}, u32[]{:S(2)}) collective-permute-start(bf16[2,16,5120]{2,1,0:T(8,128)(2,1)S(1)} %add_convert_fusion.1.refs_0_), channel_id=1, source_target_pairs={{0,2},{1,3},{2,0},{3,1},{4,6},{5,7},{6,4},{7,5},{8,10},{9,11},{10,... | collective-permute-start | bytes 983048 | tf_op jit(solution)/shard_map/ppermute | solution.py:218
  104.0 15.6 %collective-permute-start.5 = (bf16[2,16,5120]{2,1,0:T(8,128)(2,1)S(1)}, bf16[2,16,5120]{2,1,0:T(8,128)(2,1)S(1)}, u32[]{:S(2)}, u32[]{:S(2)}) collective-permute-start(bf16[2,16,5120]{2,1,0:T(8,128)(2,1)S(1)} %add_convert_fusion.1.refs_0_), channel_id=1, source_target_pairs={{0,4},{1,5},{2,6},{3,7},{4,0},{5,1},{6,2},{7,3},{8,12},{9,13},{10,... | collective-permute-start | bytes 983048 | tf_op jit(solution)/shard_map/ppermute | solution.py:218
  111.7 11.5 %collective-permute-start.22 = (bf16[4,16,3072]{2,1,0:T(8,128)(2,1)S(1)}, bf16[4,16,3072]{2,1,0:T(8,128)(2,1)S(1)}, u32[]{:S(2)}, u32[]{:S(2)}) collective-permute-start(bf16[4,16,3072]{2,1,0:T(8,128)(2,1)S(1)} %collective-permute-done.16.refs_5_), channel_id=1, source_target_pairs={{0,1},{1,0},{2,3},{3,2},{4,5},{5,4},{6,7},{7,6},{8,9},{9,8},{10,11... | collective-permute-start | bytes 1179656 | tf_op jit(solution)/shard_map/ppermute | solution.py:218
  114.4 8.8 %collective-permute-start.17 = (bf16[2,16,5120]{2,1,0:T(8,128)(2,1)S(1)}, bf16[2,16,5120]{2,1,0:T(8,128)(2,1)S(1)}, u32[]{:S(2)}, u32[]{:S(2)}) collective-permute-start(bf16[2,16,5120]{2,1,0:T(8,128)(2,1)S(1)} %add_convert_fusion.1.refs_0_), channel_id=1, source_target_pairs={{0,1},{1,0},{2,3},{3,2},{4,5},{5,4},{6,7},{7,6},{8,9},{9,8},{10,11... | collective-permute-start | bytes 983048 | tf_op jit(solution)/shard_map/ppermute | solution.py:218
  114.4 8.7 %collective-permute-start.20 = (bf16[2,16,5120]{2,1,0:T(8,128)(2,1)S(1)}, bf16[2,16,5120]{2,1,0:T(8,128)(2,1)S(1)}, u32[]{:S(2)}, u32[]{:S(2)}) collective-permute-start(bf16[2,16,5120]{2,1,0:T(8,128)(2,1)S(1)} %collective-permute-done.7.refs_3_), channel_id=1, source_target_pairs={{0,1},{1,0},{2,3},{3,2},{4,5},{5,4},{6,7},{7,6},{8,9},{9,8},{10,11... | collective-permute-start | bytes 983048 | tf_op jit(solution)/shard_map/ppermute | solution.py:218
  119.7 3.5 %collective-permute-start.19 = (bf16[2,16,5120]{2,1,0:T(8,128)(2,1)S(1)}, bf16[2,16,5120]{2,1,0:T(8,128)(2,1)S(1)}, u32[]{:S(2)}, u32[]{:S(2)}) collective-permute-start(bf16[2,16,5120]{2,1,0:T(8,128)(2,1)S(1)} %collective-permute-done.6.refs_2_), channel_id=1, source_target_pairs={{0,1},{1,0},{2,3},{3,2},{4,5},{5,4},{6,7},{7,6},{8,9},{9,8},{10,11... | collective-permute-start | bytes 983048 | tf_op jit(solution)/shard_map/ppermute | solution.py:218
  119.7 4.8 %collective-permute-start.18 = (bf16[2,16,5120]{2,1,0:T(8,128)(2,1)S(1)}, bf16[2,16,5120]{2,1,0:T(8,128)(2,1)S(1)}, u32[]{:S(2)}, u32[]{:S(2)}) collective-permute-start(bf16[2,16,5120]{2,1,0:T(8,128)(2,1)S(1)} %collective-permute-done.5.refs_1_), channel_id=1, source_target_pairs={{0,1},{1,0},{2,3},{3,2},{4,5},{5,4},{6,7},{7,6},{8,9},{9,8},{10,11... | collective-permute-start | bytes 983048 | tf_op jit(solution)/shard_map/ppermute | solution.py:218

commit v4 on v3

--- a/solution.py
+++ b/solution.py
@@ -190,19 +190,22 @@
         copy.wait()
 
 
-def put(place, pieces, names, firsts, shape):
+def put(place, pieces, names, firsts, shape, into=None, weight=0):
+    extra = () if into is None else (into,)
     return pl.pallas_call(
         functools.partial(put_body, names, firsts),
-        in_specs=[pl.BlockSpec(memory_space=pltpu.SMEM)] + [pl.BlockSpec(memory_space=pl.ANY)] * len(pieces),
+        in_specs=[pl.BlockSpec(memory_space=pltpu.SMEM)]
+        + [pl.BlockSpec(memory_space=pl.ANY)] * (len(pieces) + len(extra)),
         out_specs=pl.BlockSpec(memory_space=pl.ANY),
         out_shape=jax.ShapeDtypeStruct(shape, jnp.bfloat16),
         scratch_shapes=[pltpu.SemaphoreType.DMA((sum(map(len, names)),))],
+        input_output_aliases={} if into is None else {1 + len(pieces): 0},
         compiler_params=pltpu.CompilerParams(vmem_limit_bytes=VMEM_LIMIT),
         cost_estimate=pl.CostEstimate(
-            flops=0, bytes_accessed=4 * sum(p.size for p in pieces), transcendentals=0
+            flops=weight, bytes_accessed=4 * sum(p.size for p in pieces), transcendentals=0
         ),
         name="put",
-    )(place, *pieces)
+    )(place, *pieces, *extra)
 
 
 def local(gate_input, up_input, down_low, down_high, down_scales):
@@ -210,7 +213,7 @@
     total_rows, local_ff = gate_input.shape
     rows = total_rows // shards
     width = down_low.shape[1]
-    left = width // 8 * 5
+    left = width // 8 * 4
     place = lax.axis_index("tensor").astype(jnp.int32).reshape(1)
     f32, bf16 = jnp.float32, jnp.bfloat16
 
@@ -241,9 +244,11 @@
         at = slice(4 * y, 4 * y + 4)
         return keep_q[at].astype(f32) + got_q[at].astype(f32)
 
-    along_x = [swap(chip_p(k).astype(bf16), X[k]) for k in (2, 1, 3)]
+    sends_p = [chip_p(k).astype(bf16) for k in (2, 1, 3)]
+    along_x = [swap(t, X[k]) for t, k in zip(sends_p, (2, 1, 3))]
     along_y = swap(chip_q(1).astype(bf16), Y)
     sum_p = chip_p(0) + sum(t.astype(f32) for t in along_x)
+    along_y, *_ = lax.optimization_barrier((along_y, *sends_p))
     sum_q = chip_q(0) + along_y.astype(f32)
 
     mine_p = lax.reduce_precision(sum_p, 8, 7)
@@ -253,16 +258,25 @@
     done_q = (sum_q[0] + sum(t.astype(f32) for t in last_q)).astype(bf16)
 
     all_p = [done_p] + [swap(done_p, X[k]) for k in (2, 1, 3)]
-    row_q = jnp.stack([done_q] + [swap(done_q, X[k]) for k in (1, 2, 3)])
+    row_q = [done_q] + [swap(done_q, X[k]) for k in (1, 2, 3)]
+    *row_q, _ = lax.optimization_barrier((*row_q, done_p))
+    row_q = jnp.stack(row_q)
     all_q = [row_q, swap(row_q, Y)]
     names_p = [tuple(X[k] | y for y in (0, Y)) for k in (0, 2, 1, 3)]
     names_q = [tuple(x | y for x in X) for y in (0, Y)]
-    near = all_p + all_q
-    names = names_p + names_q
-    far = [swap(t, CORE) for t in near]
-    names += [tuple(q | CORE for q in blocks) for blocks in names]
-    firsts = [0] * len(all_p) + [left] * len(all_q)
-    return put(place, near + far, names, firsts * 2, (total_rows, width))
+    far_p = [swap(t, CORE) for t in all_p]
+    far_q = [swap(t, CORE) for t in all_q]
+
+    def across(names):
+        return [tuple(q | CORE for q in blocks) for blocks in names]
+
+    def lay(into, pieces, names, first, weight):
+        return put(place, pieces, names, [first] * len(pieces), (total_rows, width), into, weight)
+
+    out = lay(None, all_p[:1], names_p[:1], 0, 20000000000)
+    out = lay(out, all_q + far_q, names_q + across(names_q), left, 0)
+    out = lay(out, all_p[1:] + far_p[:1], names_p[1:] + across(names_p[:1]), 0, 20000000000)
+    return lay(out, far_p[1:], across(names_p[1:]), 0, 0)
 
 
 def solution(mesh):

time: 127 us -> 122 us (0.961)
  waiting for transfers between devices: 44.6 us -> 37.2 us
  Pallas kernels: 23.9 us -> 25.7 us
    ppermute x23, waiting for transfers between devices: 29.2 us -> 21.9 us  [swap(): return lax.ppermute(x, 'tensor', [(i, i ^ mask) for i in range(shards)])]
    pallas_call x1 -> x4, Pallas kernels: 2.27 us -> 4.11 us  [put(): pl.pallas_call(functools.partial(put_body, names, firsts), in_specs=[pl.B...]
  transfers between devices with their start and end apart: 24 -> 24, of which waited for: 10 -> 10; matrix products, arithmetic and copies ran while one was open for 1% -> 1% of each run, Pallas kernels for 8% -> 9%
where the time goes in v4:
time: 122 us; the launch traced here: 121 us
  waiting for transfers between devices  37.2 us (30%)
  starting transfers between devices  32.2 us (26%)
  Pallas kernels  25.7 us (21%)
  blocking collectives  23 us (19%)
  other arithmetic  2.96 us (2%)
    ppermute x23, starting transfers between devices, swap(): return lax.ppermute(x, 'tensor', [(i, i ^ mask) for i in range(shards)])  27.8 us
    all_to_all x1, blocking collectives, local(): lax.all_to_all(hidden.reshape(shards, rows, local_ff), 'tensor', 0, 0)  23 us
    ppermute x23, waiting for transfers between devices, swap(): return lax.ppermute(x, 'tensor', [(i, i ^ mask) for i in range(shards)])  21.9 us
    pallas_call x2, Pallas kernels, project(): pl.pallas_call(functools.partial(project_body, full), grid_spec=pltpu.Pre...  16.3 us
    all_to_all x1, waiting for transfers between devices, local(): rot = lax.all_to_all(turned, 'tensor', 0, 0)  15.4 us
    pallas_call x1, Pallas kernels, rotate(): pl.pallas_call(rotate_body, in_specs=[pl.BlockSpec(memory_space=pltpu.VME...  5.34 us
    all_to_all x1, starting transfers between devices, local(): rot = lax.all_to_all(turned, 'tensor', 0, 0)  4.44 us
    pallas_call x4, Pallas kernels, put(): pl.pallas_call(functools.partial(put_body, names, firsts), in_specs=[pl.B...  4.11 us
  transfers between devices with their start and end apart: 24, of which 10 were waited for; matrix products, arithmetic and copies ran while one was open for 1% of the time, Pallas kernels for 9%

profile of v4, /device:TPU:1, one launch (start us, length us, event | category | flops | bytes accessed | tf_op | source)
XLA Modules:
  0.0 121.3 jit_solution(14535955363816435203)
XLA Ops:
  0.0 1.9 %fusion.4 = bf16[256,1664]{1,0:T(8,128)(2,1)S(1)} fusion(bf16[256,1664]{1,0:T(8,128)(2,1)} %param.7, bf16[256,1664]{1,0:T(8,128)(2,1)} %param.6), kind=kLoop, calls=%fused_computation.6 | loop fusion | flops 3407872 | bytes 2555904 | tf_op jit(solution)/shard_map/convert_element_type | solution.py:228
  1.9 23.0 %all_to_all.10.hidden_ref = bf16[16,16,1664]{2,1,0:T(8,128)(2,1)S(1)} all-to-all(bf16[16,16,1664]{2,1,0:T(8,128)(2,1)S(1)} %bitcast.18), channel_id=1, replica_groups=mesh['dp'=8,'tensor'=16] {'tensor'}, dimensions={0} | all-to-all | bytes 1703936 | tf_op jit(solution)/shard_map/all_to_all | solution.py:229
  24.9 5.3 %rotate.1 = bf16[16,16,1664]{2,1,0:T(8,128)(2,1)} custom-call(bf16[16,16,1664]{2,1,0:T(8,128)(2,1)S(1)} %all_to_all.10.hidden_ref, bf16[4,1664,512]{2,1,0:T(8,128)(2,1)} %constant.9.clone.table_ref), custom_call_target="tpu_custom_call" | custom-call | flops 1417674752 | bytes 7241728 | tf_op jit(solution)/shard_map/rotate/pallas_call | solution.py:84
  30.3 4.4 %all-to-all-start.1 = ((bf16[16,16,1664]{2,1,0:T(8,128)(2,1)}), bf16[16,16,1664]{2,1,0:T(8,128)(2,1)S(1)}, u32[]{:S(2)}, u32[]{:S(2)}) async-start(bf16[16,16,1664]{2,1,0:T(8,128)(2,1)} %rotate.1), calls=%async_computation.1 | async-start | bytes 1703936 | tf_op jit(solution)/shard_map/all_to_all | solution.py:231
  34.7 15.4 %all-to-all-done.1.rot_ref = bf16[16,16,1664]{2,1,0:T(8,128)(2,1)S(1)} async-done(((bf16[16,16,1664]{2,1,0:T(8,128)(2,1)}), bf16[16,16,1664]{2,1,0:T(8,128)(2,1)S(1)}, u32[]{:S(2)}, u32[]{:S(2)}) %all-to-all-start.1) | async-done | bytes 852000 | tf_op jit(solution)/shard_map/all_to_all | solution.py:231
  50.1 8.1 %project.3 = (bf16[8,16,4096]{2,1,0:T(8,128)(2,1)S(1)}, bf16[8,16,4096]{2,1,0:T(8,128)(2,1)S(1)}) custom-call(s32[1]{0:T(128)} %bitcast.place_ref, bf16[16,16,1664]{2,1,0:T(8,128)(2,1)S(1)} %all-to-all-done.1.rot_ref, s32[208,8192]{1,0:T(8,128)} %low_ref.3, s32[208,8192]{1,0:T(8,128)} %high_ref.3, bf16[13,8192]{1,0:T(8,128)(2,1)} %scale_ref.3), custom_call_target="tpu_custom_call" | custom-call | flops 3489660928 | bytes 11010048 | tf_op jit(solution)/shard_map/project/pallas_call | solution.py:145
  59.0 8.1 %project.2 = (bf16[8,16,4096]{2,1,0:T(8,128)(2,1)S(1)}, bf16[8,16,4096]{2,1,0:T(8,128)(2,1)S(1)}) custom-call(s32[1]{0:T(128)} %bitcast.place_ref, bf16[16,16,1664]{2,1,0:T(8,128)(2,1)S(1)} %all-to-all-done.1.rot_ref, s32[208,8192]{1,0:T(8,128)} %low_ref.3, s32[208,8192]{1,0:T(8,128)} %high_ref.3, bf16[13,8192]{1,0:T(8,128)(2,1)} %scale_ref.3), custom_call_target="tpu_custom_call" | custom-call | flops 3489660928 | bytes 11010048 | tf_op jit(solution)/shard_map/project/pallas_call | solution.py:145
  67.7 2.2 %collective-permute-done = bf16[8,16,4096]{2,1,0:T(8,128)(2,1)S(1)} collective-permute-done((bf16[8,16,4096]{2,1,0:T(8,128)(2,1)S(1)}, bf16[8,16,4096]{2,1,0:T(8,128)(2,1)S(1)}, u32[]{:S(2)}, u32[]{:S(2)}) %collective-permute-start) | collective-permute-done | bytes 1048608 | tf_op jit(solution)/shard_map/ppermute | solution.py:221
  70.7 2.8 %collective-permute-start.3 = (bf16[2,16,4096]{2,1,0:T(8,128)(2,1)S(1)}, bf16[2,16,4096]{2,1,0:T(8,128)(2,1)S(1)}, u32[]{:S(2)}, u32[]{:S(2)}) collective-permute-start(bf16[2,16,4096]{2,1,0:T(8,128)(2,1)S(1)} %get-tuple-element.26), channel_id=1, source_target_pairs={{0,6},{1,7},{2,4},{3,5},{4,2},{5,3},{6,0},{7,1},{8,14},{9,15},{10,... | collective-permute-start | bytes 786440 | tf_op jit(solution)/shard_map/ppermute | solution.py:221
  73.4 8.6 %collective-permute-done.13 = bf16[4,16,4096]{2,1,0:T(8,128)(2,1)S(1)} collective-permute-done((bf16[4,16,4096]{2,1,0:T(8,128)(2,1)S(1)}, bf16[4,16,4096]{2,1,0:T(8,128)(2,1)S(1)}, u32[]{:S(2)}, u32[]{:S(2)}) %collective-permute-start.13) | collective-permute-done | bytes 524320 | tf_op jit(solution)/shard_map/ppermute | solution.py:221
  83.6 1.9 %collective-permute-start.16 = (bf16[16,4096]{1,0:T(8,128)(2,1)S(1)}, bf16[16,4096]{1,0:T(8,128)(2,1)S(1)}, u32[]{:S(2)}, u32[]{:S(2)}) collective-permute-start(bf16[16,4096]{1,0:T(8,128)(2,1)S(1)} %get-tuple-element.29), channel_id=1, source_target_pairs={{0,6},{1,7},{2,4},{3,5},{4,2},{5,3},{6,0},{7,1},{8,14},{9,15},{10,... | collective-permute-start | bytes 393224 | tf_op jit(solution)/shard_map/ppermute | solution.py:221
  86.3 1.3 %collective-permute-done.14 = bf16[16,4096]{1,0:T(8,128)(2,1)S(1)} collective-permute-done((bf16[16,4096]{1,0:T(8,128)(2,1)S(1)}, bf16[16,4096]{1,0:T(8,128)(2,1)S(1)}, u32[]{:S(2)}, u32[]{:S(2)}) %collective-permute-start.14) | collective-permute-done | bytes 131104 | tf_op jit(solution)/shard_map/ppermute | solution.py:221
  87.6 1.5 %collective-permute-done.15 = bf16[16,4096]{1,0:T(8,128)(2,1)S(1)} collective-permute-done((bf16[16,4096]{1,0:T(8,128)(2,1)S(1)}, bf16[16,4096]{1,0:T(8,128)(2,1)S(1)}, u32[]{:S(2)}, u32[]{:S(2)}) %collective-permute-start.15) | collective-permute-done | bytes 131104 | tf_op jit(solution)/shard_map/ppermute | solution.py:221
  89.2 1.9 %collective-permute-done.16 = bf16[16,4096]{1,0:T(8,128)(2,1)S(1)} collective-permute-done((bf16[16,4096]{1,0:T(8,128)(2,1)S(1)}, bf16[16,4096]{1,0:T(8,128)(2,1)S(1)}, u32[]{:S(2)}, u32[]{:S(2)}) %collective-permute-start.16) | collective-permute-done | bytes 131104 | tf_op jit(solution)/shard_map/ppermute | solution.py:221
  91.2 1.6 %collective-permute-start.18 = (bf16[16,4096]{1,0:T(8,128)(2,1)S(1)}, bf16[16,4096]{1,0:T(8,128)(2,1)S(1)}, u32[]{:S(2)}, u32[]{:S(2)}) collective-permute-start(bf16[16,4096]{1,0:T(8,128)(2,1)S(1)} %fusion.6), channel_id=1, source_target_pairs={{0,4},{1,5},{2,6},{3,7},{4,0},{5,1},{6,2},{7,3},{8,12},{9,13},{10,... | collective-permute-start | bytes 393224 | tf_op jit(solution)/shard_map/ppermute | solution.py:221
  92.9 2.2 %collective-permute-start.19 = (bf16[16,4096]{1,0:T(8,128)(2,1)S(1)}, bf16[16,4096]{1,0:T(8,128)(2,1)S(1)}, u32[]{:S(2)}, u32[]{:S(2)}) collective-permute-start(bf16[16,4096]{1,0:T(8,128)(2,1)S(1)} %fusion.6), channel_id=1, source_target_pairs={{0,6},{1,7},{2,4},{3,5},{4,2},{5,3},{6,0},{7,1},{8,14},{9,15},{10,... | collective-permute-start | bytes 393224 | tf_op jit(solution)/shard_map/ppermute | solution.py:221
  95.3 1.6 %collective-permute-done.18 = bf16[16,4096]{1,0:T(8,128)(2,1)S(1)} collective-permute-done((bf16[16,4096]{1,0:T(8,128)(2,1)S(1)}, bf16[16,4096]{1,0:T(8,128)(2,1)S(1)}, u32[]{:S(2)}, u32[]{:S(2)}) %collective-permute-start.18) | collective-permute-done | bytes 131104 | tf_op jit(solution)/shard_map/ppermute | solution.py:221
  96.9 2.0 %collective-permute-done.19 = bf16[16,4096]{1,0:T(8,128)(2,1)S(1)} collective-permute-done((bf16[16,4096]{1,0:T(8,128)(2,1)S(1)}, bf16[16,4096]{1,0:T(8,128)(2,1)S(1)}, u32[]{:S(2)}, u32[]{:S(2)}) %collective-permute-start.19) | collective-permute-done | bytes 131104 | tf_op jit(solution)/shard_map/ppermute | solution.py:221
  99.0 2.0 %collective-permute-start.20 = (bf16[4,16,4096]{2,1,0:T(8,128)(2,1)S(1)}, bf16[4,16,4096]{2,1,0:T(8,128)(2,1)S(1)}, u32[]{:S(2)}, u32[]{:S(2)}) collective-permute-start(bf16[4,16,4096]{2,1,0:T(8,128)(2,1)S(1)} %pad_maximum_fusion.refs_0_), channel_id=1, source_target_pairs={{0,8},{1,9},{2,10},{3,11},{4,12},{5,13},{6,14},{7,15},{8,0},{9,1},... | collective-permute-start | bytes 1572872 | tf_op jit(solution)/shard_map/ppermute | solution.py:221
  101.7 2.7 %collective-permute-start.11 = (bf16[2,16,4096]{2,1,0:T(8,128)(2,1)S(1)}, bf16[2,16,4096]{2,1,0:T(8,128)(2,1)S(1)}, u32[]{:S(2)}, u32[]{:S(2)}) collective-permute-start(bf16[2,16,4096]{2,1,0:T(8,128)(2,1)S(1)} %add_convert_fusion.1.refs_0_), channel_id=1, source_target_pairs={{0,1},{1,0},{2,3},{3,2},{4,5},{5,4},{6,7},{7,6},{8,9},{9,8},{10,11... | collective-permute-start | bytes 786440 | tf_op jit(solution)/shard_map/ppermute | solution.py:221
  105.4 1.2 collective-permute-start.9
  106.5 1.8 %collective-permute-done.5.refs_0_ = bf16[2,16,4096]{2,1,0:T(8,128)(2,1)S(1)} collective-permute-done((bf16[2,16,4096]{2,1,0:T(8,128)(2,1)S(1)}, bf16[2,16,4096]{2,1,0:T(8,128)(2,1)S(1)}, u32[]{:S(2)}, u32[]{:S(2)}) %collective-permute-start.5) | collective-permute-done | bytes 262176 | tf_op jit(solution)/shard_map/ppermute | solution.py:221
  108.3 5.5 %collective-permute-start.21 = (bf16[4,16,4096]{2,1,0:T(8,128)(2,1)S(1)}, bf16[4,16,4096]{2,1,0:T(8,128)(2,1)S(1)}, u32[]{:S(2)}, u32[]{:S(2)}) collective-permute-start(bf16[4,16,4096]{2,1,0:T(8,128)(2,1)S(1)} %pad_maximum_fusion.refs_0_), channel_id=1, source_target_pairs={{0,1},{1,0},{2,3},{3,2},{4,5},{5,4},{6,7},{7,6},{8,9},{9,8},{10,11... | collective-permute-start | bytes 1572872 | tf_op jit(solution)/shard_map/ppermute | solution.py:221
  117.8 1.4 %put.5.refs_4_ = bf16[256,8192]{1,0:T(8,128)(2,1)} custom-call(s32[1]{0:T(128)} %bitcast.place_ref, bf16[4,16,4096]{2,1,0:T(8,128)(2,1)S(1)} %pad_maximum_fusion.refs_0_, bf16[4,16,4096]{2,1,0:T(8,128)(2,1)S(1)} %collective-permute-done.20.refs_1_, bf16[4,16,4096]{2,1,0:T(8,128)(2,1)S(1)} %collective-permute-done.21.refs_2_, ...), custom_call_target="tpu_custom_call", output_to_operand_aliasing={{}: (5, {})} | custom-call | bytes 4194304 | tf_op jit(solution)/shard_map/put/pallas_call | solution.py:195
  (41 shorter events, 12.7 us)
Async XLA Ops:
  30.3 19.8 %all-to-all-start.1 = ((bf16[16,16,1664]{2,1,0:T(8,128)(2,1)}), bf16[16,16,1664]{2,1,0:T(8,128)(2,1)S(1)}, u32[]{:S(2)}, u32[]{:S(2)}) async-start(bf16[16,16,1664]{2,1,0:T(8,128)(2,1)} %rotate.1), calls=%async_computation.1 | async-start | bytes 1703936 | tf_op jit(solution)/shard_map/all_to_all | solution.py:231
  58.2 9.0 %collective-permute-start.12 = (bf16[8,16,4096]{2,1,0:T(8,128)(2,1)S(1)}, bf16[8,16,4096]{2,1,0:T(8,128)(2,1)S(1)}, u32[]{:S(2)}, u32[]{:S(2)}) collective-permute-start(bf16[8,16,4096]{2,1,0:T(8,128)(2,1)S(1)} %get-tuple-element.17), channel_id=1, source_target_pairs={{0,1},{1,0},{2,3},{3,2},{4,5},{5,4},{6,7},{7,6},{8,9},{9,8},{10,11... | collective-permute-start | bytes 3145736 | tf_op jit(solution)/shard_map/ppermute | solution.py:221
  67.1 2.7 %collective-permute-start = (bf16[8,16,4096]{2,1,0:T(8,128)(2,1)S(1)}, bf16[8,16,4096]{2,1,0:T(8,128)(2,1)S(1)}, u32[]{:S(2)}, u32[]{:S(2)}) collective-permute-start(bf16[8,16,4096]{2,1,0:T(8,128)(2,1)S(1)} %get-tuple-element.15), channel_id=1, source_target_pairs={{0,1},{1,0},{2,3},{3,2},{4,5},{5,4},{6,7},{7,6},{8,9},{9,8},{10,11... | collective-permute-start | bytes 3145736 | tf_op jit(solution)/shard_map/ppermute | solution.py:221
  67.4 14.6 %collective-permute-start.13 = (bf16[4,16,4096]{2,1,0:T(8,128)(2,1)S(1)}, bf16[4,16,4096]{2,1,0:T(8,128)(2,1)S(1)}, u32[]{:S(2)}, u32[]{:S(2)}) collective-permute-start(bf16[4,16,4096]{2,1,0:T(8,128)(2,1)S(1)} %add_convert_fusion), channel_id=1, source_target_pairs={{0,8},{1,9},{2,10},{3,11},{4,12},{5,13},{6,14},{7,15},{8,0},{9,1},... | collective-permute-start | bytes 1572872 | tf_op jit(solution)/shard_map/ppermute | solution.py:221
  70.1 13.6 %collective-permute-start.1 = (bf16[2,16,4096]{2,1,0:T(8,128)(2,1)S(1)}, bf16[2,16,4096]{2,1,0:T(8,128)(2,1)S(1)}, u32[]{:S(2)}, u32[]{:S(2)}) collective-permute-start(bf16[2,16,4096]{2,1,0:T(8,128)(2,1)S(1)} %get-tuple-element.25), channel_id=1, source_target_pairs={{0,4},{1,5},{2,6},{3,7},{4,0},{5,1},{6,2},{7,3},{8,12},{9,13},{10,... | collective-permute-start | bytes 786440 | tf_op jit(solution)/shard_map/ppermute | solution.py:221
  70.2 15.4 %collective-permute-start.2 = (bf16[2,16,4096]{2,1,0:T(8,128)(2,1)S(1)}, bf16[2,16,4096]{2,1,0:T(8,128)(2,1)S(1)}, u32[]{:S(2)}, u32[]{:S(2)}) collective-permute-start(bf16[2,16,4096]{2,1,0:T(8,128)(2,1)S(1)} %get-tuple-element.27), channel_id=1, source_target_pairs={{0,2},{1,3},{2,0},{3,1},{4,6},{5,7},{6,4},{7,5},{8,10},{9,11},{10,... | collective-permute-start | bytes 786440 | tf_op jit(solution)/shard_map/ppermute | solution.py:221
  70.7 14.9 %collective-permute-start.3 = (bf16[2,16,4096]{2,1,0:T(8,128)(2,1)S(1)}, bf16[2,16,4096]{2,1,0:T(8,128)(2,1)S(1)}, u32[]{:S(2)}, u32[]{:S(2)}) collective-permute-start(bf16[2,16,4096]{2,1,0:T(8,128)(2,1)S(1)} %get-tuple-element.26), channel_id=1, source_target_pairs={{0,6},{1,7},{2,4},{3,5},{4,2},{5,3},{6,0},{7,1},{8,14},{9,15},{10,... | collective-permute-start | bytes 786440 | tf_op jit(solution)/shard_map/ppermute | solution.py:221
  82.2 5.4 %collective-permute-start.14 = (bf16[16,4096]{1,0:T(8,128)(2,1)S(1)}, bf16[16,4096]{1,0:T(8,128)(2,1)S(1)}, u32[]{:S(2)}, u32[]{:S(2)}) collective-permute-start(bf16[16,4096]{1,0:T(8,128)(2,1)S(1)} %get-tuple-element.28), channel_id=1, source_target_pairs={{0,4},{1,5},{2,6},{3,7},{4,0},{5,1},{6,2},{7,3},{8,12},{9,13},{10,... | collective-permute-start | bytes 393224 | tf_op jit(solution)/shard_map/ppermute | solution.py:221
  83.1 6.0 %collective-permute-start.15 = (bf16[16,4096]{1,0:T(8,128)(2,1)S(1)}, bf16[16,4096]{1,0:T(8,128)(2,1)S(1)}, u32[]{:S(2)}, u32[]{:S(2)}) collective-permute-start(bf16[16,4096]{1,0:T(8,128)(2,1)S(1)} %get-tuple-element.30), channel_id=1, source_target_pairs={{0,2},{1,3},{2,0},{3,1},{4,6},{5,7},{6,4},{7,5},{8,10},{9,11},{10,... | collective-permute-start | bytes 393224 | tf_op jit(solution)/shard_map/ppermute | solution.py:221
  83.6 7.4 %collective-permute-start.16 = (bf16[16,4096]{1,0:T(8,128)(2,1)S(1)}, bf16[16,4096]{1,0:T(8,128)(2,1)S(1)}, u32[]{:S(2)}, u32[]{:S(2)}) collective-permute-start(bf16[16,4096]{1,0:T(8,128)(2,1)S(1)} %get-tuple-element.29), channel_id=1, source_target_pairs={{0,6},{1,7},{2,4},{3,5},{4,2},{5,3},{6,0},{7,1},{8,14},{9,15},{10,... | collective-permute-start | bytes 393224 | tf_op jit(solution)/shard_map/ppermute | solution.py:221
  85.7 9.4 %collective-permute-start.4 = (bf16[2,16,4096]{2,1,0:T(8,128)(2,1)S(1)}, bf16[2,16,4096]{2,1,0:T(8,128)(2,1)S(1)}, u32[]{:S(2)}, u32[]{:S(2)}) collective-permute-start(bf16[2,16,4096]{2,1,0:T(8,128)(2,1)S(1)} %fusion.7), channel_id=1, source_target_pairs={{0,8},{1,9},{2,10},{3,11},{4,12},{5,13},{6,14},{7,15},{8,0},{9,1},... | collective-permute-start | bytes 786440 | tf_op jit(solution)/shard_map/ppermute | solution.py:221
  91.1 4.2 %collective-permute-start.17 = (bf16[16,4096]{1,0:T(8,128)(2,1)S(1)}, bf16[16,4096]{1,0:T(8,128)(2,1)S(1)}, u32[]{:S(2)}, u32[]{:S(2)}) collective-permute-start(bf16[16,4096]{1,0:T(8,128)(2,1)S(1)} %fusion.6), channel_id=1, source_target_pairs={{0,2},{1,3},{2,0},{3,1},{4,6},{5,7},{6,4},{7,5},{8,10},{9,11},{10,... | collective-permute-start | bytes 393224 | tf_op jit(solution)/shard_map/ppermute | solution.py:221
  91.2 5.7 %collective-permute-start.18 = (bf16[16,4096]{1,0:T(8,128)(2,1)S(1)}, bf16[16,4096]{1,0:T(8,128)(2,1)S(1)}, u32[]{:S(2)}, u32[]{:S(2)}) collective-permute-start(bf16[16,4096]{1,0:T(8,128)(2,1)S(1)} %fusion.6), channel_id=1, source_target_pairs={{0,4},{1,5},{2,6},{3,7},{4,0},{5,1},{6,2},{7,3},{8,12},{9,13},{10,... | collective-permute-start | bytes 393224 | tf_op jit(solution)/shard_map/ppermute | solution.py:221
  92.9 6.0 %collective-permute-start.19 = (bf16[16,4096]{1,0:T(8,128)(2,1)S(1)}, bf16[16,4096]{1,0:T(8,128)(2,1)S(1)}, u32[]{:S(2)}, u32[]{:S(2)}) collective-permute-start(bf16[16,4096]{1,0:T(8,128)(2,1)S(1)} %fusion.6), channel_id=1, source_target_pairs={{0,6},{1,7},{2,4},{3,5},{4,2},{5,3},{6,0},{7,1},{8,14},{9,15},{10,... | collective-permute-start | bytes 393224 | tf_op jit(solution)/shard_map/ppermute | solution.py:221
  99.0 14.8 %collective-permute-start.20 = (bf16[4,16,4096]{2,1,0:T(8,128)(2,1)S(1)}, bf16[4,16,4096]{2,1,0:T(8,128)(2,1)S(1)}, u32[]{:S(2)}, u32[]{:S(2)}) collective-permute-start(bf16[4,16,4096]{2,1,0:T(8,128)(2,1)S(1)} %pad_maximum_fusion.refs_0_), channel_id=1, source_target_pairs={{0,8},{1,9},{2,10},{3,11},{4,12},{5,13},{6,14},{7,15},{8,0},{9,1},... | collective-permute-start | bytes 1572872 | tf_op jit(solution)/shard_map/ppermute | solution.py:221
  101.0 7.3 %collective-permute-start.5 = (bf16[2,16,4096]{2,1,0:T(8,128)(2,1)S(1)}, bf16[2,16,4096]{2,1,0:T(8,128)(2,1)S(1)}, u32[]{:S(2)}, u32[]{:S(2)}) collective-permute-start(bf16[2,16,4096]{2,1,0:T(8,128)(2,1)S(1)} %add_convert_fusion.1.refs_0_), channel_id=1, source_target_pairs={{0,4},{1,5},{2,6},{3,7},{4,0},{5,1},{6,2},{7,3},{8,12},{9,13},{10,... | collective-permute-start | bytes 786440 | tf_op jit(solution)/shard_map/ppermute | solution.py:221
  101.7 17.6 %collective-permute-start.11 = (bf16[2,16,4096]{2,1,0:T(8,128)(2,1)S(1)}, bf16[2,16,4096]{2,1,0:T(8,128)(2,1)S(1)}, u32[]{:S(2)}, u32[]{:S(2)}) collective-permute-start(bf16[2,16,4096]{2,1,0:T(8,128)(2,1)S(1)} %add_convert_fusion.1.refs_0_), channel_id=1, source_target_pairs={{0,1},{1,0},{2,3},{3,2},{4,5},{5,4},{6,7},{7,6},{8,9},{9,8},{10,11... | collective-permute-start | bytes 786440 | tf_op jit(solution)/shard_map/ppermute | solution.py:221
  104.4 13.0 %collective-permute-start.7 = (bf16[2,16,4096]{2,1,0:T(8,128)(2,1)S(1)}, bf16[2,16,4096]{2,1,0:T(8,128)(2,1)S(1)}, u32[]{:S(2)}, u32[]{:S(2)}) collective-permute-start(bf16[2,16,4096]{2,1,0:T(8,128)(2,1)S(1)} %add_convert_fusion.1.refs_0_), channel_id=1, source_target_pairs={{0,2},{1,3},{2,0},{3,1},{4,6},{5,7},{6,4},{7,5},{8,10},{9,11},{10,... | collective-permute-start | bytes 786440 | tf_op jit(solution)/shard_map/ppermute | solution.py:221
  105.4 11.2 %collective-permute-start.9 = (bf16[2,16,4096]{2,1,0:T(8,128)(2,1)S(1)}, bf16[2,16,4096]{2,1,0:T(8,128)(2,1)S(1)}, u32[]{:S(2)}, u32[]{:S(2)}) collective-permute-start(bf16[2,16,4096]{2,1,0:T(8,128)(2,1)S(1)} %add_convert_fusion.1.refs_0_), channel_id=1, source_target_pairs={{0,6},{1,7},{2,4},{3,5},{4,2},{5,3},{6,0},{7,1},{8,14},{9,15},{10,... | collective-permute-start | bytes 786440 | tf_op jit(solution)/shard_map/ppermute | solution.py:221
  108.3 9.1 %collective-permute-start.21 = (bf16[4,16,4096]{2,1,0:T(8,128)(2,1)S(1)}, bf16[4,16,4096]{2,1,0:T(8,128)(2,1)S(1)}, u32[]{:S(2)}, u32[]{:S(2)}) collective-permute-start(bf16[4,16,4096]{2,1,0:T(8,128)(2,1)S(1)} %pad_maximum_fusion.refs_0_), channel_id=1, source_target_pairs={{0,1},{1,0},{2,3},{3,2},{4,5},{5,4},{6,7},{7,6},{8,9},{9,8},{10,11... | collective-permute-start | bytes 1572872 | tf_op jit(solution)/shard_map/ppermute | solution.py:221
  113.7 4.1 %collective-permute-start.22 = (bf16[4,16,4096]{2,1,0:T(8,128)(2,1)S(1)}, bf16[4,16,4096]{2,1,0:T(8,128)(2,1)S(1)}, u32[]{:S(2)}, u32[]{:S(2)}) collective-permute-start(bf16[4,16,4096]{2,1,0:T(8,128)(2,1)S(1)} %collective-permute-done.20.refs_1_), channel_id=1, source_target_pairs={{0,1},{1,0},{2,3},{3,2},{4,5},{5,4},{6,7},{7,6},{8,9},{9,8},{10,11... | collective-permute-start | bytes 1572872 | tf_op jit(solution)/shard_map/ppermute | solution.py:221
  116.6 3.7 %collective-permute-start.10 = (bf16[2,16,4096]{2,1,0:T(8,128)(2,1)S(1)}, bf16[2,16,4096]{2,1,0:T(8,128)(2,1)S(1)}, u32[]{:S(2)}, u32[]{:S(2)}) collective-permute-start(bf16[2,16,4096]{2,1,0:T(8,128)(2,1)S(1)} %collective-permute-done.9.refs_2_), channel_id=1, source_target_pairs={{0,1},{1,0},{2,3},{3,2},{4,5},{5,4},{6,7},{7,6},{8,9},{9,8},{10,11... | collective-permute-start | bytes 786440 | tf_op jit(solution)/shard_map/ppermute | solution.py:221
  117.3 3.0 %collective-permute-start.6 = (bf16[2,16,4096]{2,1,0:T(8,128)(2,1)S(1)}, bf16[2,16,4096]{2,1,0:T(8,128)(2,1)S(1)}, u32[]{:S(2)}, u32[]{:S(2)}) collective-permute-start(bf16[2,16,4096]{2,1,0:T(8,128)(2,1)S(1)} %collective-permute-done.5.refs_0_), channel_id=1, source_target_pairs={{0,1},{1,0},{2,3},{3,2},{4,5},{5,4},{6,7},{7,6},{8,9},{9,8},{10,11... | collective-permute-start | bytes 786440 | tf_op jit(solution)/shard_map/ppermute | solution.py:221
  117.3 3.0 %collective-permute-start.8 = (bf16[2,16,4096]{2,1,0:T(8,128)(2,1)S(1)}, bf16[2,16,4096]{2,1,0:T(8,128)(2,1)S(1)}, u32[]{:S(2)}, u32[]{:S(2)}) collective-permute-start(bf16[2,16,4096]{2,1,0:T(8,128)(2,1)S(1)} %collective-permute-done.7.refs_1_), channel_id=1, source_target_pairs={{0,1},{1,0},{2,3},{3,2},{4,5},{5,4},{6,7},{7,6},{8,9},{9,8},{10,11... | collective-permute-start | bytes 786440 | tf_op jit(solution)/shard_map/ppermute | solution.py:221

commit v5 on v4

--- a/solution.py
+++ b/solution.py
@@ -170,6 +170,123 @@
     )(place, rot, in_hbm(low), in_hbm(high), in_hbm(scales))
 
 
+TILE = 1024
+CUTS = 4
+
+
+def dequant_body(low_ref, high_ref, scale_ref, out_ref, buf, sems):
+    step, steps = pl.program_id(0), pl.num_programs(0)
+    depth = buf.shape[1]
+
+    def stores(at):
+        slot = at % 2
+        cuts = [pl.ds(depth // CUTS * i, depth // CUTS) for i in range(CUTS)]
+        return [pltpu.make_async_copy(buf.at[slot, c], out_ref.at[at, c], sems.at[slot, i]) for i, c in enumerate(cuts)]
+
+    @pl.when(step >= 2)
+    def _():
+        for copy in stores(step - 2):
+            copy.wait()
+
+    unpack(low_ref, high_ref, scale_ref, 0, buf.at[step % 2])
+    for copy in stores(step):
+        copy.start()
+
+    @pl.when(step == steps - 1)
+    def _():
+        for at in (steps - 2, steps - 1):
+            for copy in stores(at):
+                copy.wait()
+
+
+def dequant(low, high, scales, first, width):
+    depth = low.shape[0] * 8
+    tiles, start = width // TILE, first // TILE
+    return pl.pallas_call(
+        dequant_body,
+        grid=(tiles,),
+        in_specs=[
+            pl.BlockSpec((low.shape[0], TILE), lambda j: (0, j + start)),
+            pl.BlockSpec((high.shape[0], TILE), lambda j: (0, j + start)),
+            pl.BlockSpec((scales.shape[0], TILE), lambda j: (0, j + start)),
+        ],
+        out_specs=pl.BlockSpec(memory_space=pltpu.HBM),
+        out_shape=pltpu.HBM((tiles, depth, TILE), jnp.bfloat16),
+        scratch_shapes=[pltpu.VMEM((2, depth, TILE), jnp.bfloat16), pltpu.SemaphoreType.DMA((2, CUTS))],
+        compiler_params=pltpu.CompilerParams(vmem_limit_bytes=VMEM_LIMIT),
+        cost_estimate=pl.CostEstimate(
+            flops=8 * depth * width,
+            bytes_accessed=3 * depth * width,
+            transcendentals=0,
+        ),
+        name="dequant",
+    )(in_hbm(low), in_hbm(high), in_hbm(scales))
+
+
+def stream_body(order, place_ref, rot_ref, weight_ref, keep_ref, send_ref, lhs_ref, buf, sems):
+    shards, rows, depth = rot_ref.shape
+    step, steps = pl.program_id(0), pl.num_programs(0)
+    slots = buf.shape[0]
+
+    def loads(at):
+        slot = at % slots
+        cuts = [pl.ds(depth // CUTS * i, depth // CUTS) for i in range(CUTS)]
+        return [pltpu.make_async_copy(weight_ref.at[at, c], buf.at[slot, c], sems.at[slot, i]) for i, c in enumerate(cuts)]
+
+    def load(at):
+        @pl.when(at < steps)
+        def _():
+            for copy in loads(at):
+                copy.start()
+
+    @pl.when(step == 0)
+    def _():
+        load(0)
+        load(1)
+        for at, block in enumerate(order):
+            lhs_ref[rows * at : rows * (at + 1)] = rot_ref[jnp.bitwise_xor(place_ref[0], block)]
+
+    load(step + 2)
+    for copy in loads(step):
+        copy.wait()
+    term = jnp.dot(lhs_ref[...], buf[step % slots], preferred_element_type=jnp.float32)
+    both = term.astype(jnp.bfloat16).reshape(2, shards // 2, rows, TILE)
+    send_ref[...] = both[0]
+    keep_ref[...] = both[1]
+
+
+def project_unpacked(place, rot, weights, order):
+    shards, rows, depth = rot.shape
+    tiles = weights.shape[0]
+    full = tuple(q ^ 1 for q in order) + tuple(order)
+    shape = jax.ShapeDtypeStruct((shards // 2, rows, tiles * TILE), jnp.bfloat16)
+    return pl.pallas_call(
+        functools.partial(stream_body, full),
+        grid_spec=pltpu.PrefetchScalarGridSpec(
+            num_scalar_prefetch=1,
+            grid=(tiles,),
+            in_specs=[
+                pl.BlockSpec((shards, rows, depth), lambda j, p: (0, 0, 0)),
+                pl.BlockSpec(memory_space=pltpu.HBM),
+            ],
+            out_specs=[pl.BlockSpec((shards // 2, rows, TILE), lambda j, p: (0, 0, j))] * 2,
+            scratch_shapes=[
+                pltpu.VMEM((shards * rows, depth), jnp.bfloat16),
+                pltpu.VMEM((3, depth, TILE), jnp.bfloat16),
+                pltpu.SemaphoreType.DMA((3, CUTS)),
+            ],
+        ),
+        out_shape=[shape, shape],
+        compiler_params=pltpu.CompilerParams(vmem_limit_bytes=VMEM_LIMIT),
+        cost_estimate=pl.CostEstimate(
+            flops=2 * shards * rows * depth * tiles * TILE,
+            bytes_accessed=2 * depth * tiles * TILE + 4 * shards * rows * tiles * TILE,
+            transcendentals=0,
+        ),
+        name="project_unpacked",
+    )(place, rot, in_hbm(weights))
+
+
 def put_body(names, firsts, place_ref, *refs):
     pieces, out_ref, sems = refs[:-2], refs[-2], refs[-1]
     copies = []
@@ -230,10 +347,12 @@
     turned = rotate(mine, local_table(local_ff))
     rot = lax.all_to_all(turned, "tensor", 0, 0)
     codes = (down_low, down_high, down_scales)
+    weights = dequant(*codes, left, width - left)
+    rot, weights = lax.optimization_barrier((rot, weights))
 
     keep_p, send_p = project(place, rot, *codes, by_x, 0, left)
     got_p = swap(send_p, CORE)
-    keep_q, send_q = project(place, rot, *codes, by_y, left, width - left)
+    keep_q, send_q = project_unpacked(place, rot, weights, by_y)
     got_q = swap(send_q, CORE)
 
     def chip_p(k):
@@ -257,12 +376,12 @@
     done_p = (mine_p + theirs_p[::-1].astype(f32)).astype(bf16)
     done_q = (sum_q[0] + sum(t.astype(f32) for t in last_q)).astype(bf16)
 
-    all_p = [done_p] + [swap(done_p, X[k]) for k in (2, 1, 3)]
+    all_p = [done_p] + [swap(done_p, X[k]) for k in (1, 3, 2)]
     row_q = [done_q] + [swap(done_q, X[k]) for k in (1, 2, 3)]
     *row_q, _ = lax.optimization_barrier((*row_q, done_p))
     row_q = jnp.stack(row_q)
     all_q = [row_q, swap(row_q, Y)]
-    names_p = [tuple(X[k] | y for y in (0, Y)) for k in (0, 2, 1, 3)]
+    names_p = [tuple(X[k] | y for y in (0, Y)) for k in (0, 1, 3, 2)]
     names_q = [tuple(x | y for x in X) for y in (0, Y)]
     far_p = [swap(t, CORE) for t in all_p]
     far_q = [swap(t, CORE) for t in all_q]
@@ -274,8 +393,8 @@
         return put(place, pieces, names, [first] * len(pieces), (total_rows, width), into, weight)
 
     out = lay(None, all_p[:1], names_p[:1], 0, 20000000000)
+    out = lay(out, all_p[1:] + far_p[:1], names_p[1:] + across(names_p[:1]), 0, 20000000000)
     out = lay(out, all_q + far_q, names_q + across(names_q), left, 0)
-    out = lay(out, all_p[1:] + far_p[:1], names_p[1:] + across(names_p[:1]), 0, 20000000000)
     return lay(out, far_p[1:], across(names_p[1:]), 0, 0)
 
 

time: 122 us -> 119 us (0.975)
  Pallas kernels: 25.7 us -> 34.3 us
  waiting for transfers between devices: 37.2 us -> 30.5 us
  starting transfers between devices: 32.2 us -> 27.7 us
    pallas_call x0 -> x2, Pallas kernels: none -> 16.7 us  [the longest x1 10 us: dequant(): pl.pallas_call(dequant_body, grid=(tiles,), in_specs=[pl.BlockSpec((low.s...]
    all_to_all x1, waiting for transfers between devices: 15.4 us -> 5.33 us  [local(): rot = lax.all_to_all(turned, 'tensor', 0, 0)]
    pallas_call x2 -> x1, Pallas kernels: 16.3 us -> 8.11 us  [project(): pl.pallas_call(functools.partial(project_body, full), grid_spec=pltpu.Pre...]
    ppermute x23, starting transfers between devices: 27.8 us -> 23.2 us  [swap(): return lax.ppermute(x, 'tensor', [(i, i ^ mask) for i in range(shards)])]
    ppermute x23, waiting for transfers between devices: 21.9 us -> 25.1 us  [swap(): return lax.ppermute(x, 'tensor', [(i, i ^ mask) for i in range(shards)])]
  transfers between devices with their start and end apart: 24 -> 24, of which waited for: 10 -> 10; matrix products, arithmetic and copies ran while one was open for 1% -> 1% of each run, Pallas kernels for 9% -> 18%
where the time goes in v5:
time: 119 us
  Pallas kernels  34.3 us (29%)
  waiting for transfers between devices  30.5 us (26%)
  starting transfers between devices  27.7 us (23%)
  blocking collectives  23 us (19%)
  other arithmetic  2.96 us (2%)
    ppermute x23, waiting for transfers between devices, swap(): return lax.ppermute(x, 'tensor', [(i, i ^ mask) for i in range(shards)])  25.1 us
    ppermute x23, starting transfers between devices, swap(): return lax.ppermute(x, 'tensor', [(i, i ^ mask) for i in range(shards)])  23.2 us
    all_to_all x1, blocking collectives, local(): lax.all_to_all(hidden.reshape(shards, rows, local_ff), 'tensor', 0, 0)  23 us
    pallas_call x1, Pallas kernels, dequant(): pl.pallas_call(dequant_body, grid=(tiles,), in_specs=[pl.BlockSpec((low.s...  10 us
    pallas_call x1, Pallas kernels, project(): pl.pallas_call(functools.partial(project_body, full), grid_spec=pltpu.Pre...  8.11 us
    pallas_call x1, Pallas kernels, project_unpacked(): pl.pallas_call(functools.partial(stream_body, full), grid_spec=pltpu.Pref...  6.71 us
    pallas_call x1, Pallas kernels, rotate(): pl.pallas_call(rotate_body, in_specs=[pl.BlockSpec(memory_space=pltpu.VME...  5.34 us
    all_to_all x1, waiting for transfers between devices, local(): rot = lax.all_to_all(turned, 'tensor', 0, 0)  5.33 us
  transfers between devices with their start and end apart: 24, of which 10 were waited for; matrix products, arithmetic and copies ran while one was open for 1% of the time, Pallas kernels for 18%

profile of v5, /device:TPU:1, one launch (start us, length us, event | category | flops | bytes accessed | tf_op | source)
XLA Modules:
  0.0 118.5 jit_solution(11121163409814920460)
XLA Ops:
  0.0 1.9 %fusion.4 = bf16[256,1664]{1,0:T(8,128)(2,1)S(1)} fusion(bf16[256,1664]{1,0:T(8,128)(2,1)} %param.7, bf16[256,1664]{1,0:T(8,128)(2,1)} %param.6), kind=kLoop, calls=%fused_computation.6 | loop fusion | flops 3407872 | bytes 2555904 | tf_op jit(solution)/shard_map/convert_element_type | solution.py:345
  1.9 23.0 %all_to_all.10.hidden_ref = bf16[16,16,1664]{2,1,0:T(8,128)(2,1)S(1)} all-to-all(bf16[16,16,1664]{2,1,0:T(8,128)(2,1)S(1)} %bitcast.18), channel_id=1, replica_groups=mesh['dp'=8,'tensor'=16] {'tensor'}, dimensions={0} | all-to-all | bytes 1703936 | tf_op jit(solution)/shard_map/all_to_all | solution.py:346
  24.9 5.3 %rotate.1 = bf16[16,16,1664]{2,1,0:T(8,128)(2,1)} custom-call(bf16[16,16,1664]{2,1,0:T(8,128)(2,1)S(1)} %all_to_all.10.hidden_ref, bf16[4,1664,512]{2,1,0:T(8,128)(2,1)} %constant.9.clone.table_ref), custom_call_target="tpu_custom_call" | custom-call | flops 1417674752 | bytes 7241728 | tf_op jit(solution)/shard_map/rotate/pallas_call | solution.py:84
  30.3 4.4 %all-to-all-start.1 = ((bf16[16,16,1664]{2,1,0:T(8,128)(2,1)}), bf16[16,16,1664]{2,1,0:T(8,128)(2,1)S(1)}, u32[]{:S(2)}, u32[]{:S(2)}) async-start(bf16[16,16,1664]{2,1,0:T(8,128)(2,1)} %rotate.1), calls=%async_computation.1 | async-start | bytes 1703936 | tf_op jit(solution)/shard_map/all_to_all | solution.py:348
  34.7 10.0 %dequant.1.weight_ref = bf16[4,1664,1024]{2,1,0:T(8,128)(2,1)} custom-call(s32[208,8192]{1,0:T(8,128)} %low_ref.3, s32[208,8192]{1,0:T(8,128)} %high_ref.3, bf16[13,8192]{1,0:T(8,128)(2,1)} %scale_ref.3), custom_call_target="tpu_custom_call" | custom-call | flops 54525952 | bytes 20447232 | tf_op jit(solution)/shard_map/dequant/pallas_call | solution.py:205
  44.7 5.3 %all-to-all-done.1.rot_ref = bf16[16,16,1664]{2,1,0:T(8,128)(2,1)S(1)} async-done(((bf16[16,16,1664]{2,1,0:T(8,128)(2,1)}), bf16[16,16,1664]{2,1,0:T(8,128)(2,1)S(1)}, u32[]{:S(2)}, u32[]{:S(2)}) %all-to-all-start.1) | async-done | bytes 852000 | tf_op jit(solution)/shard_map/all_to_all | solution.py:348
  50.1 6.7 %project_unpacked.1 = (bf16[8,16,4096]{2,1,0:T(8,128)(2,1)S(1)}, bf16[8,16,4096]{2,1,0:T(8,128)(2,1)S(1)}) custom-call(s32[1]{0:T(128)} %bitcast.place_ref, bf16[16,16,1664]{2,1,0:T(8,128)(2,1)S(1)} %all-to-all-done.1.rot_ref, bf16[4,1664,1024]{2,1,0:T(8,128)(2,1)} %dequant.1.weight_ref), custom_call_target="tpu_custom_call" | custom-call | flops 3489660928 | bytes 17825792 | tf_op jit(solution)/shard_map/project_unpacked/pallas_call | solution.py:263
  57.6 8.1 %project.1 = (bf16[8,16,4096]{2,1,0:T(8,128)(2,1)S(1)}, bf16[8,16,4096]{2,1,0:T(8,128)(2,1)S(1)}) custom-call(s32[1]{0:T(128)} %bitcast.place_ref, bf16[16,16,1664]{2,1,0:T(8,128)(2,1)S(1)} %all-to-all-done.1.rot_ref, s32[208,8192]{1,0:T(8,128)} %low_ref.3, s32[208,8192]{1,0:T(8,128)} %high_ref.3, bf16[13,8192]{1,0:T(8,128)(2,1)} %scale_ref.3), custom_call_target="tpu_custom_call" | custom-call | flops 3489660928 | bytes 11010048 | tf_op jit(solution)/shard_map/project/pallas_call | solution.py:145
  66.2 2.2 %collective-permute-done = bf16[8,16,4096]{2,1,0:T(8,128)(2,1)S(1)} collective-permute-done((bf16[8,16,4096]{2,1,0:T(8,128)(2,1)S(1)}, bf16[8,16,4096]{2,1,0:T(8,128)(2,1)S(1)}, u32[]{:S(2)}, u32[]{:S(2)}) %collective-permute-start) | collective-permute-done | bytes 1048608 | tf_op jit(solution)/shard_map/ppermute | solution.py:338
  69.7 1.7 %collective-permute-start.2 = (bf16[2,16,4096]{2,1,0:T(8,128)(2,1)S(1)}, bf16[2,16,4096]{2,1,0:T(8,128)(2,1)S(1)}, u32[]{:S(2)}, u32[]{:S(2)}) collective-permute-start(bf16[2,16,4096]{2,1,0:T(8,128)(2,1)S(1)} %get-tuple-element.31), channel_id=1, source_target_pairs={{0,2},{1,3},{2,0},{3,1},{4,6},{5,7},{6,4},{7,5},{8,10},{9,11},{10,... | collective-permute-start | bytes 786440 | tf_op jit(solution)/shard_map/ppermute | solution.py:338
  71.4 9.2 %collective-permute-done.12 = bf16[4,16,4096]{2,1,0:T(8,128)(2,1)S(1)} collective-permute-done((bf16[4,16,4096]{2,1,0:T(8,128)(2,1)S(1)}, bf16[4,16,4096]{2,1,0:T(8,128)(2,1)S(1)}, u32[]{:S(2)}, u32[]{:S(2)}) %collective-permute-start.12) | collective-permute-done | bytes 524320 | tf_op jit(solution)/shard_map/ppermute | solution.py:338
  82.4 1.1 collective-permute-start.14
  84.9 1.4 %collective-permute-done.13 = bf16[16,4096]{1,0:T(8,128)(2,1)S(1)} collective-permute-done((bf16[16,4096]{1,0:T(8,128)(2,1)S(1)}, bf16[16,4096]{1,0:T(8,128)(2,1)S(1)}, u32[]{:S(2)}, u32[]{:S(2)}) %collective-permute-start.13) | collective-permute-done | bytes 131104 | tf_op jit(solution)/shard_map/ppermute | solution.py:338
  86.3 3.8 %collective-permute-done.15 = bf16[16,4096]{1,0:T(8,128)(2,1)S(1)} collective-permute-done((bf16[16,4096]{1,0:T(8,128)(2,1)S(1)}, bf16[16,4096]{1,0:T(8,128)(2,1)S(1)}, u32[]{:S(2)}, u32[]{:S(2)}) %collective-permute-start.15) | collective-permute-done | bytes 131104 | tf_op jit(solution)/shard_map/ppermute | solution.py:338
  90.1 1.2 collective-permute-start.18
  91.5 2.0 %collective-permute-start.16 = (bf16[16,4096]{1,0:T(8,128)(2,1)S(1)}, bf16[16,4096]{1,0:T(8,128)(2,1)S(1)}, u32[]{:S(2)}, u32[]{:S(2)}) collective-permute-start(bf16[16,4096]{1,0:T(8,128)(2,1)S(1)} %fusion.6), channel_id=1, source_target_pairs={{0,2},{1,3},{2,0},{3,1},{4,6},{5,7},{6,4},{7,5},{8,10},{9,11},{10,... | collective-permute-start | bytes 393224 | tf_op jit(solution)/shard_map/ppermute | solution.py:338
  93.7 1.9 %collective-permute-start.22 = (bf16[2,16,4096]{2,1,0:T(8,128)(2,1)S(1)}, bf16[2,16,4096]{2,1,0:T(8,128)(2,1)S(1)}, u32[]{:S(2)}, u32[]{:S(2)}) collective-permute-start(bf16[2,16,4096]{2,1,0:T(8,128)(2,1)S(1)} %add_convert_fusion.1.refs_0_), channel_id=1, source_target_pairs={{0,1},{1,0},{2,3},{3,2},{4,5},{5,4},{6,7},{7,6},{8,9},{9,8},{10,11... | collective-permute-start | bytes 786440 | tf_op jit(solution)/shard_map/ppermute | solution.py:338
  96.5 1.3 %collective-permute-start.7 = (bf16[2,16,4096]{2,1,0:T(8,128)(2,1)S(1)}, bf16[2,16,4096]{2,1,0:T(8,128)(2,1)S(1)}, u32[]{:S(2)}, u32[]{:S(2)}) collective-permute-start(bf16[2,16,4096]{2,1,0:T(8,128)(2,1)S(1)} %add_convert_fusion.1.refs_0_), channel_id=1, source_target_pairs={{0,6},{1,7},{2,4},{3,5},{4,2},{5,3},{6,0},{7,1},{8,14},{9,15},{10,... | collective-permute-start | bytes 786440 | tf_op jit(solution)/shard_map/ppermute | solution.py:338
  99.9 5.7 %collective-permute-done.9.refs_2_ = bf16[2,16,4096]{2,1,0:T(8,128)(2,1)S(1)} collective-permute-done((bf16[2,16,4096]{2,1,0:T(8,128)(2,1)S(1)}, bf16[2,16,4096]{2,1,0:T(8,128)(2,1)S(1)}, u32[]{:S(2)}, u32[]{:S(2)}) %collective-permute-start.9) | collective-permute-done | bytes 262176 | tf_op jit(solution)/shard_map/ppermute | solution.py:338
  105.5 2.9 %collective-permute-start.10 = (bf16[2,16,4096]{2,1,0:T(8,128)(2,1)S(1)}, bf16[2,16,4096]{2,1,0:T(8,128)(2,1)S(1)}, u32[]{:S(2)}, u32[]{:S(2)}) collective-permute-start(bf16[2,16,4096]{2,1,0:T(8,128)(2,1)S(1)} %collective-permute-done.9.refs_2_), channel_id=1, source_target_pairs={{0,1},{1,0},{2,3},{3,2},{4,5},{5,4},{6,7},{7,6},{8,9},{9,8},{10,11... | collective-permute-start | bytes 786440 | tf_op jit(solution)/shard_map/ppermute | solution.py:338
  108.4 1.9 %collective-permute-done.7.refs_1_ = bf16[2,16,4096]{2,1,0:T(8,128)(2,1)S(1)} collective-permute-done((bf16[2,16,4096]{2,1,0:T(8,128)(2,1)S(1)}, bf16[2,16,4096]{2,1,0:T(8,128)(2,1)S(1)}, u32[]{:S(2)}, u32[]{:S(2)}) %collective-permute-start.7) | collective-permute-done | bytes 262176 | tf_op jit(solution)/shard_map/ppermute | solution.py:338
  110.3 1.5 %collective-permute-start.8 = (bf16[2,16,4096]{2,1,0:T(8,128)(2,1)S(1)}, bf16[2,16,4096]{2,1,0:T(8,128)(2,1)S(1)}, u32[]{:S(2)}, u32[]{:S(2)}) collective-permute-start(bf16[2,16,4096]{2,1,0:T(8,128)(2,1)S(1)} %collective-permute-done.7.refs_1_), channel_id=1, source_target_pairs={{0,1},{1,0},{2,3},{3,2},{4,5},{5,4},{6,7},{7,6},{8,9},{9,8},{10,11... | collective-permute-start | bytes 786440 | tf_op jit(solution)/shard_map/ppermute | solution.py:338
  112.3 2.3 %collective-permute-start.21 = (bf16[4,16,4096]{2,1,0:T(8,128)(2,1)S(1)}, bf16[4,16,4096]{2,1,0:T(8,128)(2,1)S(1)}, u32[]{:S(2)}, u32[]{:S(2)}) collective-permute-start(bf16[4,16,4096]{2,1,0:T(8,128)(2,1)S(1)} %collective-permute-done.19.refs_1_), channel_id=1, source_target_pairs={{0,1},{1,0},{2,3},{3,2},{4,5},{5,4},{6,7},{7,6},{8,9},{9,8},{10,11... | collective-permute-start | bytes 1572872 | tf_op jit(solution)/shard_map/ppermute | solution.py:338
  116.1 1.4 %put.6.refs_3_ = bf16[256,8192]{1,0:T(8,128)(2,1)} custom-call(s32[1]{0:T(128)} %bitcast.place_ref, bf16[4,16,4096]{2,1,0:T(8,128)(2,1)S(1)} %pad_maximum_fusion.refs_0_, bf16[4,16,4096]{2,1,0:T(8,128)(2,1)S(1)} %collective-permute-done.19.refs_1_, bf16[4,16,4096]{2,1,0:T(8,128)(2,1)S(1)} %collective-permute-done.20.refs_2_, ...), custom_call_target="tpu_custom_call", output_to_operand_aliasing={{}: (5, {})} | custom-call | bytes 4194304 | tf_op jit(solution)/shard_map/put/pallas_call | solution.py:312
  (42 shorter events, 12.2 us)
Async XLA Ops:
  30.3 19.8 %all-to-all-start.1 = ((bf16[16,16,1664]{2,1,0:T(8,128)(2,1)}), bf16[16,16,1664]{2,1,0:T(8,128)(2,1)S(1)}, u32[]{:S(2)}, u32[]{:S(2)}) async-start(bf16[16,16,1664]{2,1,0:T(8,128)(2,1)} %rotate.1), calls=%async_computation.1 | async-start | bytes 1703936 | tf_op jit(solution)/shard_map/all_to_all | solution.py:348
  56.8 9.0 %collective-permute-start.11 = (bf16[8,16,4096]{2,1,0:T(8,128)(2,1)S(1)}, bf16[8,16,4096]{2,1,0:T(8,128)(2,1)S(1)}, u32[]{:S(2)}, u32[]{:S(2)}) collective-permute-start(bf16[8,16,4096]{2,1,0:T(8,128)(2,1)S(1)} %get-tuple-element.21), channel_id=1, source_target_pairs={{0,1},{1,0},{2,3},{3,2},{4,5},{5,4},{6,7},{7,6},{8,9},{9,8},{10,11... | collective-permute-start | bytes 3145736 | tf_op jit(solution)/shard_map/ppermute | solution.py:338
  65.7 2.7 %collective-permute-start = (bf16[8,16,4096]{2,1,0:T(8,128)(2,1)S(1)}, bf16[8,16,4096]{2,1,0:T(8,128)(2,1)S(1)}, u32[]{:S(2)}, u32[]{:S(2)}) collective-permute-start(bf16[8,16,4096]{2,1,0:T(8,128)(2,1)S(1)} %get-tuple-element.18), channel_id=1, source_target_pairs={{0,1},{1,0},{2,3},{3,2},{4,5},{5,4},{6,7},{7,6},{8,9},{9,8},{10,11... | collective-permute-start | bytes 3145736 | tf_op jit(solution)/shard_map/ppermute | solution.py:338
  65.9 14.6 %collective-permute-start.12 = (bf16[4,16,4096]{2,1,0:T(8,128)(2,1)S(1)}, bf16[4,16,4096]{2,1,0:T(8,128)(2,1)S(1)}, u32[]{:S(2)}, u32[]{:S(2)}) collective-permute-start(bf16[4,16,4096]{2,1,0:T(8,128)(2,1)S(1)} %add_convert_fusion), channel_id=1, source_target_pairs={{0,8},{1,9},{2,10},{3,11},{4,12},{5,13},{6,14},{7,15},{8,0},{9,1},... | collective-permute-start | bytes 1572872 | tf_op jit(solution)/shard_map/ppermute | solution.py:338
  68.6 13.7 %collective-permute-start.1 = (bf16[2,16,4096]{2,1,0:T(8,128)(2,1)S(1)}, bf16[2,16,4096]{2,1,0:T(8,128)(2,1)S(1)}, u32[]{:S(2)}, u32[]{:S(2)}) collective-permute-start(bf16[2,16,4096]{2,1,0:T(8,128)(2,1)S(1)} %get-tuple-element.29), channel_id=1, source_target_pairs={{0,4},{1,5},{2,6},{3,7},{4,0},{5,1},{6,2},{7,3},{8,12},{9,13},{10,... | collective-permute-start | bytes 786440 | tf_op jit(solution)/shard_map/ppermute | solution.py:338
  68.7 14.9 %collective-permute-start.3 = (bf16[2,16,4096]{2,1,0:T(8,128)(2,1)S(1)}, bf16[2,16,4096]{2,1,0:T(8,128)(2,1)S(1)}, u32[]{:S(2)}, u32[]{:S(2)}) collective-permute-start(bf16[2,16,4096]{2,1,0:T(8,128)(2,1)S(1)} %get-tuple-element.30), channel_id=1, source_target_pairs={{0,6},{1,7},{2,4},{3,5},{4,2},{5,3},{6,0},{7,1},{8,14},{9,15},{10,... | collective-permute-start | bytes 786440 | tf_op jit(solution)/shard_map/ppermute | solution.py:338
  69.7 14.0 %collective-permute-start.2 = (bf16[2,16,4096]{2,1,0:T(8,128)(2,1)S(1)}, bf16[2,16,4096]{2,1,0:T(8,128)(2,1)S(1)}, u32[]{:S(2)}, u32[]{:S(2)}) collective-permute-start(bf16[2,16,4096]{2,1,0:T(8,128)(2,1)S(1)} %get-tuple-element.31), channel_id=1, source_target_pairs={{0,2},{1,3},{2,0},{3,1},{4,6},{5,7},{6,4},{7,5},{8,10},{9,11},{10,... | collective-permute-start | bytes 786440 | tf_op jit(solution)/shard_map/ppermute | solution.py:338
  80.8 5.5 %collective-permute-start.13 = (bf16[16,4096]{1,0:T(8,128)(2,1)S(1)}, bf16[16,4096]{1,0:T(8,128)(2,1)S(1)}, u32[]{:S(2)}, u32[]{:S(2)}) collective-permute-start(bf16[16,4096]{1,0:T(8,128)(2,1)S(1)} %get-tuple-element.32), channel_id=1, source_target_pairs={{0,4},{1,5},{2,6},{3,7},{4,0},{5,1},{6,2},{7,3},{8,12},{9,13},{10,... | collective-permute-start | bytes 393224 | tf_op jit(solution)/shard_map/ppermute | solution.py:338
  81.7 8.4 %collective-permute-start.15 = (bf16[16,4096]{1,0:T(8,128)(2,1)S(1)}, bf16[16,4096]{1,0:T(8,128)(2,1)S(1)}, u32[]{:S(2)}, u32[]{:S(2)}) collective-permute-start(bf16[16,4096]{1,0:T(8,128)(2,1)S(1)} %get-tuple-element.33), channel_id=1, source_target_pairs={{0,6},{1,7},{2,4},{3,5},{4,2},{5,3},{6,0},{7,1},{8,14},{9,15},{10,... | collective-permute-start | bytes 393224 | tf_op jit(solution)/shard_map/ppermute | solution.py:338
  82.4 7.7 %collective-permute-start.14 = (bf16[16,4096]{1,0:T(8,128)(2,1)S(1)}, bf16[16,4096]{1,0:T(8,128)(2,1)S(1)}, u32[]{:S(2)}, u32[]{:S(2)}) collective-permute-start(bf16[16,4096]{1,0:T(8,128)(2,1)S(1)} %get-tuple-element.34), channel_id=1, source_target_pairs={{0,2},{1,3},{2,0},{3,1},{4,6},{5,7},{6,4},{7,5},{8,10},{9,11},{10,... | collective-permute-start | bytes 393224 | tf_op jit(solution)/shard_map/ppermute | solution.py:338
  83.8 9.6 %collective-permute-start.4 = (bf16[2,16,4096]{2,1,0:T(8,128)(2,1)S(1)}, bf16[2,16,4096]{2,1,0:T(8,128)(2,1)S(1)}, u32[]{:S(2)}, u32[]{:S(2)}) collective-permute-start(bf16[2,16,4096]{2,1,0:T(8,128)(2,1)S(1)} %fusion.7), channel_id=1, source_target_pairs={{0,8},{1,9},{2,10},{3,11},{4,12},{5,13},{6,14},{7,15},{8,0},{9,1},... | collective-permute-start | bytes 786440 | tf_op jit(solution)/shard_map/ppermute | solution.py:338
  90.1 6.4 %collective-permute-start.18 = (bf16[16,4096]{1,0:T(8,128)(2,1)S(1)}, bf16[16,4096]{1,0:T(8,128)(2,1)S(1)}, u32[]{:S(2)}, u32[]{:S(2)}) collective-permute-start(bf16[16,4096]{1,0:T(8,128)(2,1)S(1)} %fusion.6), channel_id=1, source_target_pairs={{0,6},{1,7},{2,4},{3,5},{4,2},{5,3},{6,0},{7,1},{8,14},{9,15},{10,... | collective-permute-start | bytes 393224 | tf_op jit(solution)/shard_map/ppermute | solution.py:338
  91.3 6.4 %collective-permute-start.17 = (bf16[16,4096]{1,0:T(8,128)(2,1)S(1)}, bf16[16,4096]{1,0:T(8,128)(2,1)S(1)}, u32[]{:S(2)}, u32[]{:S(2)}) collective-permute-start(bf16[16,4096]{1,0:T(8,128)(2,1)S(1)} %fusion.6), channel_id=1, source_target_pairs={{0,4},{1,5},{2,6},{3,7},{4,0},{5,1},{6,2},{7,3},{8,12},{9,13},{10,... | collective-permute-start | bytes 393224 | tf_op jit(solution)/shard_map/ppermute | solution.py:338
  91.5 7.1 %collective-permute-start.16 = (bf16[16,4096]{1,0:T(8,128)(2,1)S(1)}, bf16[16,4096]{1,0:T(8,128)(2,1)S(1)}, u32[]{:S(2)}, u32[]{:S(2)}) collective-permute-start(bf16[16,4096]{1,0:T(8,128)(2,1)S(1)} %fusion.6), channel_id=1, source_target_pairs={{0,2},{1,3},{2,0},{3,1},{4,6},{5,7},{6,4},{7,5},{8,10},{9,11},{10,... | collective-permute-start | bytes 393224 | tf_op jit(solution)/shard_map/ppermute | solution.py:338
  93.7 18.3 %collective-permute-start.22 = (bf16[2,16,4096]{2,1,0:T(8,128)(2,1)S(1)}, bf16[2,16,4096]{2,1,0:T(8,128)(2,1)S(1)}, u32[]{:S(2)}, u32[]{:S(2)}) collective-permute-start(bf16[2,16,4096]{2,1,0:T(8,128)(2,1)S(1)} %add_convert_fusion.1.refs_0_), channel_id=1, source_target_pairs={{0,1},{1,0},{2,3},{3,2},{4,5},{5,4},{6,7},{7,6},{8,9},{9,8},{10,11... | collective-permute-start | bytes 786440 | tf_op jit(solution)/shard_map/ppermute | solution.py:338
  95.6 9.9 %collective-permute-start.9 = (bf16[2,16,4096]{2,1,0:T(8,128)(2,1)S(1)}, bf16[2,16,4096]{2,1,0:T(8,128)(2,1)S(1)}, u32[]{:S(2)}, u32[]{:S(2)}) collective-permute-start(bf16[2,16,4096]{2,1,0:T(8,128)(2,1)S(1)} %add_convert_fusion.1.refs_0_), channel_id=1, source_target_pairs={{0,4},{1,5},{2,6},{3,7},{4,0},{5,1},{6,2},{7,3},{8,12},{9,13},{10,... | collective-permute-start | bytes 786440 | tf_op jit(solution)/shard_map/ppermute | solution.py:338
  96.5 13.8 %collective-permute-start.7 = (bf16[2,16,4096]{2,1,0:T(8,128)(2,1)S(1)}, bf16[2,16,4096]{2,1,0:T(8,128)(2,1)S(1)}, u32[]{:S(2)}, u32[]{:S(2)}) collective-permute-start(bf16[2,16,4096]{2,1,0:T(8,128)(2,1)S(1)} %add_convert_fusion.1.refs_0_), channel_id=1, source_target_pairs={{0,6},{1,7},{2,4},{3,5},{4,2},{5,3},{6,0},{7,1},{8,14},{9,15},{10,... | collective-permute-start | bytes 786440 | tf_op jit(solution)/shard_map/ppermute | solution.py:338
  97.8 14.0 %collective-permute-start.5 = (bf16[2,16,4096]{2,1,0:T(8,128)(2,1)S(1)}, bf16[2,16,4096]{2,1,0:T(8,128)(2,1)S(1)}, u32[]{:S(2)}, u32[]{:S(2)}) collective-permute-start(bf16[2,16,4096]{2,1,0:T(8,128)(2,1)S(1)} %add_convert_fusion.1.refs_0_), channel_id=1, source_target_pairs={{0,2},{1,3},{2,0},{3,1},{4,6},{5,7},{6,4},{7,5},{8,10},{9,11},{10,... | collective-permute-start | bytes 786440 | tf_op jit(solution)/shard_map/ppermute | solution.py:338
  98.7 13.6 %collective-permute-start.19 = (bf16[4,16,4096]{2,1,0:T(8,128)(2,1)S(1)}, bf16[4,16,4096]{2,1,0:T(8,128)(2,1)S(1)}, u32[]{:S(2)}, u32[]{:S(2)}) collective-permute-start(bf16[4,16,4096]{2,1,0:T(8,128)(2,1)S(1)} %pad_maximum_fusion.refs_0_), channel_id=1, source_target_pairs={{0,8},{1,9},{2,10},{3,11},{4,12},{5,13},{6,14},{7,15},{8,0},{9,1},... | collective-permute-start | bytes 1572872 | tf_op jit(solution)/shard_map/ppermute | solution.py:338
  105.5 12.1 %collective-permute-start.10 = (bf16[2,16,4096]{2,1,0:T(8,128)(2,1)S(1)}, bf16[2,16,4096]{2,1,0:T(8,128)(2,1)S(1)}, u32[]{:S(2)}, u32[]{:S(2)}) collective-permute-start(bf16[2,16,4096]{2,1,0:T(8,128)(2,1)S(1)} %collective-permute-done.9.refs_2_), channel_id=1, source_target_pairs={{0,1},{1,0},{2,3},{3,2},{4,5},{5,4},{6,7},{7,6},{8,9},{9,8},{10,11... | collective-permute-start | bytes 786440 | tf_op jit(solution)/shard_map/ppermute | solution.py:338
  110.3 7.3 %collective-permute-start.8 = (bf16[2,16,4096]{2,1,0:T(8,128)(2,1)S(1)}, bf16[2,16,4096]{2,1,0:T(8,128)(2,1)S(1)}, u32[]{:S(2)}, u32[]{:S(2)}) collective-permute-start(bf16[2,16,4096]{2,1,0:T(8,128)(2,1)S(1)} %collective-permute-done.7.refs_1_), channel_id=1, source_target_pairs={{0,1},{1,0},{2,3},{3,2},{4,5},{5,4},{6,7},{7,6},{8,9},{9,8},{10,11... | collective-permute-start | bytes 786440 | tf_op jit(solution)/shard_map/ppermute | solution.py:338
  111.8 5.8 %collective-permute-start.6 = (bf16[2,16,4096]{2,1,0:T(8,128)(2,1)S(1)}, bf16[2,16,4096]{2,1,0:T(8,128)(2,1)S(1)}, u32[]{:S(2)}, u32[]{:S(2)}) collective-permute-start(bf16[2,16,4096]{2,1,0:T(8,128)(2,1)S(1)} %collective-permute-done.5.refs_0_), channel_id=1, source_target_pairs={{0,1},{1,0},{2,3},{3,2},{4,5},{5,4},{6,7},{7,6},{8,9},{9,8},{10,11... | collective-permute-start | bytes 786440 | tf_op jit(solution)/shard_map/ppermute | solution.py:338
  112.0 3.6 %collective-permute-start.20 = (bf16[4,16,4096]{2,1,0:T(8,128)(2,1)S(1)}, bf16[4,16,4096]{2,1,0:T(8,128)(2,1)S(1)}, u32[]{:S(2)}, u32[]{:S(2)}) collective-permute-start(bf16[4,16,4096]{2,1,0:T(8,128)(2,1)S(1)} %pad_maximum_fusion.refs_0_), channel_id=1, source_target_pairs={{0,1},{1,0},{2,3},{3,2},{4,5},{5,4},{6,7},{7,6},{8,9},{9,8},{10,11... | collective-permute-start | bytes 1572872 | tf_op jit(solution)/shard_map/ppermute | solution.py:338
  112.3 3.8 %collective-permute-start.21 = (bf16[4,16,4096]{2,1,0:T(8,128)(2,1)S(1)}, bf16[4,16,4096]{2,1,0:T(8,128)(2,1)S(1)}, u32[]{:S(2)}, u32[]{:S(2)}) collective-permute-start(bf16[4,16,4096]{2,1,0:T(8,128)(2,1)S(1)} %collective-permute-done.19.refs_1_), channel_id=1, source_target_pairs={{0,1},{1,0},{2,3},{3,2},{4,5},{5,4},{6,7},{7,6},{8,9},{9,8},{10,11... | collective-permute-start | bytes 1572872 | tf_op jit(solution)/shard_map/ppermute | solution.py:338

commit v6 on v5

--- a/solution.py
+++ b/solution.py
@@ -389,13 +389,43 @@
     def across(names):
         return [tuple(q | CORE for q in blocks) for blocks in names]
 
-    def lay(into, pieces, names, first, weight):
-        return put(place, pieces, names, [first] * len(pieces), (total_rows, width), into, weight)
-
-    out = lay(None, all_p[:1], names_p[:1], 0, 20000000000)
-    out = lay(out, all_p[1:] + far_p[:1], names_p[1:] + across(names_p[:1]), 0, 20000000000)
-    out = lay(out, all_q + far_q, names_q + across(names_q), left, 0)
-    return lay(out, far_p[1:], across(names_p[1:]), 0, 0)
+    out = put(
+        place,
+        all_p[:1],
+        names_p[:1],
+        [0] * len(all_p[:1]),
+        (total_rows, width),
+        None,
+        20000000000,
+    )
+    out = put(
+        place,
+        all_p[1:] + far_p[:1],
+        names_p[1:] + across(names_p[:1]),
+        [0] * len(all_p[1:]) + [0] * len(far_p[:1]),
+        (total_rows, width),
+        out,
+        20000000000,
+    )
+    out = put(
+        place,
+        far_p[1:] + all_q[:1] + far_q[:1],
+        across(names_p[1:]) + names_q[:1] + across(names_q[:1]),
+        [0] * len(far_p[1:]) + [left] * len(all_q[:1]) + [left] * len(far_q[:1]),
+        (total_rows, width),
+        out,
+        0,
+    )
+    out = put(
+        place,
+        all_q[1:] + far_q[1:],
+        names_q[1:] + across(names_q[1:]),
+        [left] * len(all_q[1:]) + [left] * len(far_q[1:]),
+        (total_rows, width),
+        out,
+        0,
+    )
+    return out
 
 
 def solution(mesh):

time: 119 us -> 118 us (level)
  waiting for transfers between devices: 30.5 us -> 29.2 us
    ppermute x23, waiting for transfers between devices: 25.1 us -> 23.9 us  [swap(): return lax.ppermute(x, 'tensor', [(i, i ^ mask) for i in range(shards)])]
  transfers between devices with their start and end apart: 24 -> 24, of which waited for: 10 -> 9; matrix products, arithmetic and copies ran while one was open for 1% -> 1% of each run, Pallas kernels for 18% -> 18%
where the time goes in v6:
time: 118 us
  Pallas kernels  34.3 us (29%)
  waiting for transfers between devices  29.2 us (25%)
  starting transfers between devices  28.4 us (24%)
  blocking collectives  23 us (19%)
  other arithmetic  2.96 us (3%)
    ppermute x23, starting transfers between devices, swap(): return lax.ppermute(x, 'tensor', [(i, i ^ mask) for i in range(shards)])  24 us
    ppermute x23, waiting for transfers between devices, swap(): return lax.ppermute(x, 'tensor', [(i, i ^ mask) for i in range(shards)])  23.9 us
    all_to_all x1, blocking collectives, local(): lax.all_to_all(hidden.reshape(shards, rows, local_ff), 'tensor', 0, 0)  23 us
    pallas_call x1, Pallas kernels, dequant(): pl.pallas_call(dequant_body, grid=(tiles,), in_specs=[pl.BlockSpec((low.s...  10 us
    pallas_call x1, Pallas kernels, project(): pl.pallas_call(functools.partial(project_body, full), grid_spec=pltpu.Pre...  8.11 us
    pallas_call x1, Pallas kernels, project_unpacked(): pl.pallas_call(functools.partial(stream_body, full), grid_spec=pltpu.Pref...  6.71 us
    pallas_call x1, Pallas kernels, rotate(): pl.pallas_call(rotate_body, in_specs=[pl.BlockSpec(memory_space=pltpu.VME...  5.34 us
    all_to_all x1, waiting for transfers between devices, local(): rot = lax.all_to_all(turned, 'tensor', 0, 0)  5.33 us
  transfers between devices with their start and end apart: 24, of which 9 were waited for; matrix products, arithmetic and copies ran while one was open for 1% of the time, Pallas kernels for 18%

profile of v6, /device:TPU:1, one launch (start us, length us, event | category | flops | bytes accessed | tf_op | source)
XLA Modules:
  0.0 118.1 jit_solution(15011063246197971129)
XLA Ops:
  0.0 1.9 %fusion.4 = bf16[256,1664]{1,0:T(8,128)(2,1)S(1)} fusion(bf16[256,1664]{1,0:T(8,128)(2,1)} %param.7, bf16[256,1664]{1,0:T(8,128)(2,1)} %param.6), kind=kLoop, calls=%fused_computation.6 | loop fusion | flops 3407872 | bytes 2555904 | tf_op jit(solution)/shard_map/convert_element_type | solution.py:345
  1.9 23.0 %all_to_all.10.hidden_ref = bf16[16,16,1664]{2,1,0:T(8,128)(2,1)S(1)} all-to-all(bf16[16,16,1664]{2,1,0:T(8,128)(2,1)S(1)} %bitcast.18), channel_id=1, replica_groups=mesh['dp'=8,'tensor'=16] {'tensor'}, dimensions={0} | all-to-all | bytes 1703936 | tf_op jit(solution)/shard_map/all_to_all | solution.py:346
  24.9 5.3 %rotate.1 = bf16[16,16,1664]{2,1,0:T(8,128)(2,1)} custom-call(bf16[16,16,1664]{2,1,0:T(8,128)(2,1)S(1)} %all_to_all.10.hidden_ref, bf16[4,1664,512]{2,1,0:T(8,128)(2,1)} %constant.9.clone.table_ref), custom_call_target="tpu_custom_call" | custom-call | flops 1417674752 | bytes 7241728 | tf_op jit(solution)/shard_map/rotate/pallas_call | solution.py:84
  30.3 4.4 %all-to-all-start.1 = ((bf16[16,16,1664]{2,1,0:T(8,128)(2,1)}), bf16[16,16,1664]{2,1,0:T(8,128)(2,1)S(1)}, u32[]{:S(2)}, u32[]{:S(2)}) async-start(bf16[16,16,1664]{2,1,0:T(8,128)(2,1)} %rotate.1), calls=%async_computation.1 | async-start | bytes 1703936 | tf_op jit(solution)/shard_map/all_to_all | solution.py:348
  34.7 10.0 %dequant.1.weight_ref = bf16[4,1664,1024]{2,1,0:T(8,128)(2,1)} custom-call(s32[208,8192]{1,0:T(8,128)} %low_ref.3, s32[208,8192]{1,0:T(8,128)} %high_ref.3, bf16[13,8192]{1,0:T(8,128)(2,1)} %scale_ref.3), custom_call_target="tpu_custom_call" | custom-call | flops 54525952 | bytes 20447232 | tf_op jit(solution)/shard_map/dequant/pallas_call | solution.py:205
  44.7 5.3 %all-to-all-done.1.rot_ref = bf16[16,16,1664]{2,1,0:T(8,128)(2,1)S(1)} async-done(((bf16[16,16,1664]{2,1,0:T(8,128)(2,1)}), bf16[16,16,1664]{2,1,0:T(8,128)(2,1)S(1)}, u32[]{:S(2)}, u32[]{:S(2)}) %all-to-all-start.1) | async-done | bytes 852000 | tf_op jit(solution)/shard_map/all_to_all | solution.py:348
  50.1 6.7 %project_unpacked.1 = (bf16[8,16,4096]{2,1,0:T(8,128)(2,1)S(1)}, bf16[8,16,4096]{2,1,0:T(8,128)(2,1)S(1)}) custom-call(s32[1]{0:T(128)} %bitcast.place_ref, bf16[16,16,1664]{2,1,0:T(8,128)(2,1)S(1)} %all-to-all-done.1.rot_ref, bf16[4,1664,1024]{2,1,0:T(8,128)(2,1)} %dequant.1.weight_ref), custom_call_target="tpu_custom_call" | custom-call | flops 3489660928 | bytes 17825792 | tf_op jit(solution)/shard_map/project_unpacked/pallas_call | solution.py:263
  57.6 8.1 %project.1 = (bf16[8,16,4096]{2,1,0:T(8,128)(2,1)S(1)}, bf16[8,16,4096]{2,1,0:T(8,128)(2,1)S(1)}) custom-call(s32[1]{0:T(128)} %bitcast.place_ref, bf16[16,16,1664]{2,1,0:T(8,128)(2,1)S(1)} %all-to-all-done.1.rot_ref, s32[208,8192]{1,0:T(8,128)} %low_ref.3, s32[208,8192]{1,0:T(8,128)} %high_ref.3, bf16[13,8192]{1,0:T(8,128)(2,1)} %scale_ref.3), custom_call_target="tpu_custom_call" | custom-call | flops 3489660928 | bytes 11010048 | tf_op jit(solution)/shard_map/project/pallas_call | solution.py:145
  66.2 2.2 %collective-permute-done.2 = bf16[8,16,4096]{2,1,0:T(8,128)(2,1)S(1)} collective-permute-done((bf16[8,16,4096]{2,1,0:T(8,128)(2,1)S(1)}, bf16[8,16,4096]{2,1,0:T(8,128)(2,1)S(1)}, u32[]{:S(2)}, u32[]{:S(2)}) %collective-permute-start.2) | collective-permute-done | bytes 1048608 | tf_op jit(solution)/shard_map/ppermute | solution.py:338
  68.8 3.8 %collective-permute-start.9 = (bf16[2,16,4096]{2,1,0:T(8,128)(2,1)S(1)}, bf16[2,16,4096]{2,1,0:T(8,128)(2,1)S(1)}, u32[]{:S(2)}, u32[]{:S(2)}) collective-permute-start(bf16[2,16,4096]{2,1,0:T(8,128)(2,1)S(1)} %get-tuple-element.31), channel_id=1, source_target_pairs={{0,4},{1,5},{2,6},{3,7},{4,0},{5,1},{6,2},{7,3},{8,12},{9,13},{10,... | collective-permute-start | bytes 786440 | tf_op jit(solution)/shard_map/ppermute | solution.py:338
  72.6 8.0 %collective-permute-done.1 = bf16[4,16,4096]{2,1,0:T(8,128)(2,1)S(1)} collective-permute-done((bf16[4,16,4096]{2,1,0:T(8,128)(2,1)S(1)}, bf16[4,16,4096]{2,1,0:T(8,128)(2,1)S(1)}, u32[]{:S(2)}, u32[]{:S(2)}) %collective-permute-start.1) | collective-permute-done | bytes 524320 | tf_op jit(solution)/shard_map/ppermute | solution.py:338
  82.4 1.1 collective-permute-start.4
  84.4 1.8 %collective-permute-done.3 = bf16[16,4096]{1,0:T(8,128)(2,1)S(1)} collective-permute-done((bf16[16,4096]{1,0:T(8,128)(2,1)S(1)}, bf16[16,4096]{1,0:T(8,128)(2,1)S(1)}, u32[]{:S(2)}, u32[]{:S(2)}) %collective-permute-start.3) | collective-permute-done | bytes 131104 | tf_op jit(solution)/shard_map/ppermute | solution.py:338
  86.3 3.8 %collective-permute-done.5 = bf16[16,4096]{1,0:T(8,128)(2,1)S(1)} collective-permute-done((bf16[16,4096]{1,0:T(8,128)(2,1)S(1)}, bf16[16,4096]{1,0:T(8,128)(2,1)S(1)}, u32[]{:S(2)}, u32[]{:S(2)}) %collective-permute-start.5) | collective-permute-done | bytes 131104 | tf_op jit(solution)/shard_map/ppermute | solution.py:338
  90.1 1.2 %collective-permute-start.8 = (bf16[16,4096]{1,0:T(8,128)(2,1)S(1)}, bf16[16,4096]{1,0:T(8,128)(2,1)S(1)}, u32[]{:S(2)}, u32[]{:S(2)}) collective-permute-start(bf16[16,4096]{1,0:T(8,128)(2,1)S(1)} %fusion.6), channel_id=1, source_target_pairs={{0,6},{1,7},{2,4},{3,5},{4,2},{5,3},{6,0},{7,1},{8,14},{9,15},{10,... | collective-permute-start | bytes 393224 | tf_op jit(solution)/shard_map/ppermute | solution.py:338
  91.8 1.7 %collective-permute-start.6 = (bf16[16,4096]{1,0:T(8,128)(2,1)S(1)}, bf16[16,4096]{1,0:T(8,128)(2,1)S(1)}, u32[]{:S(2)}, u32[]{:S(2)}) collective-permute-start(bf16[16,4096]{1,0:T(8,128)(2,1)S(1)} %fusion.6), channel_id=1, source_target_pairs={{0,2},{1,3},{2,0},{3,1},{4,6},{5,7},{6,4},{7,5},{8,10},{9,11},{10,... | collective-permute-start | bytes 393224 | tf_op jit(solution)/shard_map/ppermute | solution.py:338
  93.7 1.9 %collective-permute-start.22 = (bf16[2,16,4096]{2,1,0:T(8,128)(2,1)S(1)}, bf16[2,16,4096]{2,1,0:T(8,128)(2,1)S(1)}, u32[]{:S(2)}, u32[]{:S(2)}) collective-permute-start(bf16[2,16,4096]{2,1,0:T(8,128)(2,1)S(1)} %add_convert_fusion.1.refs_0_), channel_id=1, source_target_pairs={{0,1},{1,0},{2,3},{3,2},{4,5},{5,4},{6,7},{7,6},{8,9},{9,8},{10,11... | collective-permute-start | bytes 786440 | tf_op jit(solution)/shard_map/ppermute | solution.py:338
  96.5 1.3 %collective-permute-start.17 = (bf16[2,16,4096]{2,1,0:T(8,128)(2,1)S(1)}, bf16[2,16,4096]{2,1,0:T(8,128)(2,1)S(1)}, u32[]{:S(2)}, u32[]{:S(2)}) collective-permute-start(bf16[2,16,4096]{2,1,0:T(8,128)(2,1)S(1)} %add_convert_fusion.1.refs_0_), channel_id=1, source_target_pairs={{0,6},{1,7},{2,4},{3,5},{4,2},{5,3},{6,0},{7,1},{8,14},{9,15},{10,... | collective-permute-start | bytes 786440 | tf_op jit(solution)/shard_map/ppermute | solution.py:338
  100.3 5.2 %collective-permute-done.19.refs_2_ = bf16[2,16,4096]{2,1,0:T(8,128)(2,1)S(1)} collective-permute-done((bf16[2,16,4096]{2,1,0:T(8,128)(2,1)S(1)}, bf16[2,16,4096]{2,1,0:T(8,128)(2,1)S(1)}, u32[]{:S(2)}, u32[]{:S(2)}) %collective-permute-start.19) | collective-permute-done | bytes 262176 | tf_op jit(solution)/shard_map/ppermute | solution.py:338
  105.5 2.9 %collective-permute-start.20 = (bf16[2,16,4096]{2,1,0:T(8,128)(2,1)S(1)}, bf16[2,16,4096]{2,1,0:T(8,128)(2,1)S(1)}, u32[]{:S(2)}, u32[]{:S(2)}) collective-permute-start(bf16[2,16,4096]{2,1,0:T(8,128)(2,1)S(1)} %collective-permute-done.19.refs_2_), channel_id=1, source_target_pairs={{0,1},{1,0},{2,3},{3,2},{4,5},{5,4},{6,7},{7,6},{8,9},{9,8},{10,11... | collective-permute-start | bytes 786440 | tf_op jit(solution)/shard_map/ppermute | solution.py:338
  108.4 1.9 %collective-permute-done.17.refs_1_ = bf16[2,16,4096]{2,1,0:T(8,128)(2,1)S(1)} collective-permute-done((bf16[2,16,4096]{2,1,0:T(8,128)(2,1)S(1)}, bf16[2,16,4096]{2,1,0:T(8,128)(2,1)S(1)}, u32[]{:S(2)}, u32[]{:S(2)}) %collective-permute-start.17) | collective-permute-done | bytes 262176 | tf_op jit(solution)/shard_map/ppermute | solution.py:338
  110.3 1.5 %collective-permute-start.18 = (bf16[2,16,4096]{2,1,0:T(8,128)(2,1)S(1)}, bf16[2,16,4096]{2,1,0:T(8,128)(2,1)S(1)}, u32[]{:S(2)}, u32[]{:S(2)}) collective-permute-start(bf16[2,16,4096]{2,1,0:T(8,128)(2,1)S(1)} %collective-permute-done.17.refs_1_), channel_id=1, source_target_pairs={{0,1},{1,0},{2,3},{3,2},{4,5},{5,4},{6,7},{7,6},{8,9},{9,8},{10,11... | collective-permute-start | bytes 786440 | tf_op jit(solution)/shard_map/ppermute | solution.py:338
  112.3 2.3 %collective-permute-start.14 = (bf16[4,16,4096]{2,1,0:T(8,128)(2,1)S(1)}, bf16[4,16,4096]{2,1,0:T(8,128)(2,1)S(1)}, u32[]{:S(2)}, u32[]{:S(2)}) collective-permute-start(bf16[4,16,4096]{2,1,0:T(8,128)(2,1)S(1)} %collective-permute-done.13.refs_0_), channel_id=1, source_target_pairs={{0,1},{1,0},{2,3},{3,2},{4,5},{5,4},{6,7},{7,6},{8,9},{9,8},{10,11... | collective-permute-start | bytes 1572872 | tf_op jit(solution)/shard_map/ppermute | solution.py:338
  115.7 1.3 %put.6.refs_2_ = bf16[256,8192]{1,0:T(8,128)(2,1)} custom-call(s32[1]{0:T(128)} %bitcast.place_ref, bf16[2,16,4096]{2,1,0:T(8,128)(2,1)S(1)} %collective-permute-done.16.refs_0_, bf16[2,16,4096]{2,1,0:T(8,128)(2,1)S(1)} %collective-permute-done.18.refs_1_, bf16[2,16,4096]{2,1,0:T(8,128)(2,1)S(1)} %collective-permute-done.20.refs_2_, ...), custom_call_target="tpu_custom_call", output_to_operand_aliasing={{}: (6, {})} | custom-call | bytes 3670016 | tf_op jit(solution)/shard_map/put/pallas_call | solution.py:312
  (42 shorter events, 11.3 us)
Async XLA Ops:
  30.3 19.8 %all-to-all-start.1 = ((bf16[16,16,1664]{2,1,0:T(8,128)(2,1)}), bf16[16,16,1664]{2,1,0:T(8,128)(2,1)S(1)}, u32[]{:S(2)}, u32[]{:S(2)}) async-start(bf16[16,16,1664]{2,1,0:T(8,128)(2,1)} %rotate.1), calls=%async_computation.1 | async-start | bytes 1703936 | tf_op jit(solution)/shard_map/all_to_all | solution.py:348
  56.8 9.0 %collective-permute-start = (bf16[8,16,4096]{2,1,0:T(8,128)(2,1)S(1)}, bf16[8,16,4096]{2,1,0:T(8,128)(2,1)S(1)}, u32[]{:S(2)}, u32[]{:S(2)}) collective-permute-start(bf16[8,16,4096]{2,1,0:T(8,128)(2,1)S(1)} %get-tuple-element.19), channel_id=1, source_target_pairs={{0,1},{1,0},{2,3},{3,2},{4,5},{5,4},{6,7},{7,6},{8,9},{9,8},{10,11... | collective-permute-start | bytes 3145736 | tf_op jit(solution)/shard_map/ppermute | solution.py:338
  65.7 2.7 %collective-permute-start.2 = (bf16[8,16,4096]{2,1,0:T(8,128)(2,1)S(1)}, bf16[8,16,4096]{2,1,0:T(8,128)(2,1)S(1)}, u32[]{:S(2)}, u32[]{:S(2)}) collective-permute-start(bf16[8,16,4096]{2,1,0:T(8,128)(2,1)S(1)} %get-tuple-element.21), channel_id=1, source_target_pairs={{0,1},{1,0},{2,3},{3,2},{4,5},{5,4},{6,7},{7,6},{8,9},{9,8},{10,11... | collective-permute-start | bytes 3145736 | tf_op jit(solution)/shard_map/ppermute | solution.py:338
  65.9 14.6 %collective-permute-start.1 = (bf16[4,16,4096]{2,1,0:T(8,128)(2,1)S(1)}, bf16[4,16,4096]{2,1,0:T(8,128)(2,1)S(1)}, u32[]{:S(2)}, u32[]{:S(2)}) collective-permute-start(bf16[4,16,4096]{2,1,0:T(8,128)(2,1)S(1)} %add_convert_fusion), channel_id=1, source_target_pairs={{0,8},{1,9},{2,10},{3,11},{4,12},{5,13},{6,14},{7,15},{8,0},{9,1},... | collective-permute-start | bytes 1572872 | tf_op jit(solution)/shard_map/ppermute | solution.py:338
  68.6 13.7 %collective-permute-start.11 = (bf16[2,16,4096]{2,1,0:T(8,128)(2,1)S(1)}, bf16[2,16,4096]{2,1,0:T(8,128)(2,1)S(1)}, u32[]{:S(2)}, u32[]{:S(2)}) collective-permute-start(bf16[2,16,4096]{2,1,0:T(8,128)(2,1)S(1)} %get-tuple-element.29), channel_id=1, source_target_pairs={{0,6},{1,7},{2,4},{3,5},{4,2},{5,3},{6,0},{7,1},{8,14},{9,15},{10,... | collective-permute-start | bytes 786440 | tf_op jit(solution)/shard_map/ppermute | solution.py:338
  68.7 14.8 %collective-permute-start.10 = (bf16[2,16,4096]{2,1,0:T(8,128)(2,1)S(1)}, bf16[2,16,4096]{2,1,0:T(8,128)(2,1)S(1)}, u32[]{:S(2)}, u32[]{:S(2)}) collective-permute-start(bf16[2,16,4096]{2,1,0:T(8,128)(2,1)S(1)} %get-tuple-element.30), channel_id=1, source_target_pairs={{0,2},{1,3},{2,0},{3,1},{4,6},{5,7},{6,4},{7,5},{8,10},{9,11},{10,... | collective-permute-start | bytes 786440 | tf_op jit(solution)/shard_map/ppermute | solution.py:338
  68.8 15.4 %collective-permute-start.9 = (bf16[2,16,4096]{2,1,0:T(8,128)(2,1)S(1)}, bf16[2,16,4096]{2,1,0:T(8,128)(2,1)S(1)}, u32[]{:S(2)}, u32[]{:S(2)}) collective-permute-start(bf16[2,16,4096]{2,1,0:T(8,128)(2,1)S(1)} %get-tuple-element.31), channel_id=1, source_target_pairs={{0,4},{1,5},{2,6},{3,7},{4,0},{5,1},{6,2},{7,3},{8,12},{9,13},{10,... | collective-permute-start | bytes 786440 | tf_op jit(solution)/shard_map/ppermute | solution.py:338
  80.8 5.5 %collective-permute-start.3 = (bf16[16,4096]{1,0:T(8,128)(2,1)S(1)}, bf16[16,4096]{1,0:T(8,128)(2,1)S(1)}, u32[]{:S(2)}, u32[]{:S(2)}) collective-permute-start(bf16[16,4096]{1,0:T(8,128)(2,1)S(1)} %get-tuple-element.32), channel_id=1, source_target_pairs={{0,4},{1,5},{2,6},{3,7},{4,0},{5,1},{6,2},{7,3},{8,12},{9,13},{10,... | collective-permute-start | bytes 393224 | tf_op jit(solution)/shard_map/ppermute | solution.py:338
  81.7 8.4 %collective-permute-start.5 = (bf16[16,4096]{1,0:T(8,128)(2,1)S(1)}, bf16[16,4096]{1,0:T(8,128)(2,1)S(1)}, u32[]{:S(2)}, u32[]{:S(2)}) collective-permute-start(bf16[16,4096]{1,0:T(8,128)(2,1)S(1)} %get-tuple-element.33), channel_id=1, source_target_pairs={{0,6},{1,7},{2,4},{3,5},{4,2},{5,3},{6,0},{7,1},{8,14},{9,15},{10,... | collective-permute-start | bytes 393224 | tf_op jit(solution)/shard_map/ppermute | solution.py:338
  82.4 7.7 %collective-permute-start.4 = (bf16[16,4096]{1,0:T(8,128)(2,1)S(1)}, bf16[16,4096]{1,0:T(8,128)(2,1)S(1)}, u32[]{:S(2)}, u32[]{:S(2)}) collective-permute-start(bf16[16,4096]{1,0:T(8,128)(2,1)S(1)} %get-tuple-element.34), channel_id=1, source_target_pairs={{0,2},{1,3},{2,0},{3,1},{4,6},{5,7},{6,4},{7,5},{8,10},{9,11},{10,... | collective-permute-start | bytes 393224 | tf_op jit(solution)/shard_map/ppermute | solution.py:338
  84.3 9.1 %collective-permute-start.12 = (bf16[2,16,4096]{2,1,0:T(8,128)(2,1)S(1)}, bf16[2,16,4096]{2,1,0:T(8,128)(2,1)S(1)}, u32[]{:S(2)}, u32[]{:S(2)}) collective-permute-start(bf16[2,16,4096]{2,1,0:T(8,128)(2,1)S(1)} %fusion.7), channel_id=1, source_target_pairs={{0,8},{1,9},{2,10},{3,11},{4,12},{5,13},{6,14},{7,15},{8,0},{9,1},... | collective-permute-start | bytes 786440 | tf_op jit(solution)/shard_map/ppermute | solution.py:338
  90.1 6.4 %collective-permute-start.8 = (bf16[16,4096]{1,0:T(8,128)(2,1)S(1)}, bf16[16,4096]{1,0:T(8,128)(2,1)S(1)}, u32[]{:S(2)}, u32[]{:S(2)}) collective-permute-start(bf16[16,4096]{1,0:T(8,128)(2,1)S(1)} %fusion.6), channel_id=1, source_target_pairs={{0,6},{1,7},{2,4},{3,5},{4,2},{5,3},{6,0},{7,1},{8,14},{9,15},{10,... | collective-permute-start | bytes 393224 | tf_op jit(solution)/shard_map/ppermute | solution.py:338
  91.3 6.4 %collective-permute-start.7 = (bf16[16,4096]{1,0:T(8,128)(2,1)S(1)}, bf16[16,4096]{1,0:T(8,128)(2,1)S(1)}, u32[]{:S(2)}, u32[]{:S(2)}) collective-permute-start(bf16[16,4096]{1,0:T(8,128)(2,1)S(1)} %fusion.6), channel_id=1, source_target_pairs={{0,4},{1,5},{2,6},{3,7},{4,0},{5,1},{6,2},{7,3},{8,12},{9,13},{10,... | collective-permute-start | bytes 393224 | tf_op jit(solution)/shard_map/ppermute | solution.py:338
  91.8 6.8 %collective-permute-start.6 = (bf16[16,4096]{1,0:T(8,128)(2,1)S(1)}, bf16[16,4096]{1,0:T(8,128)(2,1)S(1)}, u32[]{:S(2)}, u32[]{:S(2)}) collective-permute-start(bf16[16,4096]{1,0:T(8,128)(2,1)S(1)} %fusion.6), channel_id=1, source_target_pairs={{0,2},{1,3},{2,0},{3,1},{4,6},{5,7},{6,4},{7,5},{8,10},{9,11},{10,... | collective-permute-start | bytes 393224 | tf_op jit(solution)/shard_map/ppermute | solution.py:338
  93.7 18.3 %collective-permute-start.22 = (bf16[2,16,4096]{2,1,0:T(8,128)(2,1)S(1)}, bf16[2,16,4096]{2,1,0:T(8,128)(2,1)S(1)}, u32[]{:S(2)}, u32[]{:S(2)}) collective-permute-start(bf16[2,16,4096]{2,1,0:T(8,128)(2,1)S(1)} %add_convert_fusion.1.refs_0_), channel_id=1, source_target_pairs={{0,1},{1,0},{2,3},{3,2},{4,5},{5,4},{6,7},{7,6},{8,9},{9,8},{10,11... | collective-permute-start | bytes 786440 | tf_op jit(solution)/shard_map/ppermute | solution.py:338
  95.6 9.9 %collective-permute-start.19 = (bf16[2,16,4096]{2,1,0:T(8,128)(2,1)S(1)}, bf16[2,16,4096]{2,1,0:T(8,128)(2,1)S(1)}, u32[]{:S(2)}, u32[]{:S(2)}) collective-permute-start(bf16[2,16,4096]{2,1,0:T(8,128)(2,1)S(1)} %add_convert_fusion.1.refs_0_), channel_id=1, source_target_pairs={{0,4},{1,5},{2,6},{3,7},{4,0},{5,1},{6,2},{7,3},{8,12},{9,13},{10,... | collective-permute-start | bytes 786440 | tf_op jit(solution)/shard_map/ppermute | solution.py:338
  96.5 13.8 %collective-permute-start.17 = (bf16[2,16,4096]{2,1,0:T(8,128)(2,1)S(1)}, bf16[2,16,4096]{2,1,0:T(8,128)(2,1)S(1)}, u32[]{:S(2)}, u32[]{:S(2)}) collective-permute-start(bf16[2,16,4096]{2,1,0:T(8,128)(2,1)S(1)} %add_convert_fusion.1.refs_0_), channel_id=1, source_target_pairs={{0,6},{1,7},{2,4},{3,5},{4,2},{5,3},{6,0},{7,1},{8,14},{9,15},{10,... | collective-permute-start | bytes 786440 | tf_op jit(solution)/shard_map/ppermute | solution.py:338
  97.8 14.0 %collective-permute-start.15 = (bf16[2,16,4096]{2,1,0:T(8,128)(2,1)S(1)}, bf16[2,16,4096]{2,1,0:T(8,128)(2,1)S(1)}, u32[]{:S(2)}, u32[]{:S(2)}) collective-permute-start(bf16[2,16,4096]{2,1,0:T(8,128)(2,1)S(1)} %add_convert_fusion.1.refs_0_), channel_id=1, source_target_pairs={{0,2},{1,3},{2,0},{3,1},{4,6},{5,7},{6,4},{7,5},{8,10},{9,11},{10,... | collective-permute-start | bytes 786440 | tf_op jit(solution)/shard_map/ppermute | solution.py:338
  98.7 13.6 %collective-permute-start.13 = (bf16[4,16,4096]{2,1,0:T(8,128)(2,1)S(1)}, bf16[4,16,4096]{2,1,0:T(8,128)(2,1)S(1)}, u32[]{:S(2)}, u32[]{:S(2)}) collective-permute-start(bf16[4,16,4096]{2,1,0:T(8,128)(2,1)S(1)} %pad_maximum_fusion.refs_3_), channel_id=1, source_target_pairs={{0,8},{1,9},{2,10},{3,11},{4,12},{5,13},{6,14},{7,15},{8,0},{9,1},... | collective-permute-start | bytes 1572872 | tf_op jit(solution)/shard_map/ppermute | solution.py:338
  105.5 10.1 %collective-permute-start.20 = (bf16[2,16,4096]{2,1,0:T(8,128)(2,1)S(1)}, bf16[2,16,4096]{2,1,0:T(8,128)(2,1)S(1)}, u32[]{:S(2)}, u32[]{:S(2)}) collective-permute-start(bf16[2,16,4096]{2,1,0:T(8,128)(2,1)S(1)} %collective-permute-done.19.refs_2_), channel_id=1, source_target_pairs={{0,1},{1,0},{2,3},{3,2},{4,5},{5,4},{6,7},{7,6},{8,9},{9,8},{10,11... | collective-permute-start | bytes 786440 | tf_op jit(solution)/shard_map/ppermute | solution.py:338
  110.3 5.3 %collective-permute-start.18 = (bf16[2,16,4096]{2,1,0:T(8,128)(2,1)S(1)}, bf16[2,16,4096]{2,1,0:T(8,128)(2,1)S(1)}, u32[]{:S(2)}, u32[]{:S(2)}) collective-permute-start(bf16[2,16,4096]{2,1,0:T(8,128)(2,1)S(1)} %collective-permute-done.17.refs_1_), channel_id=1, source_target_pairs={{0,1},{1,0},{2,3},{3,2},{4,5},{5,4},{6,7},{7,6},{8,9},{9,8},{10,11... | collective-permute-start | bytes 786440 | tf_op jit(solution)/shard_map/ppermute | solution.py:338
  111.8 3.8 %collective-permute-start.16 = (bf16[2,16,4096]{2,1,0:T(8,128)(2,1)S(1)}, bf16[2,16,4096]{2,1,0:T(8,128)(2,1)S(1)}, u32[]{:S(2)}, u32[]{:S(2)}) collective-permute-start(bf16[2,16,4096]{2,1,0:T(8,128)(2,1)S(1)} %collective-permute-done.15.refs_0_), channel_id=1, source_target_pairs={{0,1},{1,0},{2,3},{3,2},{4,5},{5,4},{6,7},{7,6},{8,9},{9,8},{10,11... | collective-permute-start | bytes 786440 | tf_op jit(solution)/shard_map/ppermute | solution.py:338
  112.0 3.7 %collective-permute-start.21 = (bf16[4,16,4096]{2,1,0:T(8,128)(2,1)S(1)}, bf16[4,16,4096]{2,1,0:T(8,128)(2,1)S(1)}, u32[]{:S(2)}, u32[]{:S(2)}) collective-permute-start(bf16[4,16,4096]{2,1,0:T(8,128)(2,1)S(1)} %pad_maximum_fusion.refs_3_), channel_id=1, source_target_pairs={{0,1},{1,0},{2,3},{3,2},{4,5},{5,4},{6,7},{7,6},{8,9},{9,8},{10,11... | collective-permute-start | bytes 1572872 | tf_op jit(solution)/shard_map/ppermute | solution.py:338
  112.3 4.7 %collective-permute-start.14 = (bf16[4,16,4096]{2,1,0:T(8,128)(2,1)S(1)}, bf16[4,16,4096]{2,1,0:T(8,128)(2,1)S(1)}, u32[]{:S(2)}, u32[]{:S(2)}) collective-permute-start(bf16[4,16,4096]{2,1,0:T(8,128)(2,1)S(1)} %collective-permute-done.13.refs_0_), channel_id=1, source_target_pairs={{0,1},{1,0},{2,3},{3,2},{4,5},{5,4},{6,7},{7,6},{8,9},{9,8},{10,11... | collective-permute-start | bytes 1572872 | tf_op jit(solution)/shard_map/ppermute | solution.py:338

commit v7 on v6

--- a/solution.py
+++ b/solution.py
@@ -46,7 +46,7 @@
 def local_table(local_ff):
     table = np.kron(sylvester(local_ff // 52), paley_table())
     order = np.arange(local_ff).reshape(-1, GROUP // 8, 8).transpose(0, 2, 1).reshape(-1)
-    tile = 512
+    tile = 896
     table = np.pad(table[:, order], ((0, 0), (0, -local_ff % tile)))
     return jnp.asarray(table.reshape(local_ff, -1, tile).transpose(1, 0, 2), jnp.bfloat16)
 

time: 118 us -> 118 us (level)
  no operation moved by 1% of the time
where the time goes in v7:
time: 118 us
  Pallas kernels  34.2 us (29%)
  waiting for transfers between devices  29.2 us (25%)
  starting transfers between devices  28.4 us (24%)
  blocking collectives  23 us (19%)
  other arithmetic  2.96 us (3%)
    ppermute x23, starting transfers between devices, swap(): return lax.ppermute(x, 'tensor', [(i, i ^ mask) for i in range(shards)])  23.9 us
    ppermute x23, waiting for transfers between devices, swap(): return lax.ppermute(x, 'tensor', [(i, i ^ mask) for i in range(shards)])  23.9 us
    all_to_all x1, blocking collectives, local(): lax.all_to_all(hidden.reshape(shards, rows, local_ff), 'tensor', 0, 0)  23 us
    pallas_call x1, Pallas kernels, dequant(): pl.pallas_call(dequant_body, grid=(tiles,), in_specs=[pl.BlockSpec((low.s...  10 us
    pallas_call x1, Pallas kernels, project(): pl.pallas_call(functools.partial(project_body, full), grid_spec=pltpu.Pre...  8.12 us
    pallas_call x1, Pallas kernels, project_unpacked(): pl.pallas_call(functools.partial(stream_body, full), grid_spec=pltpu.Pref...  6.71 us
    all_to_all x1, waiting for transfers between devices, local(): rot = lax.all_to_all(turned, 'tensor', 0, 0)  5.33 us
    pallas_call x1, Pallas kernels, rotate(): pl.pallas_call(rotate_body, in_specs=[pl.BlockSpec(memory_space=pltpu.VME...  5.25 us
  transfers between devices with their start and end apart: 24, of which 9 were waited for; matrix products, arithmetic and copies ran while one was open for 1% of the time, Pallas kernels for 18%

profile of v7, /device:TPU:1, one launch (start us, length us, event | category | flops | bytes accessed | tf_op | source)
XLA Modules:
  0.0 118.0 jit_solution(15773280522924827503)
XLA Ops:
  0.0 1.9 %fusion.4 = bf16[256,1664]{1,0:T(8,128)(2,1)S(1)} fusion(bf16[256,1664]{1,0:T(8,128)(2,1)} %param.7, bf16[256,1664]{1,0:T(8,128)(2,1)} %param.6), kind=kLoop, calls=%fused_computation.6 | loop fusion | flops 3407872 | bytes 2555904 | tf_op jit(solution)/shard_map/convert_element_type | solution.py:345
  1.9 23.0 %all_to_all.10.hidden_ref = bf16[16,16,1664]{2,1,0:T(8,128)(2,1)S(1)} all-to-all(bf16[16,16,1664]{2,1,0:T(8,128)(2,1)S(1)} %bitcast.18), channel_id=1, replica_groups=mesh['dp'=8,'tensor'=16] {'tensor'}, dimensions={0} | all-to-all | bytes 1703936 | tf_op jit(solution)/shard_map/all_to_all | solution.py:346
  24.9 5.2 %rotate.1 = bf16[16,16,1664]{2,1,0:T(8,128)(2,1)} custom-call(bf16[16,16,1664]{2,1,0:T(8,128)(2,1)S(1)} %all_to_all.10.hidden_ref, bf16[2,1664,896]{2,1,0:T(8,128)(2,1)} %constant.9.clone.table_ref), custom_call_target="tpu_custom_call" | custom-call | flops 1417674752 | bytes 7241728 | tf_op jit(solution)/shard_map/rotate/pallas_call | solution.py:84
  30.2 4.4 %all-to-all-start.1 = ((bf16[16,16,1664]{2,1,0:T(8,128)(2,1)}), bf16[16,16,1664]{2,1,0:T(8,128)(2,1)S(1)}, u32[]{:S(2)}, u32[]{:S(2)}) async-start(bf16[16,16,1664]{2,1,0:T(8,128)(2,1)} %rotate.1), calls=%async_computation.1 | async-start | bytes 1703936 | tf_op jit(solution)/shard_map/all_to_all | solution.py:348
  34.6 10.0 %dequant.1.weight_ref = bf16[4,1664,1024]{2,1,0:T(8,128)(2,1)} custom-call(s32[208,8192]{1,0:T(8,128)} %low_ref.3, s32[208,8192]{1,0:T(8,128)} %high_ref.3, bf16[13,8192]{1,0:T(8,128)(2,1)} %scale_ref.3), custom_call_target="tpu_custom_call" | custom-call | flops 54525952 | bytes 20447232 | tf_op jit(solution)/shard_map/dequant/pallas_call | solution.py:205
  44.6 5.3 %all-to-all-done.1.rot_ref = bf16[16,16,1664]{2,1,0:T(8,128)(2,1)S(1)} async-done(((bf16[16,16,1664]{2,1,0:T(8,128)(2,1)}), bf16[16,16,1664]{2,1,0:T(8,128)(2,1)S(1)}, u32[]{:S(2)}, u32[]{:S(2)}) %all-to-all-start.1) | async-done | bytes 852000 | tf_op jit(solution)/shard_map/all_to_all | solution.py:348
  50.0 6.7 %project_unpacked.1 = (bf16[8,16,4096]{2,1,0:T(8,128)(2,1)S(1)}, bf16[8,16,4096]{2,1,0:T(8,128)(2,1)S(1)}) custom-call(s32[1]{0:T(128)} %bitcast.place_ref, bf16[16,16,1664]{2,1,0:T(8,128)(2,1)S(1)} %all-to-all-done.1.rot_ref, bf16[4,1664,1024]{2,1,0:T(8,128)(2,1)} %dequant.1.weight_ref), custom_call_target="tpu_custom_call" | custom-call | flops 3489660928 | bytes 17825792 | tf_op jit(solution)/shard_map/project_unpacked/pallas_call | solution.py:263
  57.5 8.1 %project.1 = (bf16[8,16,4096]{2,1,0:T(8,128)(2,1)S(1)}, bf16[8,16,4096]{2,1,0:T(8,128)(2,1)S(1)}) custom-call(s32[1]{0:T(128)} %bitcast.place_ref, bf16[16,16,1664]{2,1,0:T(8,128)(2,1)S(1)} %all-to-all-done.1.rot_ref, s32[208,8192]{1,0:T(8,128)} %low_ref.3, s32[208,8192]{1,0:T(8,128)} %high_ref.3, bf16[13,8192]{1,0:T(8,128)(2,1)} %scale_ref.3), custom_call_target="tpu_custom_call" | custom-call | flops 3489660928 | bytes 11010048 | tf_op jit(solution)/shard_map/project/pallas_call | solution.py:145
  66.1 2.2 %collective-permute-done.2 = bf16[8,16,4096]{2,1,0:T(8,128)(2,1)S(1)} collective-permute-done((bf16[8,16,4096]{2,1,0:T(8,128)(2,1)S(1)}, bf16[8,16,4096]{2,1,0:T(8,128)(2,1)S(1)}, u32[]{:S(2)}, u32[]{:S(2)}) %collective-permute-start.2) | collective-permute-done | bytes 1048608 | tf_op jit(solution)/shard_map/ppermute | solution.py:338
  68.7 3.8 %collective-permute-start.9 = (bf16[2,16,4096]{2,1,0:T(8,128)(2,1)S(1)}, bf16[2,16,4096]{2,1,0:T(8,128)(2,1)S(1)}, u32[]{:S(2)}, u32[]{:S(2)}) collective-permute-start(bf16[2,16,4096]{2,1,0:T(8,128)(2,1)S(1)} %get-tuple-element.31), channel_id=1, source_target_pairs={{0,4},{1,5},{2,6},{3,7},{4,0},{5,1},{6,2},{7,3},{8,12},{9,13},{10,... | collective-permute-start | bytes 786440 | tf_op jit(solution)/shard_map/ppermute | solution.py:338
  72.5 7.9 %collective-permute-done.1 = bf16[4,16,4096]{2,1,0:T(8,128)(2,1)S(1)} collective-permute-done((bf16[4,16,4096]{2,1,0:T(8,128)(2,1)S(1)}, bf16[4,16,4096]{2,1,0:T(8,128)(2,1)S(1)}, u32[]{:S(2)}, u32[]{:S(2)}) %collective-permute-start.1) | collective-permute-done | bytes 524320 | tf_op jit(solution)/shard_map/ppermute | solution.py:338
  82.3 1.1 collective-permute-start.4
  84.4 1.8 %collective-permute-done.3 = bf16[16,4096]{1,0:T(8,128)(2,1)S(1)} collective-permute-done((bf16[16,4096]{1,0:T(8,128)(2,1)S(1)}, bf16[16,4096]{1,0:T(8,128)(2,1)S(1)}, u32[]{:S(2)}, u32[]{:S(2)}) %collective-permute-start.3) | collective-permute-done | bytes 131104 | tf_op jit(solution)/shard_map/ppermute | solution.py:338
  86.2 3.8 %collective-permute-done.5 = bf16[16,4096]{1,0:T(8,128)(2,1)S(1)} collective-permute-done((bf16[16,4096]{1,0:T(8,128)(2,1)S(1)}, bf16[16,4096]{1,0:T(8,128)(2,1)S(1)}, u32[]{:S(2)}, u32[]{:S(2)}) %collective-permute-start.5) | collective-permute-done | bytes 131104 | tf_op jit(solution)/shard_map/ppermute | solution.py:338
  90.0 1.2 collective-permute-start.8
  91.7 1.6 %collective-permute-start.6 = (bf16[16,4096]{1,0:T(8,128)(2,1)S(1)}, bf16[16,4096]{1,0:T(8,128)(2,1)S(1)}, u32[]{:S(2)}, u32[]{:S(2)}) collective-permute-start(bf16[16,4096]{1,0:T(8,128)(2,1)S(1)} %fusion.6), channel_id=1, source_target_pairs={{0,2},{1,3},{2,0},{3,1},{4,6},{5,7},{6,4},{7,5},{8,10},{9,11},{10,... | collective-permute-start | bytes 393224 | tf_op jit(solution)/shard_map/ppermute | solution.py:338
  93.6 1.9 %collective-permute-start.22 = (bf16[2,16,4096]{2,1,0:T(8,128)(2,1)S(1)}, bf16[2,16,4096]{2,1,0:T(8,128)(2,1)S(1)}, u32[]{:S(2)}, u32[]{:S(2)}) collective-permute-start(bf16[2,16,4096]{2,1,0:T(8,128)(2,1)S(1)} %add_convert_fusion.1.refs_0_), channel_id=1, source_target_pairs={{0,1},{1,0},{2,3},{3,2},{4,5},{5,4},{6,7},{7,6},{8,9},{9,8},{10,11... | collective-permute-start | bytes 786440 | tf_op jit(solution)/shard_map/ppermute | solution.py:338
  96.4 1.3 %collective-permute-start.17 = (bf16[2,16,4096]{2,1,0:T(8,128)(2,1)S(1)}, bf16[2,16,4096]{2,1,0:T(8,128)(2,1)S(1)}, u32[]{:S(2)}, u32[]{:S(2)}) collective-permute-start(bf16[2,16,4096]{2,1,0:T(8,128)(2,1)S(1)} %add_convert_fusion.1.refs_0_), channel_id=1, source_target_pairs={{0,6},{1,7},{2,4},{3,5},{4,2},{5,3},{6,0},{7,1},{8,14},{9,15},{10,... | collective-permute-start | bytes 786440 | tf_op jit(solution)/shard_map/ppermute | solution.py:338
  100.3 5.2 %collective-permute-done.19.refs_2_ = bf16[2,16,4096]{2,1,0:T(8,128)(2,1)S(1)} collective-permute-done((bf16[2,16,4096]{2,1,0:T(8,128)(2,1)S(1)}, bf16[2,16,4096]{2,1,0:T(8,128)(2,1)S(1)}, u32[]{:S(2)}, u32[]{:S(2)}) %collective-permute-start.19) | collective-permute-done | bytes 262176 | tf_op jit(solution)/shard_map/ppermute | solution.py:338
  105.4 2.8 %collective-permute-start.20 = (bf16[2,16,4096]{2,1,0:T(8,128)(2,1)S(1)}, bf16[2,16,4096]{2,1,0:T(8,128)(2,1)S(1)}, u32[]{:S(2)}, u32[]{:S(2)}) collective-permute-start(bf16[2,16,4096]{2,1,0:T(8,128)(2,1)S(1)} %collective-permute-done.19.refs_2_), channel_id=1, source_target_pairs={{0,1},{1,0},{2,3},{3,2},{4,5},{5,4},{6,7},{7,6},{8,9},{9,8},{10,11... | collective-permute-start | bytes 786440 | tf_op jit(solution)/shard_map/ppermute | solution.py:338
  108.3 1.9 %collective-permute-done.17.refs_1_ = bf16[2,16,4096]{2,1,0:T(8,128)(2,1)S(1)} collective-permute-done((bf16[2,16,4096]{2,1,0:T(8,128)(2,1)S(1)}, bf16[2,16,4096]{2,1,0:T(8,128)(2,1)S(1)}, u32[]{:S(2)}, u32[]{:S(2)}) %collective-permute-start.17) | collective-permute-done | bytes 262176 | tf_op jit(solution)/shard_map/ppermute | solution.py:338
  110.2 1.5 %collective-permute-start.18 = (bf16[2,16,4096]{2,1,0:T(8,128)(2,1)S(1)}, bf16[2,16,4096]{2,1,0:T(8,128)(2,1)S(1)}, u32[]{:S(2)}, u32[]{:S(2)}) collective-permute-start(bf16[2,16,4096]{2,1,0:T(8,128)(2,1)S(1)} %collective-permute-done.17.refs_1_), channel_id=1, source_target_pairs={{0,1},{1,0},{2,3},{3,2},{4,5},{5,4},{6,7},{7,6},{8,9},{9,8},{10,11... | collective-permute-start | bytes 786440 | tf_op jit(solution)/shard_map/ppermute | solution.py:338
  112.2 2.3 %collective-permute-start.14 = (bf16[4,16,4096]{2,1,0:T(8,128)(2,1)S(1)}, bf16[4,16,4096]{2,1,0:T(8,128)(2,1)S(1)}, u32[]{:S(2)}, u32[]{:S(2)}) collective-permute-start(bf16[4,16,4096]{2,1,0:T(8,128)(2,1)S(1)} %collective-permute-done.13.refs_0_), channel_id=1, source_target_pairs={{0,1},{1,0},{2,3},{3,2},{4,5},{5,4},{6,7},{7,6},{8,9},{9,8},{10,11... | collective-permute-start | bytes 1572872 | tf_op jit(solution)/shard_map/ppermute | solution.py:338
  115.6 1.3 %put.6.refs_2_ = bf16[256,8192]{1,0:T(8,128)(2,1)} custom-call(s32[1]{0:T(128)} %bitcast.place_ref, bf16[2,16,4096]{2,1,0:T(8,128)(2,1)S(1)} %collective-permute-done.16.refs_0_, bf16[2,16,4096]{2,1,0:T(8,128)(2,1)S(1)} %collective-permute-done.18.refs_1_, bf16[2,16,4096]{2,1,0:T(8,128)(2,1)S(1)} %collective-permute-done.20.refs_2_, ...), custom_call_target="tpu_custom_call", output_to_operand_aliasing={{}: (6, {})} | custom-call | bytes 3670016 | tf_op jit(solution)/shard_map/put/pallas_call | solution.py:312
  (42 shorter events, 11.3 us)
Async XLA Ops:
  30.2 19.8 %all-to-all-start.1 = ((bf16[16,16,1664]{2,1,0:T(8,128)(2,1)}), bf16[16,16,1664]{2,1,0:T(8,128)(2,1)S(1)}, u32[]{:S(2)}, u32[]{:S(2)}) async-start(bf16[16,16,1664]{2,1,0:T(8,128)(2,1)} %rotate.1), calls=%async_computation.1 | async-start | bytes 1703936 | tf_op jit(solution)/shard_map/all_to_all | solution.py:348
  56.7 9.0 %collective-permute-start = (bf16[8,16,4096]{2,1,0:T(8,128)(2,1)S(1)}, bf16[8,16,4096]{2,1,0:T(8,128)(2,1)S(1)}, u32[]{:S(2)}, u32[]{:S(2)}) collective-permute-start(bf16[8,16,4096]{2,1,0:T(8,128)(2,1)S(1)} %get-tuple-element.19), channel_id=1, source_target_pairs={{0,1},{1,0},{2,3},{3,2},{4,5},{5,4},{6,7},{7,6},{8,9},{9,8},{10,11... | collective-permute-start | bytes 3145736 | tf_op jit(solution)/shard_map/ppermute | solution.py:338
  65.6 2.7 %collective-permute-start.2 = (bf16[8,16,4096]{2,1,0:T(8,128)(2,1)S(1)}, bf16[8,16,4096]{2,1,0:T(8,128)(2,1)S(1)}, u32[]{:S(2)}, u32[]{:S(2)}) collective-permute-start(bf16[8,16,4096]{2,1,0:T(8,128)(2,1)S(1)} %get-tuple-element.21), channel_id=1, source_target_pairs={{0,1},{1,0},{2,3},{3,2},{4,5},{5,4},{6,7},{7,6},{8,9},{9,8},{10,11... | collective-permute-start | bytes 3145736 | tf_op jit(solution)/shard_map/ppermute | solution.py:338
  65.8 14.6 %collective-permute-start.1 = (bf16[4,16,4096]{2,1,0:T(8,128)(2,1)S(1)}, bf16[4,16,4096]{2,1,0:T(8,128)(2,1)S(1)}, u32[]{:S(2)}, u32[]{:S(2)}) collective-permute-start(bf16[4,16,4096]{2,1,0:T(8,128)(2,1)S(1)} %add_convert_fusion), channel_id=1, source_target_pairs={{0,8},{1,9},{2,10},{3,11},{4,12},{5,13},{6,14},{7,15},{8,0},{9,1},... | collective-permute-start | bytes 1572872 | tf_op jit(solution)/shard_map/ppermute | solution.py:338
  68.6 13.7 %collective-permute-start.11 = (bf16[2,16,4096]{2,1,0:T(8,128)(2,1)S(1)}, bf16[2,16,4096]{2,1,0:T(8,128)(2,1)S(1)}, u32[]{:S(2)}, u32[]{:S(2)}) collective-permute-start(bf16[2,16,4096]{2,1,0:T(8,128)(2,1)S(1)} %get-tuple-element.29), channel_id=1, source_target_pairs={{0,6},{1,7},{2,4},{3,5},{4,2},{5,3},{6,0},{7,1},{8,14},{9,15},{10,... | collective-permute-start | bytes 786440 | tf_op jit(solution)/shard_map/ppermute | solution.py:338
  68.6 14.8 %collective-permute-start.10 = (bf16[2,16,4096]{2,1,0:T(8,128)(2,1)S(1)}, bf16[2,16,4096]{2,1,0:T(8,128)(2,1)S(1)}, u32[]{:S(2)}, u32[]{:S(2)}) collective-permute-start(bf16[2,16,4096]{2,1,0:T(8,128)(2,1)S(1)} %get-tuple-element.30), channel_id=1, source_target_pairs={{0,2},{1,3},{2,0},{3,1},{4,6},{5,7},{6,4},{7,5},{8,10},{9,11},{10,... | collective-permute-start | bytes 786440 | tf_op jit(solution)/shard_map/ppermute | solution.py:338
  68.7 15.4 %collective-permute-start.9 = (bf16[2,16,4096]{2,1,0:T(8,128)(2,1)S(1)}, bf16[2,16,4096]{2,1,0:T(8,128)(2,1)S(1)}, u32[]{:S(2)}, u32[]{:S(2)}) collective-permute-start(bf16[2,16,4096]{2,1,0:T(8,128)(2,1)S(1)} %get-tuple-element.31), channel_id=1, source_target_pairs={{0,4},{1,5},{2,6},{3,7},{4,0},{5,1},{6,2},{7,3},{8,12},{9,13},{10,... | collective-permute-start | bytes 786440 | tf_op jit(solution)/shard_map/ppermute | solution.py:338
  80.7 5.5 %collective-permute-start.3 = (bf16[16,4096]{1,0:T(8,128)(2,1)S(1)}, bf16[16,4096]{1,0:T(8,128)(2,1)S(1)}, u32[]{:S(2)}, u32[]{:S(2)}) collective-permute-start(bf16[16,4096]{1,0:T(8,128)(2,1)S(1)} %get-tuple-element.32), channel_id=1, source_target_pairs={{0,4},{1,5},{2,6},{3,7},{4,0},{5,1},{6,2},{7,3},{8,12},{9,13},{10,... | collective-permute-start | bytes 393224 | tf_op jit(solution)/shard_map/ppermute | solution.py:338
  81.6 8.4 %collective-permute-start.5 = (bf16[16,4096]{1,0:T(8,128)(2,1)S(1)}, bf16[16,4096]{1,0:T(8,128)(2,1)S(1)}, u32[]{:S(2)}, u32[]{:S(2)}) collective-permute-start(bf16[16,4096]{1,0:T(8,128)(2,1)S(1)} %get-tuple-element.33), channel_id=1, source_target_pairs={{0,6},{1,7},{2,4},{3,5},{4,2},{5,3},{6,0},{7,1},{8,14},{9,15},{10,... | collective-permute-start | bytes 393224 | tf_op jit(solution)/shard_map/ppermute | solution.py:338
  82.3 7.7 %collective-permute-start.4 = (bf16[16,4096]{1,0:T(8,128)(2,1)S(1)}, bf16[16,4096]{1,0:T(8,128)(2,1)S(1)}, u32[]{:S(2)}, u32[]{:S(2)}) collective-permute-start(bf16[16,4096]{1,0:T(8,128)(2,1)S(1)} %get-tuple-element.34), channel_id=1, source_target_pairs={{0,2},{1,3},{2,0},{3,1},{4,6},{5,7},{6,4},{7,5},{8,10},{9,11},{10,... | collective-permute-start | bytes 393224 | tf_op jit(solution)/shard_map/ppermute | solution.py:338
  84.3 9.1 %collective-permute-start.12 = (bf16[2,16,4096]{2,1,0:T(8,128)(2,1)S(1)}, bf16[2,16,4096]{2,1,0:T(8,128)(2,1)S(1)}, u32[]{:S(2)}, u32[]{:S(2)}) collective-permute-start(bf16[2,16,4096]{2,1,0:T(8,128)(2,1)S(1)} %fusion.7), channel_id=1, source_target_pairs={{0,8},{1,9},{2,10},{3,11},{4,12},{5,13},{6,14},{7,15},{8,0},{9,1},... | collective-permute-start | bytes 786440 | tf_op jit(solution)/shard_map/ppermute | solution.py:338
  90.0 6.4 %collective-permute-start.8 = (bf16[16,4096]{1,0:T(8,128)(2,1)S(1)}, bf16[16,4096]{1,0:T(8,128)(2,1)S(1)}, u32[]{:S(2)}, u32[]{:S(2)}) collective-permute-start(bf16[16,4096]{1,0:T(8,128)(2,1)S(1)} %fusion.6), channel_id=1, source_target_pairs={{0,6},{1,7},{2,4},{3,5},{4,2},{5,3},{6,0},{7,1},{8,14},{9,15},{10,... | collective-permute-start | bytes 393224 | tf_op jit(solution)/shard_map/ppermute | solution.py:338
  91.2 6.5 %collective-permute-start.7 = (bf16[16,4096]{1,0:T(8,128)(2,1)S(1)}, bf16[16,4096]{1,0:T(8,128)(2,1)S(1)}, u32[]{:S(2)}, u32[]{:S(2)}) collective-permute-start(bf16[16,4096]{1,0:T(8,128)(2,1)S(1)} %fusion.6), channel_id=1, source_target_pairs={{0,4},{1,5},{2,6},{3,7},{4,0},{5,1},{6,2},{7,3},{8,12},{9,13},{10,... | collective-permute-start | bytes 393224 | tf_op jit(solution)/shard_map/ppermute | solution.py:338
  91.7 6.8 %collective-permute-start.6 = (bf16[16,4096]{1,0:T(8,128)(2,1)S(1)}, bf16[16,4096]{1,0:T(8,128)(2,1)S(1)}, u32[]{:S(2)}, u32[]{:S(2)}) collective-permute-start(bf16[16,4096]{1,0:T(8,128)(2,1)S(1)} %fusion.6), channel_id=1, source_target_pairs={{0,2},{1,3},{2,0},{3,1},{4,6},{5,7},{6,4},{7,5},{8,10},{9,11},{10,... | collective-permute-start | bytes 393224 | tf_op jit(solution)/shard_map/ppermute | solution.py:338
  93.6 18.3 %collective-permute-start.22 = (bf16[2,16,4096]{2,1,0:T(8,128)(2,1)S(1)}, bf16[2,16,4096]{2,1,0:T(8,128)(2,1)S(1)}, u32[]{:S(2)}, u32[]{:S(2)}) collective-permute-start(bf16[2,16,4096]{2,1,0:T(8,128)(2,1)S(1)} %add_convert_fusion.1.refs_0_), channel_id=1, source_target_pairs={{0,1},{1,0},{2,3},{3,2},{4,5},{5,4},{6,7},{7,6},{8,9},{9,8},{10,11... | collective-permute-start | bytes 786440 | tf_op jit(solution)/shard_map/ppermute | solution.py:338
  95.5 9.9 %collective-permute-start.19 = (bf16[2,16,4096]{2,1,0:T(8,128)(2,1)S(1)}, bf16[2,16,4096]{2,1,0:T(8,128)(2,1)S(1)}, u32[]{:S(2)}, u32[]{:S(2)}) collective-permute-start(bf16[2,16,4096]{2,1,0:T(8,128)(2,1)S(1)} %add_convert_fusion.1.refs_0_), channel_id=1, source_target_pairs={{0,4},{1,5},{2,6},{3,7},{4,0},{5,1},{6,2},{7,3},{8,12},{9,13},{10,... | collective-permute-start | bytes 786440 | tf_op jit(solution)/shard_map/ppermute | solution.py:338
  96.4 13.8 %collective-permute-start.17 = (bf16[2,16,4096]{2,1,0:T(8,128)(2,1)S(1)}, bf16[2,16,4096]{2,1,0:T(8,128)(2,1)S(1)}, u32[]{:S(2)}, u32[]{:S(2)}) collective-permute-start(bf16[2,16,4096]{2,1,0:T(8,128)(2,1)S(1)} %add_convert_fusion.1.refs_0_), channel_id=1, source_target_pairs={{0,6},{1,7},{2,4},{3,5},{4,2},{5,3},{6,0},{7,1},{8,14},{9,15},{10,... | collective-permute-start | bytes 786440 | tf_op jit(solution)/shard_map/ppermute | solution.py:338
  97.7 14.0 %collective-permute-start.15 = (bf16[2,16,4096]{2,1,0:T(8,128)(2,1)S(1)}, bf16[2,16,4096]{2,1,0:T(8,128)(2,1)S(1)}, u32[]{:S(2)}, u32[]{:S(2)}) collective-permute-start(bf16[2,16,4096]{2,1,0:T(8,128)(2,1)S(1)} %add_convert_fusion.1.refs_0_), channel_id=1, source_target_pairs={{0,2},{1,3},{2,0},{3,1},{4,6},{5,7},{6,4},{7,5},{8,10},{9,11},{10,... | collective-permute-start | bytes 786440 | tf_op jit(solution)/shard_map/ppermute | solution.py:338
  98.6 13.6 %collective-permute-start.13 = (bf16[4,16,4096]{2,1,0:T(8,128)(2,1)S(1)}, bf16[4,16,4096]{2,1,0:T(8,128)(2,1)S(1)}, u32[]{:S(2)}, u32[]{:S(2)}) collective-permute-start(bf16[4,16,4096]{2,1,0:T(8,128)(2,1)S(1)} %pad_maximum_fusion.refs_3_), channel_id=1, source_target_pairs={{0,8},{1,9},{2,10},{3,11},{4,12},{5,13},{6,14},{7,15},{8,0},{9,1},... | collective-permute-start | bytes 1572872 | tf_op jit(solution)/shard_map/ppermute | solution.py:338
  105.4 10.1 %collective-permute-start.20 = (bf16[2,16,4096]{2,1,0:T(8,128)(2,1)S(1)}, bf16[2,16,4096]{2,1,0:T(8,128)(2,1)S(1)}, u32[]{:S(2)}, u32[]{:S(2)}) collective-permute-start(bf16[2,16,4096]{2,1,0:T(8,128)(2,1)S(1)} %collective-permute-done.19.refs_2_), channel_id=1, source_target_pairs={{0,1},{1,0},{2,3},{3,2},{4,5},{5,4},{6,7},{7,6},{8,9},{9,8},{10,11... | collective-permute-start | bytes 786440 | tf_op jit(solution)/shard_map/ppermute | solution.py:338
  110.2 5.3 %collective-permute-start.18 = (bf16[2,16,4096]{2,1,0:T(8,128)(2,1)S(1)}, bf16[2,16,4096]{2,1,0:T(8,128)(2,1)S(1)}, u32[]{:S(2)}, u32[]{:S(2)}) collective-permute-start(bf16[2,16,4096]{2,1,0:T(8,128)(2,1)S(1)} %collective-permute-done.17.refs_1_), channel_id=1, source_target_pairs={{0,1},{1,0},{2,3},{3,2},{4,5},{5,4},{6,7},{7,6},{8,9},{9,8},{10,11... | collective-permute-start | bytes 786440 | tf_op jit(solution)/shard_map/ppermute | solution.py:338
  111.7 3.9 %collective-permute-start.16 = (bf16[2,16,4096]{2,1,0:T(8,128)(2,1)S(1)}, bf16[2,16,4096]{2,1,0:T(8,128)(2,1)S(1)}, u32[]{:S(2)}, u32[]{:S(2)}) collective-permute-start(bf16[2,16,4096]{2,1,0:T(8,128)(2,1)S(1)} %collective-permute-done.15.refs_0_), channel_id=1, source_target_pairs={{0,1},{1,0},{2,3},{3,2},{4,5},{5,4},{6,7},{7,6},{8,9},{9,8},{10,11... | collective-permute-start | bytes 786440 | tf_op jit(solution)/shard_map/ppermute | solution.py:338
  111.9 3.7 %collective-permute-start.21 = (bf16[4,16,4096]{2,1,0:T(8,128)(2,1)S(1)}, bf16[4,16,4096]{2,1,0:T(8,128)(2,1)S(1)}, u32[]{:S(2)}, u32[]{:S(2)}) collective-permute-start(bf16[4,16,4096]{2,1,0:T(8,128)(2,1)S(1)} %pad_maximum_fusion.refs_3_), channel_id=1, source_target_pairs={{0,1},{1,0},{2,3},{3,2},{4,5},{5,4},{6,7},{7,6},{8,9},{9,8},{10,11... | collective-permute-start | bytes 1572872 | tf_op jit(solution)/shard_map/ppermute | solution.py:338
  112.2 4.7 %collective-permute-start.14 = (bf16[4,16,4096]{2,1,0:T(8,128)(2,1)S(1)}, bf16[4,16,4096]{2,1,0:T(8,128)(2,1)S(1)}, u32[]{:S(2)}, u32[]{:S(2)}) collective-permute-start(bf16[4,16,4096]{2,1,0:T(8,128)(2,1)S(1)} %collective-permute-done.13.refs_0_), channel_id=1, source_target_pairs={{0,1},{1,0},{2,3},{3,2},{4,5},{5,4},{6,7},{7,6},{8,9},{9,8},{10,11... | collective-permute-start | bytes 1572872 | tf_op jit(solution)/shard_map/ppermute | solution.py:338
